TPU v7x, 32 devices: a whole 2x2x4 slice. The times are simulated.
32 devices in a mesh: seq: 16 (over z, y, x), head: 2 (over core).
Axes of the slice: x: 2, y: 2, z: 4, core: 2. Of those that a mesh axis runs over, the one named last changes fastest.
Arguments:
- tokens: bfloat16 [16384, 1024], P('seq'), may hold values from -6 to 6
- cotangent: bfloat16 [16384, 1024], P('seq'), may hold values from -6 to 6
- lengths: int32 [8], replicated, may hold values from 1024 to 8192, as said below
- packing: int32 [8], replicated, may hold values from 0 to 7, each once
- owners: int32 [2, 49], P('head'), may hold values from 0 to 63, as said below
- slot_copy: bfloat16 [128, 1024, 128], P(('seq', 'head')), may hold values from -0.1875 to 0.1875
- slot_master: float32 [128, 1024, 128], P(('seq', 'head')), may hold values from -0.1875 to 0.1875
- slot_first: float32 [128, 1024, 128], P(('seq', 'head'))
- slot_second: float32 [128, 1024, 128], P(('seq', 'head')), as said below
- basis_left: float32 [128, 1024, 1024], P(('seq', 'head')), may hold values from -1 to 1, as said below
- basis_right: float32 [128, 128, 128], P(('seq', 'head')), may hold values from -1 to 1, as said below
- norm_gains: float32 [2, 1024], replicated, may hold values from 0.25 to 1.75
- gains_first: float32 [2, 1024], replicated
- gains_second: float32 [2, 1024], replicated, as said below
- gate_down: float32 [1024, 16], replicated, may hold values from -0.1875 to 0.1875
- down_first: float32 [1024, 16], replicated
- down_second: float32 [1024, 16], replicated, as said below
- gate_up: float32 [17, 512], P(None, 'head')
- upper_first: float32 [17, 512], P(None, 'head')
- upper_second: float32 [17, 512], P(None, 'head'), as said below
- head_gain: float32 [256], replicated, may hold values from 0.25 to 1.75
- head_first: float32 [256], replicated
- head_second: float32 [256], replicated, as said below
- conv_weight: float32 [4, 2048], P(None, 'head'), may hold values from -3 to 3
- conv_first: float32 [4, 2048], P(None, 'head')
- conv_second: float32 [4, 2048], P(None, 'head'), as said below
Outputs:
- result: bfloat16 [16384, 1024], P('seq')
- input_grad: float32 [16384, 1024], P('seq')
- slot_grad: float32 [128, 1024, 128], P(('seq', 'head'))
- master_new: float32 [128, 1024, 128], P(('seq', 'head'))
- first_new: float32 [128, 1024, 128], P(('seq', 'head'))
- second_new: float32 [128, 1024, 128], P(('seq', 'head'))
- copy_new: bfloat16 [128, 1024, 128], P(('seq', 'head'))
- gains_grad: float32 [2, 1024], replicated
- gains_new: float32 [2, 1024], replicated
- gains_first_new: float32 [2, 1024], replicated
- gains_second_new: float32 [2, 1024], replicated
- down_grad: float32 [1024, 16], replicated
- down_new: float32 [1024, 16], replicated
- down_first_new: float32 [1024, 16], replicated
- down_second_new: float32 [1024, 16], replicated
- upper_grad: float32 [17, 512], P(None, 'head')
- upper_new: float32 [17, 512], P(None, 'head')
- upper_first_new: float32 [17, 512], P(None, 'head')
- upper_second_new: float32 [17, 512], P(None, 'head')
- head_grad: float32 [256], replicated
- head_new: float32 [256], replicated
- head_first_new: float32 [256], replicated
- head_second_new: float32 [256], replicated
- conv_grad: float32 [4, 2048], P(None, 'head')
- conv_new: float32 [4, 2048], P(None, 'head')
- conv_first_new: float32 [4, 2048], P(None, 'head')
- conv_second_new: float32 [4, 2048], P(None, 'head')
Inputs may be any that keep to these rules, and one draw needn't show every extreme that they name: `owners`: each row lists 49 distinct slots; slots 0 and 63 appear in every row. The lengths sum to 15872; the largest is 8192. `packing`: each sequence appears once. `basis_left`: every [1024, 1024] slice is orthogonal. `basis_right`: every [128, 128] slice is orthogonal. `slot_second`: Positive. `gains_second`: Positive. `down_second`: Positive. `upper_second`: Positive. `head_second`: Positive. `conv_second`: Positive.
All inputs are finite; a program needn't handle non-finite values.
Results may differ from a plain program's by a relative error of at most 0.0095.
The roundings to bfloat16 on the way count: a program that leaves them out, or rounds other values in their place, can miss the bound.
Values may be sent and summed in bfloat16 or wider, within the bound.
A program may use at most 256 MiB of HBM per device.

v0:
```python
import jax
import jax.numpy as jnp
from jax import lax
from jax.sharding import PartitionSpec as P

DK = 128
DV = 256
CH = 64


highest_precision = lax.Precision.HIGHEST
norm_epsilon = 1e-06
adam_epsilon = 1e-08
gate_scale = 16.0
moment_decay = 0.5
rate_block = 0.03
rate_gains = 0.45
rate_down = 0.02
rate_upper = 0.6
rate_head = 0.5
rate_conv = 0.1


def passed_along(array, axis, by):
    devices = lax.axis_size(axis)
    pairs = [(i, i + by) for i in range(devices) if 0 <= i + by < devices]
    return lax.ppermute(array, axis, pairs)


def carried_in(value, axis, join, neutral, backward):
    count, mine = (lax.axis_size(axis), lax.axis_index(axis))
    pieces = jax.tree.map(lambda part: lax.all_gather(part, axis), value)
    if backward:
        pieces = jax.tree.map(lambda part: part[::-1], pieces)
        mine = count - 1 - mine
    running = jax.tree.map(
        lambda part, zero: jnp.full_like(part, 0) + jnp.asarray(zero, part.dtype), value, neutral
    )

    def step(position, running):
        longer = join(running, jax.tree.map(lambda part: part[position], pieces))
        return jax.tree.map(lambda new, old: jnp.where(position < mine, new, old), longer, running)

    return lax.fori_loop(0, count - 1, step, running)


def rms_stats(values):
    return lax.rsqrt(jnp.mean(values * values, axis=-1, keepdims=True) + norm_epsilon)


def rms_back(values, inverse, gain, upstream):
    scaled = gain * upstream
    return inverse * scaled - values * inverse * inverse * inverse * jnp.mean(
        scaled * values, axis=-1, keepdims=True
    )


def swish_slope(values):
    sigmoid = jax.nn.sigmoid(values)
    return sigmoid * (1.0 + values * (1.0 - sigmoid))


def segment_of(positions, lengths, packing):
    packed = jnp.take(lengths, packing)
    starts = jnp.cumsum(packed) - packed
    filled = jnp.sum(packed)
    counted = jnp.sum((starts[None, :] <= positions[:, None]).astype(jnp.int32), axis=1)
    return (counted + (positions >= filled).astype(jnp.int32), positions < filled)


def compose(earlier, later_part):
    return (earlier[0] * later_part[0], later_part[0][..., None] * earlier[1] + later_part[1])


def advance(current_state, piece_pair):
    return (piece_pair[0][..., None] * current_state + piece_pair[1], current_state)


def retreat(adjoint, piece_pair):
    return (piece_pair[1] + piece_pair[0][..., None] * adjoint, adjoint)


def plain_adam(param, gradient, first, second, rate):
    first_next = moment_decay * first + (1.0 - moment_decay) * gradient
    second_next = moment_decay * second + (1.0 - moment_decay) * gradient * gradient
    return (
        param - rate * first_next / (jnp.sqrt(second_next) + adam_epsilon),
        first_next,
        second_next,
    )


def body(
    tokens,
    cotangent,
    lengths,
    packing,
    owners,
    slot_copy,
    slot_master,
    slot_first,
    slot_second,
    basis_left,
    basis_right,
    norm_gains,
    gains_first,
    gains_second,
    gate_down,
    down_first,
    down_second,
    gate_up,
    upper_first,
    upper_second,
    head_gain,
    head_first,
    head_second,
    conv_weight,
    conv_first,
    conv_second,
):
    tok_rows = tokens.shape[0]
    model_width = tokens.shape[1]
    block_width = slot_copy.shape[2]
    rank_width = gate_down.shape[1]
    tap_count = conv_weight.shape[0]
    key_width = gate_up.shape[1]
    channels = conv_weight.shape[1]
    value_width = channels - 2 * key_width
    heads_here = key_width // DK
    tile_len = CH
    tiles = tok_rows // tile_len
    block_total = owners.shape[1]
    count_in = (channels + value_width) // block_width
    count_out = value_width // block_width
    count_down = (block_total - count_in - count_out) // 3
    count_up = 2 * count_down
    up_end = count_in + count_up
    out_end = up_end + count_out
    score_scale = DK ** (-0.5)
    seq_index = lax.axis_index("seq")
    head_index = lax.axis_index("head")
    head_count = lax.axis_size("head")
    base_pos = seq_index * tok_rows
    ext_pos = base_pos - (tap_count - 1) + jnp.arange(tok_rows + tap_count - 1, dtype=jnp.int32)
    ext_seg, ext_valid = segment_of(ext_pos, lengths, packing)
    own_seg = ext_seg[tap_count - 1 :]
    own_valid = ext_valid[tap_count - 1 :].astype(jnp.float32)
    tile_prev = segment_of(
        base_pos - 1 + tile_len * jnp.arange(tiles, dtype=jnp.int32), lengths, packing
    )[0]
    gathered = lax.all_gather(slot_copy, "seq", axis=0, tiled=True)
    owner_row = owners[0]
    blocks = jnp.take(gathered, owner_row, axis=0)
    in_blocks = blocks[:count_in]
    up_blocks = blocks[count_in:up_end]
    out_blocks = blocks[up_end:out_end]
    down_blocks = blocks[out_end:]
    inputs = tokens.astype(jnp.float32)
    inverse_one = rms_stats(inputs)
    normed = (inputs * inverse_one * norm_gains[0]).astype(jnp.bfloat16)
    projected = jnp.einsum(
        "td,ndb->tnb", normed, in_blocks, preferred_element_type=jnp.float32
    ).reshape(tok_rows, count_in * block_width)
    mixed_proj = projected[:, :channels].astype(jnp.bfloat16)
    gate_pre = projected[:, channels:]
    down_low = gate_down.astype(jnp.bfloat16)
    lowrank = jnp.dot(normed, down_low, preferred_element_type=jnp.float32)
    logits = (
        jnp.dot(lowrank, gate_up[:rank_width], precision=highest_precision) + gate_up[rank_width]
    )
    log_gate = jax.nn.log_sigmoid(logits) / gate_scale
    rim_rows = passed_along(mixed_proj[tok_rows - (tap_count - 1) :], "seq", 1)
    extended = jnp.concatenate([rim_rows, mixed_proj], axis=0).astype(jnp.float32)
    same_seg = []
    conv_pre = jnp.zeros((tok_rows, channels), jnp.float32)
    for tap_index in range(tap_count):
        tap_mask = (ext_seg[tap_index : tap_index + tok_rows] == own_seg).astype(jnp.float32)[
            :, None
        ]
        same_seg.append(tap_mask)
        conv_pre = (
            conv_pre
            + conv_weight[tap_index] * extended[tap_index : tap_index + tok_rows] * tap_mask
        )
    active = jax.nn.silu(conv_pre)
    queries = active[:, :key_width].reshape(tiles, tile_len, heads_here, DK)
    keys_all = active[:, key_width : 2 * key_width].reshape(tiles, tile_len, heads_here, DK)
    values_all = active[:, 2 * key_width :].reshape(tiles, tile_len, heads_here, DV)
    log_gates = log_gate.reshape(tiles, tile_len, heads_here, DK)
    seg_tiles = own_seg.reshape(tiles, tile_len)
    incoming_carry = (seg_tiles == tile_prev[:, None]).astype(jnp.float32)
    causal = jnp.tril(jnp.ones((tile_len, tile_len), jnp.float32))
    pair_mask = causal[None] * (seg_tiles[:, :, None] == seg_tiles[:, None, :]).astype(jnp.float32)
    tail_mask = (seg_tiles == seg_tiles[:, -1:]).astype(jnp.float32)
    cumulative = jnp.cumsum(log_gates, axis=1)
    final_cumulative_decay = cumulative[:, -1]
    query_scaled = queries * jnp.exp(cumulative) * score_scale
    k_scaled = keys_all * jnp.exp(-cumulative)
    key_remainder = (
        keys_all
        * jnp.exp(final_cumulative_decay[:, None] - cumulative)
        * tail_mask[:, :, None, None]
    )
    scores = (
        jnp.einsum("cthk,cshk->chts", query_scaled, k_scaled, precision=highest_precision)
        * pair_mask[:, None]
    )
    intra_out = jnp.einsum("chts,cshv->cthv", scores, values_all, precision=highest_precision)
    contrib = jnp.einsum("cshk,cshv->chkv", key_remainder, values_all, precision=highest_precision)
    tile_decay = jnp.exp(final_cumulative_decay) * incoming_carry[:, -1][:, None, None]
    zero_state = jnp.zeros((heads_here, DK, DV), jnp.float32)
    unit_decay = jnp.ones((heads_here, DK), jnp.float32)
    local_end, local_start = lax.scan(advance, zero_state, (tile_decay, contrib))
    running = jnp.cumprod(tile_decay, axis=0)
    before = jnp.concatenate([unit_decay[None], running[:-1]], axis=0)
    device_decay = running[-1]
    incoming = carried_in(
        (device_decay, local_end), "seq", compose, (unit_decay, zero_state), False
    )[1]
    start_state = before[..., None] * incoming[None] + local_start
    cross_piece_output = (
        jnp.einsum("cthk,chkv->cthv", query_scaled, start_state, precision=highest_precision)
        * incoming_carry[:, :, None, None]
    )
    attended = (cross_piece_output + intra_out).reshape(tok_rows, heads_here, DV)
    inverse_head = rms_stats(attended)
    head_normed = attended * inverse_head * head_gain
    gate_view = gate_pre.reshape(tok_rows, heads_here, DV)
    swished = jax.nn.silu(gate_view)
    gated_out = (head_normed * swished).reshape(tok_rows, value_width).astype(jnp.bfloat16)
    gated_view = gated_out.reshape(tok_rows, count_out, block_width)
    attn_part = jnp.einsum(
        "tnb,ndb->td", gated_view, out_blocks, preferred_element_type=jnp.float32
    )
    attn_branch = lax.psum(attn_part, "head")
    hidden_one = inputs + attn_branch
    inverse_two = rms_stats(hidden_one)
    normed_two = (hidden_one * inverse_two * norm_gains[1]).astype(jnp.bfloat16)
    pair_proj = jnp.einsum(
        "td,ndb->tnb", normed_two, up_blocks, preferred_element_type=jnp.float32
    ).reshape(tok_rows, count_up * block_width)
    half_width = pair_proj.shape[1] // 2
    gate_mlp = pair_proj[:, :half_width]
    up_mlp = pair_proj[:, half_width:]
    hidden = (jax.nn.silu(gate_mlp) * up_mlp).astype(jnp.bfloat16)
    hidden_view = hidden.reshape(tok_rows, count_down, block_width)
    mlp_part = jnp.einsum(
        "tnb,ndb->td", hidden_view, down_blocks, preferred_element_type=jnp.float32
    )
    mlp_branch = lax.psum(mlp_part.astype(jnp.bfloat16), "head").astype(jnp.float32)
    result = (hidden_one + mlp_branch).astype(jnp.bfloat16)
    upstream = cotangent.astype(jnp.float32) * own_valid[:, None]
    upstream_low = upstream.astype(jnp.bfloat16)
    grad_hidden = jnp.einsum(
        "td,ndb->tnb", upstream_low, down_blocks, preferred_element_type=jnp.float32
    ).reshape(tok_rows, half_width)
    grad_gate_mlp = grad_hidden * up_mlp * swish_slope(gate_mlp)
    grad_up_mlp = grad_hidden * jax.nn.silu(gate_mlp)
    grad_pair = jnp.concatenate([grad_gate_mlp, grad_up_mlp], axis=1).astype(jnp.bfloat16)
    pair_view = grad_pair.reshape(tok_rows, count_up, block_width)
    grad_normed_two = lax.psum(
        jnp.einsum("tnb,ndb->td", pair_view, up_blocks, preferred_element_type=jnp.float32), "head"
    )
    grad_gains_two = jnp.sum(grad_normed_two * hidden_one * inverse_two, axis=0)
    grad_one = upstream + rms_back(hidden_one, inverse_two, norm_gains[1], grad_normed_two)
    grad_attn = grad_one.astype(jnp.bfloat16)
    grad_gated = jnp.einsum(
        "td,ndb->tnb", grad_attn, out_blocks, preferred_element_type=jnp.float32
    ).reshape(tok_rows, heads_here, DV)
    grad_gate_pre = (grad_gated * head_normed * swish_slope(gate_view)).reshape(
        tok_rows, value_width
    )
    grad_head_normed = grad_gated * swished
    grad_head_gain = jnp.sum(grad_head_normed * attended * inverse_head, axis=(0, 1))
    grad_attended = rms_back(attended, inverse_head, head_gain, grad_head_normed)
    grad_out = grad_attended.reshape(tiles, tile_len, heads_here, DV)
    weighted = jnp.einsum(
        "cthk,cthv->chkv",
        query_scaled * incoming_carry[:, :, None, None],
        grad_out,
        precision=highest_precision,
    )
    local_adjoint, local_end_adj = lax.scan(
        retreat, zero_state, (tile_decay, weighted), reverse=True
    )
    reverse_run = jnp.cumprod(tile_decay[::-1], axis=0)[::-1]
    after_decay = jnp.concatenate([reverse_run[1:], unit_decay[None]], axis=0)
    outgoing = carried_in(
        (device_decay, local_adjoint), "seq", compose, (unit_decay, zero_state), True
    )[1]
    end_adjoint = after_decay[..., None] * outgoing[None] + local_end_adj
    end_state = tile_decay[..., None] * start_state + contrib
    grad_scores = (
        jnp.einsum("cthv,cshv->chts", grad_out, values_all, precision=highest_precision)
        * pair_mask[:, None]
    )
    grad_q_scaled = jnp.einsum(
        "chts,cshk->cthk", grad_scores, k_scaled, precision=highest_precision
    ) + incoming_carry[:, :, None, None] * jnp.einsum(
        "cthv,chkv->cthk", grad_out, start_state, precision=highest_precision
    )
    grad_queries = grad_q_scaled * jnp.exp(cumulative) * score_scale
    grad_k_scaled = jnp.einsum(
        "chts,cthk->cshk", grad_scores, query_scaled, precision=highest_precision
    )
    grad_k_tail = jnp.einsum(
        "cshv,chkv->cshk", values_all, end_adjoint, precision=highest_precision
    )
    grad_keys = (
        grad_k_scaled * jnp.exp(-cumulative)
        + grad_k_tail
        * jnp.exp(final_cumulative_decay[:, None] - cumulative)
        * tail_mask[:, :, None, None]
    )
    grad_values = jnp.einsum(
        "chts,cthv->cshv", scores, grad_out, precision=highest_precision
    ) + jnp.einsum("cshk,chkv->cshv", key_remainder, end_adjoint, precision=highest_precision)
    boundary = jnp.sum(end_adjoint * end_state, axis=-1)
    grad_cumul = queries * grad_queries - keys_all * grad_keys
    grad_cumul = jnp.concatenate(
        [grad_cumul[:, :-1], grad_cumul[:, -1:] + boundary[:, None]], axis=1
    )
    grad_log_gates = jnp.cumsum(grad_cumul[:, ::-1], axis=1)[:, ::-1]
    grad_active = jnp.concatenate(
        [
            grad_queries.reshape(tok_rows, key_width),
            grad_keys.reshape(tok_rows, key_width),
            grad_values.reshape(tok_rows, value_width),
        ],
        axis=1,
    )
    grad_conv = grad_active * swish_slope(conv_pre)
    grad_extended = jnp.zeros((tok_rows + tap_count - 1, channels), jnp.float32)
    tap_grads = []
    for tap_index in range(tap_count):
        grad_extended = grad_extended + jnp.pad(
            conv_weight[tap_index] * same_seg[tap_index] * grad_conv,
            ((tap_index, tap_count - 1 - tap_index), (0, 0)),
        )
        tap_grads.append(
            jnp.sum(
                same_seg[tap_index] * extended[tap_index : tap_index + tok_rows] * grad_conv, axis=0
            )
        )
    grad_conv_weight = jnp.stack(tap_grads)
    returned = passed_along(grad_extended[: tap_count - 1], "seq", -1)
    grad_mixed = grad_extended[tap_count - 1 :] + jnp.concatenate(
        [jnp.zeros((tok_rows - (tap_count - 1), channels), jnp.float32), returned], axis=0
    )
    grad_logits = grad_log_gates.reshape(tok_rows, key_width) / gate_scale * jax.nn.sigmoid(-logits)
    grad_upper = jnp.concatenate(
        [
            jnp.einsum("tr,tk->rk", lowrank, grad_logits, precision=highest_precision),
            jnp.sum(grad_logits, axis=0, keepdims=True),
        ],
        axis=0,
    )
    grad_lowrank = jnp.einsum(
        "tk,rk->tr", grad_logits, gate_up[:rank_width], precision=highest_precision
    ).astype(jnp.bfloat16)
    grad_down_part = jnp.einsum(
        "td,tr->dr", normed, grad_lowrank, preferred_element_type=jnp.float32
    )
    grad_projected = jnp.concatenate(
        [grad_mixed.astype(jnp.bfloat16), grad_gate_pre.astype(jnp.bfloat16)], axis=1
    )
    projected_view = grad_projected.reshape(tok_rows, count_in, block_width)
    grad_normed_part = jnp.einsum(
        "tnb,ndb->td", projected_view, in_blocks, preferred_element_type=jnp.float32
    ) + jnp.einsum("tr,dr->td", grad_lowrank, down_low, preferred_element_type=jnp.float32)
    grad_normed = lax.psum(grad_normed_part.astype(jnp.bfloat16), "head").astype(jnp.float32)
    grad_gains_one = jnp.sum(grad_normed * inputs * inverse_one, axis=0)
    grad_input = grad_one + rms_back(inputs, inverse_one, norm_gains[0], grad_normed)
    slot_total = gathered.shape[0]
    block_grads = jnp.concatenate(
        [
            jnp.einsum("td,tnb->ndb", normed, projected_view, preferred_element_type=jnp.float32),
            jnp.einsum("td,tnb->ndb", normed_two, pair_view, preferred_element_type=jnp.float32),
            jnp.einsum("td,tnb->ndb", grad_attn, gated_view, preferred_element_type=jnp.float32),
            jnp.einsum(
                "td,tnb->ndb", upstream_low, hidden_view, preferred_element_type=jnp.float32
            ),
        ],
        axis=0,
    )
    slot_grads = (
        jnp.zeros((slot_total, model_width, block_width), jnp.float32)
        .at[owner_row]
        .set(block_grads)
    )
    owned_grads = lax.psum_scatter(slot_grads, "seq", scatter_dimension=0, tiled=True)
    rotated = jnp.einsum("sij,sik->sjk", basis_left, owned_grads, precision=highest_precision)
    rotated = jnp.einsum("sjk,skl->sjl", rotated, basis_right, precision=highest_precision)
    first_next = moment_decay * slot_first + (1.0 - moment_decay) * rotated
    second_next = moment_decay * slot_second + (1.0 - moment_decay) * rotated * rotated
    direction = first_next / (jnp.sqrt(second_next) + adam_epsilon)
    restored = jnp.einsum("sij,sjk->sik", basis_left, direction, precision=highest_precision)
    restored = jnp.einsum("sik,slk->sil", restored, basis_right, precision=highest_precision)
    master_next = slot_master - rate_block * restored
    first_head = (head_index == 0).astype(jnp.float32)
    head_pick = (jnp.arange(head_count, dtype=jnp.int32) == head_index).astype(jnp.float32)
    upper_spread = (head_pick[None, :, None] * grad_upper[:, None, :]).reshape(
        rank_width + 1, head_count * key_width
    )
    conv_spread = (head_pick[None, :, None] * grad_conv_weight[:, None, :]).reshape(
        tap_count, head_count * channels
    )
    gains_grad, head_grad, down_grad, upper_all, conv_all = lax.psum(
        (
            jnp.stack([grad_gains_one, grad_gains_two]) * first_head,
            grad_head_gain,
            grad_down_part,
            upper_spread,
            conv_spread,
        ),
        ("seq", "head"),
    )
    upper_grad = lax.dynamic_slice_in_dim(upper_all, head_index * key_width, key_width, 1)
    conv_grad = lax.dynamic_slice_in_dim(conv_all, head_index * channels, channels, 1)
    gains_next, gains_first_next, gains_second_next = plain_adam(
        norm_gains, gains_grad, gains_first, gains_second, rate_gains
    )
    down_next, down_first_next, down_second_next = plain_adam(
        gate_down, down_grad, down_first, down_second, rate_down
    )
    upper_next, upper_first_next, upper_second_next = plain_adam(
        gate_up, upper_grad, upper_first, upper_second, rate_upper
    )
    head_next, head_first_next, head_second_next = plain_adam(
        head_gain, head_grad, head_first, head_second, rate_head
    )
    conv_next, conv_first_next, conv_second_next = plain_adam(
        conv_weight, conv_grad, conv_first, conv_second, rate_conv
    )
    return (
        result,
        grad_input,
        owned_grads,
        master_next,
        first_next,
        second_next,
        master_next.astype(jnp.bfloat16),
        gains_grad,
        gains_next,
        gains_first_next,
        gains_second_next,
        down_grad,
        down_next,
        down_first_next,
        down_second_next,
        upper_grad,
        upper_next,
        upper_first_next,
        upper_second_next,
        head_grad,
        head_next,
        head_first_next,
        head_second_next,
        conv_grad,
        conv_next,
        conv_first_next,
        conv_second_next,
    )


def solution(mesh):
    placed = (
        P("seq", None),
        P("seq", None),
        P(),
        P(),
        P("head", None),
        P(("seq", "head"), None, None),
        P(("seq", "head"), None, None),
        P(("seq", "head"), None, None),
        P(("seq", "head"), None, None),
        P(("seq", "head"), None, None),
        P(("seq", "head"), None, None),
        P(),
        P(),
        P(),
        P(),
        P(),
        P(),
        P(None, "head"),
        P(None, "head"),
        P(None, "head"),
        P(),
        P(),
        P(),
        P(None, "head"),
        P(None, "head"),
        P(None, "head"),
    )
    return jax.shard_map(
        body,
        mesh=mesh,
        in_specs=placed,
        out_specs=(
            P("seq", None),
            P("seq", None),
            P(("seq", "head"), None, None),
            P(("seq", "head"), None, None),
            P(("seq", "head"), None, None),
            P(("seq", "head"), None, None),
            P(("seq", "head"), None, None),
            P(),
            P(),
            P(),
            P(),
            P(),
            P(),
            P(),
            P(),
            P(None, "head"),
            P(None, "head"),
            P(None, "head"),
            P(None, "head"),
            P(),
            P(),
            P(),
            P(),
            P(None, "head"),
            P(None, "head"),
            P(None, "head"),
            P(None, "head"),
        ),
        check_vma=False,
    )
```

profile of v0, /device:TPU:30, one launch (start us, length us, event | category | flops | bytes accessed | tf_op | source)
XLA Modules:
  0.0 1892.5 jit_solution(9444922759656485524)
XLA Ops:
  24.0 176.6 %all-gather.6.cloned.1.call-done = bf16[64,1024,128]{2,1,0:T(8,128)(2,1)} async-done(((bf16[4,1024,128]{2,1,0:T(8,128)(2,1)}), bf16[64,1024,128]{2,1,0:T(8,128)(2,1)}) %all-gather.6.cloned.1.call-update) | async-done | bytes 16777232 | tf_op jit(solution)/shard_map/all_gather | solution.py:151
  200.6 12.4 gather_fusion
  213.0 17.5 copy.243
  230.5 7.3 broadcast_select_fusion
  270.3 7.3 fusion.51
  280.1 55.2 %while.58 = (s32[]{:T(128)}, f32[2,128,256]{2,1,0:T(8,128)}, f32[16,2,128,256]{3,2,1,0:T(8,128)}, f32[16,2,128]{2,1,0:T(2,128)S(1)}, f32[16,2,128,256]{3,2,1,0:T(8,128)}, /*index=5*/s32[]{:T(128)}, s32[]{:T(128)}) while((s32[]{:T(128)}, f32[2,128,256]{2,1,0:T(8,128)}, f32[16,2,128,256]{3,2,1,0:T(8,128)}, ...), condition=%wide.region_8.10_spmd.clone, body=%wide.region_7.9_spmd.clone.sunk | while | flops 262147 | bytes 1313900 | solution.py:213
  336.1 35.7 %all_gather.19 = f32[16,2,128]{2,1,0:T(2,128)S(1)} all-gather(f32[1,2,128]{2,1,0:T(2,128)S(1)} %slice.185), channel_id=1, replica_groups=mesh['seq'=16,'head'=2] {'seq'}, dimensions={0}, use_global_device_ids=true | all-gather | bytes 17408 | tf_op jit(solution)/shard_map/all_gather | solution.py:32
  383.9 27.2 %all-gather.8.cloned.1.call-done = f32[32,128,256]{2,1,0:T(8,128)} async-done(((f32[2,128,256]{2,1,0:T(8,128)}), f32[32,128,256]{2,1,0:T(8,128)}) %all-gather.8.cloned.1.call-update) | async-done | bytes 4194320 | tf_op jit(solution)/shard_map/all_gather | solution.py:32
  411.2 27.6 %while.59 = (s32[]{:T(128)}, f32[2,128,256]{2,1,0:T(8,128)}, s32[]{:T(128)}, f32[16,2,128]{2,1,0:T(2,128)S(1)}, f32[16,2,128,256]{3,2,1,0:T(8,128)}, /*index=5*/s32[]{:T(128)}, s32[]{:T(128)}) while((s32[]{:T(128)}, f32[2,128,256]{2,1,0:T(8,128)}, s32[]{:T(128)}, f32[16,2,128]{2,1,0:T(2,128)S(1)}, ...), condition=%wide.region_10.12_spmd.clone, body=%wide.region_9.11_spmd.clone.sunk | while | flops 262148 | bytes 789617 | solution.py:44
  438.8 8.0 multiply_reduce_fusion.10
  464.9 29.0 %all-reduce.15.cloned.1.call-done = f32[1024,1024]{1,0:T(8,128)} async-done(((f32[1024,1024]{1,0:T(8,128)}), f32[1024,1024]{1,0:T(8,128)}) %all-reduce.15.cloned.1.call-update) | async-done | bytes 4194320 | tf_op jit(solution)/shard_map/psum | solution.py:235
  498.4 9.4 convolution_bitcast_fusion
  507.8 11.1 fusion.3
  528.1 11.2 fusion.27
  539.3 29.7 %all-reduce.17.cloned.1.call-done = f32[1024,1024]{1,0:T(8,128)} async-done(((f32[1024,1024]{1,0:T(8,128)}), f32[1024,1024]{1,0:T(8,128)}) %all-reduce.17.cloned.1.call-update) | async-done | bytes 4194320 | tf_op jit(solution)/shard_map/psum | solution.py:261
  616.5 55.4 %while.60 = (s32[]{:T(128)}, f32[2,128,256]{2,1,0:T(8,128)}, f32[16,2,128,256]{3,2,1,0:T(8,128)}, f32[16,2,128,256]{3,2,1,0:T(8,128)}, f32[16,2,128]{2,1,0:T(2,128)S(1)}, /*index=5*/s32[]{:T(128)}, s32[]{:T(128)}, s32[]{:T(128)}) while((s32[]{:T(128)}, f32[2,128,256]{2,1,0:T(8,128)}, f32[16,2,128,256]{3,2,1,0:T(8,128)}, ...), condition=%wide.region_20.22_spmd.clone, body=%wide.region_19.21_spmd.clone.sunk | while | flops 262148 | bytes 1313920 | solution.py:283
  672.8 7.6 bitcast_convert_fusion
  696.7 49.9 %all-gather.10.cloned.1.call-done = f32[32,128,256]{2,1,0:T(8,128)} async-done(((f32[2,128,256]{2,1,0:T(8,128)}), f32[32,128,256]{2,1,0:T(8,128)}) %all-gather.10.cloned.1.call-update) | async-done | bytes 4194320 | tf_op jit(solution)/shard_map/all_gather | solution.py:32
  751.3 37.7 %while.61 = (s32[]{:T(128)}, f32[2,128,256]{2,1,0:T(8,128)}, s32[]{:T(128)}, f32[16,2,128]{2,1,0:T(2,128)}, f32[16,2,128,256]{3,2,1,0:T(8,128)}, /*index=5*/s32[]{:T(128)}, s32[]{:T(128)}) while((s32[]{:T(128)}, f32[2,128,256]{2,1,0:T(8,128)}, s32[]{:T(128)}, f32[16,2,128]{2,1,0:T(2,128)}, f32[16,2,128,256]{3,2,1,0:T(8,128)}, ...), condition=%wide.region_22.24_spmd.clone, body=%wide.region_21.23_spmd.clone.sunk | while | flops 262148 | bytes 789617 | solution.py:44
  843.3 8.9 fusion.19
  853.7 7.1 convolution_bitcast_fusion.3
  860.9 9.7 convolution_bitcast_fusion.1
  876.6 7.7 convolution_bitcast_fusion.2
  888.2 19.6 %pad_maximum_fusion = f32[49,1024,128]{1,2,0:T(8,128)} fusion(f32[11,1024,128]{1,2,0:T(8,128)} %convolution_bitcast_fusion.3, f32[4,1024,128]{1,2,0:T(8,128)} %fusion.53, f32[22,1024,128]{1,2,0:T(8,128)} %convolution_bitcast_fusion.1, f32[12,1024,128]{1,2,0:T(8,128)} %convolution_bitcast_fusion.2), kind=kLoop, calls=%fused_computation.15 | loop fusion | flops 19267584 | bytes 51380224 | tf_op jit(solution)/shard_map/concatenate | solution.py:375
  907.8 25.7 %copy.290 = f32[49,1024,128]{2,1,0:T(8,128)} copy(f32[49,1024,128]{1,2,0:T(8,128)} %pad_maximum_fusion) | data formatting | bytes 51380224 | tf_op jit(solution)/shard_map/concatenate | solution.py:375
  933.6 11.1 broadcast_in_dim.48
  944.6 48.1 %scatter_fusion = f32[64,1024,128]{2,1,0:T(8,128)} fusion(f32[64,1024,128]{2,1,0:T(8,128)} %broadcast_in_dim.48, s32[49]{0:T(128)S(1)} %copy-done.98, f32[49,1024,128]{2,1,0:T(8,128)} %copy.290), kind=kCustom, calls=%fused_computation.2 | custom fusion | bytes 77070528 | tf_op jit(solution)/shard_map/scatter | solution.py:389
  992.8 14.0 all-reduce.19.cloned.1.call-done
  1016.5 123.2 %all-reduce.21.cloned.1.call-done = (f32[2,1024]{1,0:T(2,128)}, f32[17,512]{1,0:T(8,128)}, f32[256]{0:T(256)}, f32[4,2048]{1,0:T(4,128)}) async-done(((f32[2,1024]{1,0:T(2,128)}, f32[17,512]{1,0:T(8,128)}, f32[256]{0:T(256)}, f32[4,2048]{1,0:T(4,128)}), (f32[2,1024]{1,0:T(2,128)}, f32[17,512]{1,0:T(8,128)}, f32[256]{0:T(256)}, f32[4,2048]{1,0:T(4,128)})) %all-reduce.21.cloned.1.call-update) | async-done | bytes 76816 | tf_op jit(solution)/shard_map/psum | solution.py:408
  1145.0 684.6 %reduce-scatter.2.cloned.1.call-done = f32[4,1024,128]{2,1,0:T(8,128)} async-done(((f32[64,1024,128]{2,1,0:T(8,128)}), f32[4,1024,128]{2,1,0:T(8,128)}) %reduce-scatter.2.cloned.1.call-update) | async-done | bytes 2097168 | tf_op jit(solution)/shard_map/reduce_scatter | solution.py:391
  1829.6 30.2 %fusion.152 = f32[4,128,1024]{1,2,0:T(8,128)S(1)} fusion(f32[4,1024,128]{2,1,0:T(8,128)} %reduce-scatter.2.cloned.1.call-done, f32[4,1024,1024]{2,1,0:T(8,128)} %param.45), kind=kOutput, calls=%fused_computation.280 | convolution fusion | flops 6442450944 | bytes 20971520 | tf_op jit(solution)/shard_map/sij,sik->sjk/dot_general | solution.py:392
  1864.3 15.1 fusion.34
  (567 shorter events, 431.9 us)
Async XLA Ops:
  7.2 1852.6 %copy-start = (f32[4,128,128]{2,1,0:T(8,128)S(1)}, f32[4,128,128]{2,1,0:T(8,128)}, u32[]{:S(2)}) copy-start(f32[4,128,128]{2,1,0:T(8,128)} %param.46) | copy-start | bytes 786436
  7.2 193.3 %all-gather.6.cloned.1.call-start = ((), (), s32[]{:S(2)}) async-start(), calls=%async_computation.1 | async-start | bytes 17825792 | tf_op jit(solution)/shard_map/all_gather | solution.py:151
  8.0 403.2 %all-gather.8.cloned.1.call-start = ((), (), s32[]{:S(2)}) async-start(), calls=%async_computation.6 | async-start | bytes 4456448 | tf_op jit(solution)/shard_map/all_gather | solution.py:32
  15.9 226.9 %copy-start.62 = (f32[1024]{0:T(1024)}, f32[1024]{0:T(1024)S(1)}, u32[]{:S(2)}) copy-start(f32[1024]{0:T(1024)S(1)} %add_rsqrt_fusion.2) | copy-start | bytes 12292
  16.7 226.1 %copy-start.64 = (f32[1,1024]{1,0:T(1,128)}, f32[1,1024]{1,0:T(1,128)S(1)}, u32[]{:S(2)}) copy-start(f32[1,1024]{1,0:T(1,128)S(1)} %get-tuple-element.578) | copy-start | bytes 12292
  23.2 234.1 %copy-start.66 = (f32[1,1024]{1,0:T(1,128)}, f32[1,1024]{1,0:T(1,128)S(1)}, u32[]{:S(2)}) copy-start(f32[1,1024]{1,0:T(1,128)S(1)} %get-tuple-element.573) | copy-start | bytes 12292
  23.2 234.1 %copy-start.68 = (f32[1,1024]{1,0:T(1,128)}, f32[1,1024]{1,0:T(1,128)S(1)}, u32[]{:S(2)}) copy-start(f32[1,1024]{1,0:T(1,128)S(1)} %get-tuple-element.574) | copy-start | bytes 12292
  23.2 234.1 %copy-start.70 = (f32[1,1024]{1,0:T(1,128)}, f32[1,1024]{1,0:T(1,128)S(1)}, u32[]{:S(2)}) copy-start(f32[1,1024]{1,0:T(1,128)S(1)} %get-tuple-element.575) | copy-start | bytes 12292
  23.2 234.1 %copy-start.72 = (f32[1,1024]{1,0:T(1,128)}, f32[1,1024]{1,0:T(1,128)S(1)}, u32[]{:S(2)}) copy-start(f32[1,1024]{1,0:T(1,128)S(1)} %get-tuple-element.576) | copy-start | bytes 12292
  251.1 5.5 collective-permute-start
  280.1 55.4 %copy-start.81 = (f32[256]{0:T(256)S(1)}, f32[256]{0:T(256)}, u32[]{:S(2)}) copy-start(f32[256]{0:T(256)} %param.56) | copy-start | bytes 3076
  335.4 158.5 %all-reduce.15.cloned.1.call-start = ((), (), s32[]{:S(2)}) async-start(), calls=%async_computation.2 | async-start | bytes 8388608 | tf_op jit(solution)/shard_map/psum | solution.py:235
  464.1 104.9 %all-reduce.17.cloned.1.call-start = ((), (), s32[]{:S(2)}) async-start(), calls=%async_computation.3 | async-start | bytes 8388608 | tf_op jit(solution)/shard_map/psum | solution.py:261
  464.9 109.4 %copy-start.84 = (f32[1024]{0:T(1024)}, f32[1024]{0:T(1024)S(1)}, u32[]{:S(2)}) copy-start(f32[1024]{0:T(1024)S(1)} %fusion.117) | copy-start | bytes 12292
  539.3 207.4 %all-gather.10.cloned.1.call-start = ((), (), s32[]{:S(2)}) async-start(), calls=%async_computation.7 | async-start | bytes 4456448 | tf_op jit(solution)/shard_map/all_gather | solution.py:32
  671.9 212.4 %all-reduce.23.cloned.1.call-start = ((), (), s32[]{:S(2)}) async-start(), calls=%async_computation.9 | async-start | bytes 8388608 | tf_op jit(solution)/shard_map/psum | solution.py:250
  832.6 6.1 collective-permute-start.1
  852.1 154.6 %all-reduce.19.cloned.1.call-start = ((), (), s32[]{:S(2)}) async-start(), calls=%async_computation.5 | async-start | bytes 131072 | tf_op jit(solution)/shard_map/psum | solution.py:408
  876.5 263.1 %all-reduce.21.cloned.1.call-start = ((), (), s32[]{:S(2)}) async-start(), calls=%async_computation.8 | async-start | bytes 182272 | tf_op jit(solution)/shard_map/psum | solution.py:408
  888.2 941.5 %reduce-scatter.2.cloned.1.call-start = ((), (), s32[]{:S(2)}) async-start(), calls=%async_computation.4 | async-start | bytes 35651584 | tf_op jit(solution)/shard_map/reduce_scatter | solution.py:391
  1013.4 126.3 %copy-start.83 = (f32[256]{0:T(256)S(1)}, f32[256]{0:T(256)}, u32[]{:S(2)}) copy-start(f32[256]{0:T(256)} %param.56) | copy-start | bytes 3076
  1013.4 126.3 %copy-start.99 = (f32[256]{0:T(256)S(1)}, f32[256]{0:T(256)}, u32[]{:S(2)}) copy-start(f32[256]{0:T(256)} %param.57) | copy-start | bytes 3076
  1013.4 126.3 %copy-start.100 = (f32[256]{0:T(256)S(1)}, f32[256]{0:T(256)}, u32[]{:S(2)}) copy-start(f32[256]{0:T(256)} %param.58) | copy-start | bytes 3076
  1013.4 127.6 %copy-start.75 = (f32[2,1024]{1,0:T(2,128)S(1)}, f32[2,1024]{1,0:T(2,128)}, u32[]{:S(2)}) copy-start(f32[2,1024]{1,0:T(2,128)} %param.47) | copy-start | bytes 24580
  1013.4 127.5 %copy-start.93 = (f32[2,1024]{1,0:T(2,128)S(1)}, f32[2,1024]{1,0:T(2,128)}, u32[]{:S(2)}) copy-start(f32[2,1024]{1,0:T(2,128)} %param.48) | copy-start | bytes 24580
  1013.4 127.5 %copy-start.94 = (f32[2,1024]{1,0:T(2,128)S(1)}, f32[2,1024]{1,0:T(2,128)}, u32[]{:S(2)}) copy-start(f32[2,1024]{1,0:T(2,128)} %param.49) | copy-start | bytes 24580
  1013.4 128.9 %copy-start.61 = (f32[4,1024]{1,0:T(4,128)S(1)}, f32[4,1024]{1,0:T(4,128)}, u32[]{:S(2)}) copy-start(f32[4,1024]{1,0:T(4,128)} %param.59) | copy-start | bytes 49156
  1013.4 128.8 %copy-start.91 = (f32[4,1024]{1,0:T(4,128)S(1)}, f32[4,1024]{1,0:T(4,128)}, u32[]{:S(2)}) copy-start(f32[4,1024]{1,0:T(4,128)} %param.60) | copy-start | bytes 49156
  1013.5 128.8 %copy-start.92 = (f32[4,1024]{1,0:T(4,128)S(1)}, f32[4,1024]{1,0:T(4,128)}, u32[]{:S(2)}) copy-start(f32[4,1024]{1,0:T(4,128)} %param.61) | copy-start | bytes 49156
  1013.5 130.2 %copy-start.77 = (f32[17,256]{1,0:T(8,128)S(1)}, f32[17,256]{1,0:T(8,128)}, u32[]{:S(2)}) copy-start(f32[17,256]{1,0:T(8,128)} %param.54) | copy-start | bytes 52228
  1013.5 130.2 %copy-start.78 = (f32[17,256]{1,0:T(8,128)S(1)}, f32[17,256]{1,0:T(8,128)}, u32[]{:S(2)}) copy-start(f32[17,256]{1,0:T(8,128)} %param.55) | copy-start | bytes 52228
  1829.6 34.6 %slice-start.4 = ((s8[16777216]{0:T(1024)(128)(4,1)}), s8[4194304]{0:T(1024)(128)(4,1)S(1)}, s32[]{:S(2)}) async-start(s8[16777216]{0:T(1024)(128)(4,1)} %bitcast.242), calls=%async_computation.14 | async-start | bytes 8388608
  (93 other events, 526.8 us)
Sparse Core Ops, SparseCore 0:
  10.8 189.6 all-gather.5
  335.5 75.6 all-gather.7
  464.2 29.6 all-reduce.14
  539.4 29.5 all-reduce.16
  672.0 74.6 all-gather.9
  852.3 30.4 all-reduce.22
  889.8 116.8 all-reduce.18
  1015.5 124.0 all-reduce.20
  1142.7 686.8 reduce-scatter.1
where the time goes:
time: 1910 us; the launch traced here: 1890 us
  waiting for transfers between devices  1140 us (60%)
  other arithmetic  277 us (15%)
  local copies, waits for them, and re-layouts  216 us (11%)
  matrix products  205 us (11%)
  blocking collectives  35.7 us (2%)
    reduce_scatter x1, waiting for transfers between devices, body(): lax.psum_scatter(slot_grads, 'seq', scatter_dimension=0, tiled=True)  685 us
    all_gather x1, waiting for transfers between devices, body(): gathered = lax.all_gather(slot_copy, 'seq', axis=0, tiled=True)  177 us
    psum x2, waiting for transfers between devices, body(): lax.psum((jnp.stack([grad_gains_one, grad_gains_two]) * first_head, grad_...  137 us
    all_gather x2, waiting for transfers between devices, carried_in(): pieces = jax.tree.map(lambda part: lax.all_gather(part, axis), value)  77.2 us
    select_n x30, other arithmetic, step(): jnp.where(position < mine, new, old)  54.9 us
    dynamic_update_slice x32, other arithmetic, body(): lax.scan(advance, zero_state, (tile_decay, contrib))  51.9 us
    scatter x1, local copies, waits for them, and re-layouts, body(): slot_grads = jnp.zeros((slot_total, model_width, block_width), jnp.float3...  48.1 us
  transfers between devices with their start and end apart: 11, of which 9 were waited for; matrix products, arithmetic and copies ran while one was open for 11% of the time, Pallas kernels for 0%

commit v1 on v0

--- a/solution.py
+++ b/solution.py
@@ -1,7 +1,13 @@
+import functools
+
 import jax
 import jax.numpy as jnp
 from jax import lax
+from jax.experimental import pallas as pl
+from jax.experimental.pallas import tpu as pltpu
 from jax.sharding import PartitionSpec as P
+
+MESH = pl.DeviceIdType.MESH
 
 DK = 128
 DV = 256
@@ -19,6 +25,286 @@
 rate_upper = 0.6
 rate_head = 0.5
 rate_conv = 0.1
+
+
+def axis_sizes(n):
+    side=1
+    while (side*2)**2*4<=n: side*=2
+    return (n//(side*side),side,side)
+
+def coords(me,sizes):
+    Z,Y,X=sizes
+    return [me//(Y*X),(me//X)%Y,me%X]
+
+def index_of(c,sizes):
+    Z,Y,X=sizes
+    return (c[0]*Y+c[1])*X+c[2]
+
+def enter(n,me):
+    barrier=pltpu.get_barrier_semaphore()
+    for j in range(1,n):
+        pl.semaphore_signal(barrier,inc=1,device_id={"seq":lax.rem(me+j,n)},device_id_type=MESH)
+    pl.semaphore_wait(barrier,n-1)
+
+def remote(src,dst,ss,rs,peer):
+    return pltpu.make_async_remote_copy(src_ref=src,dst_ref=dst,send_sem=ss,recv_sem=rs,device_id={"seq":peer},device_id_type=MESH)
+
+def gather_kernel(n,sizes,plan,owners_ref,slot_ref,out_ref,recv,piece,a_send,a_recv,g_send,g_recv,l_sem):
+    me=lax.axis_index("seq"); c=coords(me,sizes)
+    sd=slot_ref.shape[0]; rows=piece.shape[0]; bw=slot_ref.shape[2]; nb=owners_ref.shape[1]
+    enter(n,me)
+    def a2a(j):
+        p=lax.rem(me+j,n)
+        return remote(slot_ref.at[:,pl.ds(p*rows,rows),:],recv.at[pl.ds(me*sd,sd)],a_send.at[j],a_recv.at[j],p)
+    for j in range(1,n): a2a(j).start()
+    mine=pltpu.make_async_copy(slot_ref.at[:,pl.ds(me*rows,rows),:],recv.at[pl.ds(me*sd,sd)],l_sem.at[0])
+    mine.start(); mine.wait()
+    for j in range(1,n): a2a(j).wait()
+    for b in range(nb):
+        piece[:,b*bw:(b+1)*bw]=recv[owners_ref[0,b]]
+    own=pltpu.make_async_copy(piece,out_ref.at[c[0],c[1],c[2]],l_sem.at[1])
+    own.start()
+    def ag(i,k,j):
+        lo,hi,order=plan[i]
+        ax=order[k]
+        idx=tuple(slice(None) if a in order[:k] else c[a] for a in range(3))+(slice(None),pl.ds(lo*bw,(hi-lo)*bw))
+        d=list(c); d[ax]=lax.rem(c[ax]+j,sizes[ax])
+        src=piece.at[:,pl.ds(lo*bw,(hi-lo)*bw)] if k==0 else out_ref.at[idx]
+        s=(i*3+k)*max(sizes)+j
+        return remote(src,out_ref.at[idx],g_send.at[s],g_recv.at[s],index_of(d,sizes))
+    own.wait()
+    streams={}
+    for i,p in enumerate(plan): streams.setdefault(p[2],[]).append(i)
+    longest=max([len(v) for v in streams.values()],default=0)
+    for s in range(longest+2 if plan else 0):
+        for k in (2,1,0):
+            for order,ids in streams.items():
+                if not 0<=s-k<len(ids): continue
+                i=ids[s-k]
+                if k:
+                    for j in range(1,sizes[order[k-1]]): ag(i,k-1,j).wait_recv()
+                for j in range(1,sizes[order[k]]): ag(i,k,j).start()
+    for i in range(len(plan)):
+        for j in range(1,sizes[plan[i][2][2]]): ag(i,2,j).wait_recv()
+    for k in range(3):
+        for i in range(len(plan)):
+            for j in range(1,sizes[plan[i][2][k]]): ag(i,k,j).wait_send()
+
+def gather_weights(slot_copy,owners,plan):
+    n=lax.axis_size("seq"); sizes=axis_sizes(n)
+    sd,d,bw=slot_copy.shape; nb=owners.shape[1]; rows=d//n
+    out=pl.pallas_call(functools.partial(gather_kernel,n,sizes,plan),
+        out_shape=jax.ShapeDtypeStruct(sizes+(rows,nb*bw),slot_copy.dtype),
+        in_specs=[pl.BlockSpec(memory_space=pltpu.SMEM),pl.BlockSpec(memory_space=pl.ANY)],
+        out_specs=pl.BlockSpec(memory_space=pl.ANY),
+        scratch_shapes=[pltpu.VMEM((n*sd,rows,bw),slot_copy.dtype),pltpu.VMEM((rows,nb*bw),slot_copy.dtype),
+            pltpu.SemaphoreType.DMA((n,)),pltpu.SemaphoreType.DMA((n,)),
+            pltpu.SemaphoreType.DMA((len(plan)*3*max(sizes),)),pltpu.SemaphoreType.DMA((len(plan)*3*max(sizes),)),
+            pltpu.SemaphoreType.DMA((2,))],
+        compiler_params=pltpu.CompilerParams(collective_id=1,has_side_effects=True,vmem_limit_bytes=48<<20),
+    )(owners,slot_copy)
+    return out.reshape(d,nb*bw)
+
+def scatter_kernel(n,sizes,plan,nin,inv_ref,*refs):
+    g_refs=refs[:nin]; out_ref=refs[nin];
+    np_=len(plan)
+    sc=refs[nin+1:]
+    own=sc[0:np_]; b0=sc[np_:2*np_]; b1=sc[2*np_:3*np_]; b2=sc[3*np_:4*np_]
+    fin,send,r_send,r_recv,a_send,a_recv,l_sem=sc[4*np_:]
+    me=lax.axis_index("seq"); c=coords(me,sizes)
+    sd,_,rows,bw=out_ref.shape
+    nb=fin.shape[0]-1
+    bufs=(b0,b1,b2)
+    def part(view,done,left,coord):
+        pass
+    enter(n,me)
+    loads=[]
+    for i,(a,lo,hi,base,order) in enumerate(plan):
+        ax=order[0]
+        idx=tuple(c[ax] if q==ax else slice(None) for q in range(3))+(slice(None),pl.ds(lo*bw,(hi-lo)*bw))
+        cp=pltpu.make_async_copy(g_refs[a].at[idx],own[i],l_sem.at[i]); cp.start(); loads.append(cp)
+    def rs(i,k,j):
+        a,lo,hi,base,order=plan[i]
+        ax=order[k]
+        d=list(c); d[ax]=lax.rem(c[ax]+j,sizes[ax])
+        left=sorted(set(range(3))-set(order[:k]))
+        idx=tuple(d[ax] if q==ax else slice(None) for q in left)
+        if k==0: src=g_refs[a].at[idx+(slice(None),pl.ds(lo*bw,(hi-lo)*bw))]
+        elif k==1: src=own[i].at[idx]
+        else: src=b1[i].at[(0,)+idx]
+        dst=bufs[k][i].at[j]
+        s=(i*3+k)*max(sizes)+j
+        return remote(src,dst,r_send.at[s],r_recv.at[s],index_of(d,sizes))
+    fin[nb]=jnp.zeros(fin.shape[1:],fin.dtype)
+    def combine(i,k):
+        a,lo,hi,base,order=plan[i]
+        if k==0: loads[i].wait()
+        for j in range(1,sizes[order[k]]): rs(i,k,j).wait_recv()
+        if k==0:
+            s0,s1=own[i].shape[0],own[i].shape[1]
+            def add0(t,_):
+                u,v=t//s1,t%s1
+                tot=own[i][u,v].astype(jnp.float32)
+                for j in range(1,sizes[order[0]]): tot=tot+b0[i][j,u,v].astype(jnp.float32)
+                own[i][u,v]=tot.astype(own[i].dtype)
+                return 0
+            lax.fori_loop(0,s0*s1,add0,0)
+        elif k==1:
+            pos=sorted(set(range(3))-set(order[:1])).index(order[1])
+            def add1(t,_):
+                at=(c[order[1]],t) if pos==0 else (t,c[order[1]])
+                tot=own[i][at].astype(jnp.float32)
+                for j in range(1,sizes[order[1]]): tot=tot+b1[i][j,t].astype(jnp.float32)
+                b1[i][0,t]=tot.astype(own[i].dtype)
+                return 0
+            lax.fori_loop(0,sizes[order[2]],add1,0)
+        else:
+            tot=b1[i][0,c[order[2]]].astype(jnp.float32)
+            for j in range(1,sizes[order[2]]): tot=tot+b2[i][j].astype(jnp.float32)
+            for b in range(lo,hi): fin[base+b-lo]=tot[:,(b-lo)*bw:(b-lo+1)*bw].astype(fin.dtype)
+    streams={}
+    for i,p in enumerate(plan): streams.setdefault(p[4],[]).append(i)
+    longest=max([len(v) for v in streams.values()],default=0)
+    for s in range(longest+3 if plan else 0):
+        for k in range(4):
+            for order,ids in streams.items():
+                if not 0<=s-k<len(ids): continue
+                i=ids[s-k]
+                if k: combine(i,k-1)
+                if k<3:
+                    for j in range(1,sizes[order[k]]): rs(i,k,j).start()
+    for s in range(send.shape[0]): send[s]=fin[inv_ref[0,s]]
+    def a2a(j):
+        p=lax.rem(me+j,n)
+        return remote(send.at[pl.ds(p*sd,sd)],out_ref.at[:,me],a_send.at[j],a_recv.at[j],p)
+    for j in range(1,n): a2a(j).start()
+    mine=pltpu.make_async_copy(send.at[pl.ds(me*sd,sd)],out_ref.at[:,me],l_sem.at[np_])
+    mine.start(); mine.wait()
+    for j in range(1,n): a2a(j).wait()
+    for k in range(3):
+        for i in range(np_):
+            for j in range(1,sizes[plan[i][4][k]]): rs(i,k,j).wait_send()
+
+def scatter_grads(grads,inverse,plan,slots_dev,nb):
+    n=lax.axis_size("seq"); sizes=axis_sizes(n)
+    d=grads[0].shape[0]; bw=128; rows=d//n
+    views=[g.reshape(sizes+(rows,g.shape[1])) for g in grads]
+    dt=grads[0].dtype
+    own=[];b0=[];b1=[];b2=[]
+    for a,lo,hi,base,order in plan:
+        w=(hi-lo)*bw
+        rem=[sizes[q] for q in range(3) if q!=order[0]]
+        own.append(pltpu.VMEM(tuple(rem)+(rows,w),dt))
+        b0.append(pltpu.VMEM((sizes[order[0]],)+tuple(rem)+(rows,w),dt))
+        b1.append(pltpu.VMEM((sizes[order[1]],sizes[order[2]],rows,w),dt))
+        b2.append(pltpu.VMEM((sizes[order[2]],rows,w),dt))
+    m=len(plan)*3*max(sizes)
+    out=pl.pallas_call(functools.partial(scatter_kernel,n,sizes,plan,len(views)),
+        out_shape=jax.ShapeDtypeStruct((slots_dev,n,rows,bw),dt),
+        in_specs=[pl.BlockSpec(memory_space=pltpu.SMEM)]+[pl.BlockSpec(memory_space=pl.ANY)]*len(views),
+        out_specs=pl.BlockSpec(memory_space=pl.ANY),
+        scratch_shapes=own+b0+b1+b2+[pltpu.VMEM((nb+1,rows,bw),dt),pltpu.VMEM((slots_dev*n,rows,bw),dt),
+            pltpu.SemaphoreType.DMA((m,)),pltpu.SemaphoreType.DMA((m,)),pltpu.SemaphoreType.DMA((n,)),pltpu.SemaphoreType.DMA((n,)),
+            pltpu.SemaphoreType.DMA((len(plan)+1,))],
+        compiler_params=pltpu.CompilerParams(collective_id=2,has_side_effects=True,vmem_limit_bytes=60<<20),
+    )(inverse,*views)
+    return out.reshape(slots_dev,d,bw)
+
+
+def build_plan(widths, parts, pieces, orders):
+    total = sum(widths)
+    bounds = [sum(widths[:i]) for i in range(len(widths) + 1)]
+    cuts = [round(total * f) for f in (0.0,) + parts]
+    plan, at = [], 0
+    for i in range(pieces):
+        for order, lo, hi in zip(orders, cuts[:-1], cuts[1:], strict=True):
+            size = hi - lo
+            left = size * (i + 1) // pieces - size * i // pieces
+            while left:
+                which = max(q for q in range(len(widths)) if bounds[q] <= at)
+                step = min(left, bounds[which + 1] - at)
+                start = at - bounds[which]
+                plan.append((which, start, start + step, at, order))
+                at += step
+                left -= step
+    return plan
+
+
+def sum_kernel(n, sizes, shared, x_ref, out_ref, mate, acc, bufs, send, recv):
+    me, core = lax.axis_index("seq"), lax.axis_index("head")
+    c = coords(me, sizes)
+    barrier = pltpu.get_barrier_semaphore()
+    peers = []
+    for ax in range(3):
+        for j in range(1, sizes[ax]):
+            d = list(c)
+            d[ax] = lax.rem(c[ax] + j, sizes[ax])
+            peers.append((ax, j, index_of(d, sizes)))
+    for _, _, p in peers:
+        pl.semaphore_signal(barrier, inc=1, device_id={"seq": p}, device_id_type=MESH)
+    pl.semaphore_signal(barrier, inc=1, device_id={"head": 1 - core}, device_id_type=MESH)
+    pl.semaphore_wait(barrier, len(peers) + 1)
+    swap = pltpu.make_async_remote_copy(
+        src_ref=x_ref.at[pl.ds(0, shared)],
+        dst_ref=mate,
+        send_sem=send.at[0],
+        recv_sem=recv.at[0],
+        device_id={"head": 1 - core},
+        device_id_type=MESH,
+    )
+    swap.start()
+    swap.wait()
+    acc[0, 0:shared] = x_ref[0:shared] + mate[...]
+    acc[0, shared:] = x_ref[shared:]
+    copies = []
+    for step, ax in enumerate((2, 1, 0)):
+        bufs[ax, c[ax]] = acc[step]
+        going = []
+        for q, j, p in peers:
+            if q == ax:
+                going.append(
+                    remote(
+                        acc.at[step],
+                        bufs.at[ax, c[ax]],
+                        send.at[1 + ax * max(sizes) + j],
+                        recv.at[1 + ax * max(sizes) + j],
+                        p,
+                    )
+                )
+        for copy in going:
+            copy.start()
+        for copy in going:
+            copy.wait_recv()
+        total = bufs[ax, 0]
+        for j in range(1, sizes[ax]):
+            total = total + bufs[ax, j]
+        if step < 2:
+            acc[step + 1] = total
+        else:
+            out_ref[...] = total
+        copies += going
+    for copy in copies:
+        copy.wait_send()
+
+
+def sum_small(x, shared):
+    n = lax.axis_size("seq")
+    sizes = axis_sizes(n)
+    most = max(sizes)
+    return pl.pallas_call(
+        functools.partial(sum_kernel, n, sizes, shared),
+        out_shape=jax.ShapeDtypeStruct(x.shape, x.dtype),
+        scratch_shapes=[
+            pltpu.VMEM((shared,) + x.shape[1:], x.dtype),
+            pltpu.VMEM((3,) + x.shape, x.dtype),
+            pltpu.VMEM((3, most) + x.shape, x.dtype),
+            pltpu.SemaphoreType.DMA((1 + 3 * most,)),
+            pltpu.SemaphoreType.DMA((1 + 3 * most,)),
+        ],
+        compiler_params=pltpu.CompilerParams(
+            collective_id=3, has_side_effects=True, vmem_limit_bytes=32 << 20
+        ),
+    )(x)
 
 
 def passed_along(array, axis, by):
@@ -138,8 +424,6 @@
     out_end = up_end + count_out
     score_scale = DK ** (-0.5)
     seq_index = lax.axis_index("seq")
-    head_index = lax.axis_index("head")
-    head_count = lax.axis_size("head")
     base_pos = seq_index * tok_rows
     ext_pos = base_pos - (tap_count - 1) + jnp.arange(tok_rows + tap_count - 1, dtype=jnp.int32)
     ext_seg, ext_valid = segment_of(ext_pos, lengths, packing)
@@ -148,19 +432,24 @@
     tile_prev = segment_of(
         base_pos - 1 + tile_len * jnp.arange(tiles, dtype=jnp.int32), lengths, packing
     )[0]
-    gathered = lax.all_gather(slot_copy, "seq", axis=0, tiled=True)
-    owner_row = owners[0]
-    blocks = jnp.take(gathered, owner_row, axis=0)
-    in_blocks = blocks[:count_in]
-    up_blocks = blocks[count_in:up_end]
-    out_blocks = blocks[up_end:out_end]
-    down_blocks = blocks[out_end:]
+    weights = gather_weights(
+        slot_copy,
+        owners,
+        [
+            (at, at + hi - lo, order)
+            for _, lo, hi, at, order in build_plan(
+                (block_total,), (0.43, 0.86, 1.0), 4, ((0, 1, 2), (0, 2, 1), (2, 1, 0))
+            )
+        ],
+    )
+    in_weights = weights[:, : count_in * block_width]
+    up_weights = weights[:, count_in * block_width : up_end * block_width]
+    out_weights = weights[:, up_end * block_width : out_end * block_width]
+    down_weights = weights[:, out_end * block_width :]
     inputs = tokens.astype(jnp.float32)
     inverse_one = rms_stats(inputs)
     normed = (inputs * inverse_one * norm_gains[0]).astype(jnp.bfloat16)
-    projected = jnp.einsum(
-        "td,ndb->tnb", normed, in_blocks, preferred_element_type=jnp.float32
-    ).reshape(tok_rows, count_in * block_width)
+    projected = jnp.dot(normed, in_weights, preferred_element_type=jnp.float32)
     mixed_proj = projected[:, :channels].astype(jnp.bfloat16)
     gate_pre = projected[:, channels:]
     down_low = gate_down.astype(jnp.bfloat16)
@@ -228,45 +517,36 @@
     gate_view = gate_pre.reshape(tok_rows, heads_here, DV)
     swished = jax.nn.silu(gate_view)
     gated_out = (head_normed * swished).reshape(tok_rows, value_width).astype(jnp.bfloat16)
-    gated_view = gated_out.reshape(tok_rows, count_out, block_width)
     attn_part = jnp.einsum(
-        "tnb,ndb->td", gated_view, out_blocks, preferred_element_type=jnp.float32
+        "tn,dn->td", gated_out, out_weights, preferred_element_type=jnp.float32
     )
     attn_branch = lax.psum(attn_part, "head")
     hidden_one = inputs + attn_branch
     inverse_two = rms_stats(hidden_one)
     normed_two = (hidden_one * inverse_two * norm_gains[1]).astype(jnp.bfloat16)
-    pair_proj = jnp.einsum(
-        "td,ndb->tnb", normed_two, up_blocks, preferred_element_type=jnp.float32
-    ).reshape(tok_rows, count_up * block_width)
+    pair_proj = jnp.dot(normed_two, up_weights, preferred_element_type=jnp.float32)
     half_width = pair_proj.shape[1] // 2
     gate_mlp = pair_proj[:, :half_width]
     up_mlp = pair_proj[:, half_width:]
     hidden = (jax.nn.silu(gate_mlp) * up_mlp).astype(jnp.bfloat16)
-    hidden_view = hidden.reshape(tok_rows, count_down, block_width)
-    mlp_part = jnp.einsum(
-        "tnb,ndb->td", hidden_view, down_blocks, preferred_element_type=jnp.float32
-    )
+    mlp_part = jnp.einsum("tn,dn->td", hidden, down_weights, preferred_element_type=jnp.float32)
     mlp_branch = lax.psum(mlp_part.astype(jnp.bfloat16), "head").astype(jnp.float32)
     result = (hidden_one + mlp_branch).astype(jnp.bfloat16)
     upstream = cotangent.astype(jnp.float32) * own_valid[:, None]
     upstream_low = upstream.astype(jnp.bfloat16)
-    grad_hidden = jnp.einsum(
-        "td,ndb->tnb", upstream_low, down_blocks, preferred_element_type=jnp.float32
-    ).reshape(tok_rows, half_width)
+    grad_hidden = jnp.dot(upstream_low, down_weights, preferred_element_type=jnp.float32)
     grad_gate_mlp = grad_hidden * up_mlp * swish_slope(gate_mlp)
     grad_up_mlp = grad_hidden * jax.nn.silu(gate_mlp)
     grad_pair = jnp.concatenate([grad_gate_mlp, grad_up_mlp], axis=1).astype(jnp.bfloat16)
-    pair_view = grad_pair.reshape(tok_rows, count_up, block_width)
     grad_normed_two = lax.psum(
-        jnp.einsum("tnb,ndb->td", pair_view, up_blocks, preferred_element_type=jnp.float32), "head"
+        jnp.einsum("tn,dn->td", grad_pair, up_weights, preferred_element_type=jnp.float32), "head"
     )
     grad_gains_two = jnp.sum(grad_normed_two * hidden_one * inverse_two, axis=0)
     grad_one = upstream + rms_back(hidden_one, inverse_two, norm_gains[1], grad_normed_two)
     grad_attn = grad_one.astype(jnp.bfloat16)
-    grad_gated = jnp.einsum(
-        "td,ndb->tnb", grad_attn, out_blocks, preferred_element_type=jnp.float32
-    ).reshape(tok_rows, heads_here, DV)
+    grad_gated = jnp.dot(grad_attn, out_weights, preferred_element_type=jnp.float32).reshape(
+        tok_rows, heads_here, DV
+    )
     grad_gate_pre = (grad_gated * head_normed * swish_slope(gate_view)).reshape(
         tok_rows, value_width
     )
@@ -359,36 +639,48 @@
         "tk,rk->tr", grad_logits, gate_up[:rank_width], precision=highest_precision
     ).astype(jnp.bfloat16)
     grad_down_part = jnp.einsum(
-        "td,tr->dr", normed, grad_lowrank, preferred_element_type=jnp.float32
+        "tr,td->rd", grad_lowrank, normed, preferred_element_type=jnp.float32
     )
     grad_projected = jnp.concatenate(
         [grad_mixed.astype(jnp.bfloat16), grad_gate_pre.astype(jnp.bfloat16)], axis=1
     )
-    projected_view = grad_projected.reshape(tok_rows, count_in, block_width)
     grad_normed_part = jnp.einsum(
-        "tnb,ndb->td", projected_view, in_blocks, preferred_element_type=jnp.float32
+        "tn,dn->td", grad_projected, in_weights, preferred_element_type=jnp.float32
     ) + jnp.einsum("tr,dr->td", grad_lowrank, down_low, preferred_element_type=jnp.float32)
     grad_normed = lax.psum(grad_normed_part.astype(jnp.bfloat16), "head").astype(jnp.float32)
     grad_gains_one = jnp.sum(grad_normed * inputs * inverse_one, axis=0)
     grad_input = grad_one + rms_back(inputs, inverse_one, norm_gains[0], grad_normed)
-    slot_total = gathered.shape[0]
-    block_grads = jnp.concatenate(
-        [
-            jnp.einsum("td,tnb->ndb", normed, projected_view, preferred_element_type=jnp.float32),
-            jnp.einsum("td,tnb->ndb", normed_two, pair_view, preferred_element_type=jnp.float32),
-            jnp.einsum("td,tnb->ndb", grad_attn, gated_view, preferred_element_type=jnp.float32),
-            jnp.einsum(
-                "td,tnb->ndb", upstream_low, hidden_view, preferred_element_type=jnp.float32
-            ),
-        ],
-        axis=0,
-    )
-    slot_grads = (
-        jnp.zeros((slot_total, model_width, block_width), jnp.float32)
-        .at[owner_row]
-        .set(block_grads)
-    )
-    owned_grads = lax.psum_scatter(slot_grads, "seq", scatter_dimension=0, tiled=True)
+    slots_dev = slot_copy.shape[0]
+    slot_total = slots_dev * lax.axis_size("seq")
+    grads = [
+        jnp.einsum("td,tn->dn", left, right, preferred_element_type=jnp.float32).astype(
+            jnp.bfloat16
+        )
+        for left, right in (
+            (normed, grad_projected),
+            (normed_two, grad_pair),
+            (grad_attn, gated_out),
+            (upstream_low, hidden),
+        )
+    ]
+    named = jnp.arange(slot_total, dtype=jnp.int32)[:, None] == owners
+    inverse = jnp.where(
+        jnp.any(named, axis=1),
+        jnp.sum(named * jnp.arange(block_total, dtype=jnp.int32), axis=1),
+        block_total,
+    ).astype(jnp.int32)[None]
+    owned_grads = scatter_grads(
+        grads,
+        inverse,
+        build_plan(
+            (count_in, count_up, count_out, count_down),
+            (0.43, 0.86, 1.0),
+            8,
+            ((2, 1, 0), (1, 2, 0), (0, 1, 2)),
+        ),
+        slots_dev,
+        block_total,
+    ).astype(jnp.float32)
     rotated = jnp.einsum("sij,sik->sjk", basis_left, owned_grads, precision=highest_precision)
     rotated = jnp.einsum("sjk,skl->sjl", rotated, basis_right, precision=highest_precision)
     first_next = moment_decay * slot_first + (1.0 - moment_decay) * rotated
@@ -397,26 +689,36 @@
     restored = jnp.einsum("sij,sjk->sik", basis_left, direction, precision=highest_precision)
     restored = jnp.einsum("sik,slk->sil", restored, basis_right, precision=highest_precision)
     master_next = slot_master - rate_block * restored
-    first_head = (head_index == 0).astype(jnp.float32)
-    head_pick = (jnp.arange(head_count, dtype=jnp.int32) == head_index).astype(jnp.float32)
-    upper_spread = (head_pick[None, :, None] * grad_upper[:, None, :]).reshape(
-        rank_width + 1, head_count * key_width
-    )
-    conv_spread = (head_pick[None, :, None] * grad_conv_weight[:, None, :]).reshape(
-        tap_count, head_count * channels
-    )
-    gains_grad, head_grad, down_grad, upper_all, conv_all = lax.psum(
-        (
-            jnp.stack([grad_gains_one, grad_gains_two]) * first_head,
-            grad_head_gain,
+    shared_rows, own_rows = rank_width + 8, 16
+    shared = jnp.concatenate(
+        [
             grad_down_part,
-            upper_spread,
-            conv_spread,
-        ),
-        ("seq", "head"),
-    )
-    upper_grad = lax.dynamic_slice_in_dim(upper_all, head_index * key_width, key_width, 1)
-    conv_grad = lax.dynamic_slice_in_dim(conv_all, head_index * channels, channels, 1)
+            jnp.pad(grad_head_gain, (0, model_width - grad_head_gain.shape[0]))[None],
+            jnp.zeros((7, model_width), jnp.float32),
+        ]
+    )
+    flat_upper = grad_upper.reshape(-1)
+    upper_rows = -(-flat_upper.shape[0] // model_width)
+    alone = jnp.concatenate(
+        [
+            jnp.stack([grad_gains_one, grad_gains_two]),
+            grad_conv_weight,
+            jnp.pad(flat_upper, (0, upper_rows * model_width - flat_upper.shape[0])).reshape(
+                upper_rows, model_width
+            ),
+        ]
+    )
+    alone = jnp.pad(alone, ((0, own_rows - alone.shape[0]), (0, 0)))
+    summed = sum_small(jnp.concatenate([shared, alone]), shared_rows)
+    down_grad = summed[:rank_width].T
+    head_grad = summed[rank_width, : grad_head_gain.shape[0]]
+    gains_grad = summed[shared_rows : shared_rows + 2]
+    conv_grad = summed[shared_rows + 2 : shared_rows + 2 + tap_count]
+    upper_grad = (
+        summed[shared_rows + 2 + tap_count : shared_rows + 2 + tap_count + upper_rows]
+        .reshape(-1)[: flat_upper.shape[0]]
+        .reshape(grad_upper.shape)
+    )
     gains_next, gains_first_next, gains_second_next = plain_adam(
         norm_gains, gains_grad, gains_first, gains_second, rate_gains
     )

time: 1910 us -> 1010 us (0.53)
  waiting for transfers between devices: 1140 us -> 119 us
  Pallas kernels: 0 us -> 307 us
  local copies, waits for them, and re-layouts: 216 us -> 76.3 us
  other arithmetic: 277 us -> 240 us
    reduce_scatter x1 -> x0, waiting for transfers between devices: 685 us -> none  [body(): lax.psum_scatter(slot_grads, 'seq', scatter_dimension=0, tiled=True)]
    pallas_call x0 -> x3, Pallas kernels: none -> 307 us  [the longest x1 140 us: gather_weights(): pl.pallas_call(functools.partial(gather_kernel, n, sizes, plan), out_shap...]
    all_gather x1 -> x0, waiting for transfers between devices: 177 us -> none  [body(): gathered = lax.all_gather(slot_copy, 'seq', axis=0, tiled=True)]
    psum x3 -> x1, waiting for transfers between devices: 167 us -> 29.7 us  [body(): lax.psum(jnp.einsum('tn,dn->td', grad_pair, up_weights, preferred_element...]
    scatter x1 -> x0, local copies, waits for them, and re-layouts: 48.1 us -> none  [body(): slot_grads = jnp.zeros((slot_total, model_width, block_width), jnp.float3...]
    concatenate x4 -> x2, local copies, waits for them, and re-layouts: 38 us -> 0.74 us  [the longest x1 0.59 us: body(): summed = sum_small(jnp.concatenate([shared, alone]), shared_rows)]
    gather x2 -> x0, local copies, waits for them, and re-layouts: 29.9 us -> none  [body(): blocks = jnp.take(gathered, owner_row, axis=0)]
    dot_general x9 -> x13, matrix products: 60.8 us -> 86.7 us  [the longest x4 26.2 us: body(): jnp.einsum('td,tn->dn', left, right, preferred_element_type=jnp.float32)]
  transfers between devices with their start and end apart: 11 -> 7, of which waited for: 9 -> 4; matrix products, arithmetic and copies ran while one was open for 11% -> 13% of each run, Pallas kernels for 0% -> 14%
where the time goes in v1:
time: 1010 us; the launch traced here: 995 us
  Pallas kernels  307 us (30%)
  other arithmetic  240 us (24%)
  matrix products  193 us (19%)
  waiting for transfers between devices  119 us (12%)
  local copies, waits for them, and re-layouts  76.3 us (8%)
  blocking collectives  37.6 us (4%)
  between operations  15.6 us (2%)
    pallas_call x1, Pallas kernels, gather_weights(): pl.pallas_call(functools.partial(gather_kernel, n, sizes, plan), out_shap...  140 us
    pallas_call x1, Pallas kernels, scatter_grads(): pl.pallas_call(functools.partial(scatter_kernel, n, sizes, plan, len(view...  140 us
    all_gather x2, waiting for transfers between devices, carried_in(): pieces = jax.tree.map(lambda part: lax.all_gather(part, axis), value)  60.6 us
    select_n x30, other arithmetic, step(): jnp.where(position < mine, new, old)  55.2 us
    dynamic_update_slice x32, other arithmetic, body(): lax.scan(advance, zero_state, (tile_decay, contrib))  51.9 us
    all_gather x1, blocking collectives, carried_in(): pieces = jax.tree.map(lambda part: lax.all_gather(part, axis), value)  37.6 us
    psum x1, waiting for transfers between devices, body(): lax.psum(jnp.einsum('tn,dn->td', grad_pair, up_weights, preferred_element...  29.7 us
    add x16, other arithmetic, retreat(): return (piece_pair[1] + piece_pair[0][..., None] * adjoint, adjoint)  29.5 us
  transfers between devices with their start and end apart: 7, of which 4 were waited for; matrix products, arithmetic and copies ran while one was open for 13% of the time, Pallas kernels for 14%

profile of v1, /device:TPU:30, one launch (start us, length us, event | category | flops | bytes accessed | tf_op | source)
XLA Modules:
  0.0 995.0 jit_solution(9362788144068183677)
XLA Ops:
  12.6 140.2 %shard_map.457 = bf16[4,2,2,64,6272]{4,3,2,1,0:T(8,128)(2,1)} custom-call(s32[1,49]{1,0:T(1,128)S(1)} %copy-done.2, bf16[4,1024,128]{2,1,0:T(8,128)(2,1)S(1)} %copy-done.1), custom_call_target="tpu_custom_call" | custom-call | tf_op jit(solution)/shard_map/pallas_call | solution.py:96
  152.8 7.6 fusion.151
  187.3 7.3 fusion.55
  197.1 55.3 %while.58 = (s32[]{:T(128)}, f32[2,128,256]{2,1,0:T(8,128)}, f32[16,2,128,256]{3,2,1,0:T(8,128)}, f32[16,2,128]{2,1,0:T(2,128)S(1)}, f32[16,2,128,256]{3,2,1,0:T(8,128)}, /*index=5*/s32[]{:T(128)}, s32[]{:T(128)}) while((s32[]{:T(128)}, f32[2,128,256]{2,1,0:T(8,128)}, f32[16,2,128,256]{3,2,1,0:T(8,128)}, ...), condition=%wide.region_8.10_spmd.clone, body=%wide.region_7.9_spmd.clone.sunk | while | flops 262147 | bytes 1314400 | solution.py:502
  253.1 37.6 %all_gather.16 = f32[16,2,128]{2,1,0:T(2,128)S(1)} all-gather(f32[1,2,128]{2,1,0:T(2,128)S(1)} %slice.211), channel_id=1, replica_groups=mesh['seq'=16,'head'=2] {'seq'}, dimensions={0}, use_global_device_ids=true | all-gather | bytes 17408 | tf_op jit(solution)/shard_map/all_gather | solution.py:318
  303.0 29.3 %all-gather.5.cloned.1.call-done = f32[32,128,256]{2,1,0:T(8,128)} async-done(((f32[2,128,256]{2,1,0:T(8,128)}), f32[32,128,256]{2,1,0:T(8,128)}) %all-gather.5.cloned.1.call-update) | async-done | bytes 4194320 | tf_op jit(solution)/shard_map/all_gather | solution.py:318
  332.3 27.7 %while.59 = (s32[]{:T(128)}, f32[2,128,256]{2,1,0:T(8,128)}, s32[]{:T(128)}, f32[16,2,128]{2,1,0:T(2,128)S(1)}, f32[16,2,128,256]{3,2,1,0:T(8,128)}, /*index=5*/s32[]{:T(128)}, s32[]{:T(128)}) while((s32[]{:T(128)}, f32[2,128,256]{2,1,0:T(8,128)}, s32[]{:T(128)}, f32[16,2,128]{2,1,0:T(2,128)S(1)}, ...), condition=%wide.region_10.12_spmd.clone, body=%wide.region_9.11_spmd.clone.sunk | while | flops 262148 | bytes 789609 | solution.py:330
  360.0 8.0 multiply_reduce_fusion.10
  383.0 29.0 %all-reduce.15.cloned.1.call-done = f32[1024,1024]{1,0:T(8,128)} async-done(((f32[1024,1024]{1,0:T(8,128)}), f32[1024,1024]{1,0:T(8,128)}) %all-reduce.15.cloned.1.call-update) | async-done | bytes 4194320 | tf_op jit(solution)/shard_map/psum | solution.py:523
  417.6 12.5 %fusion.5 = f32[1024,2816]{1,0:T(8,128)} fusion(bf16[1024,6272]{1,0:T(8,128)(2,1)} %bitcast.170, f32[1024,1024]{1,0:T(8,128)S(1)} %get-tuple-element.554, f32[1024]{0:T(1024)S(1)} %bitcast.202, f32[1024]{0:T(1024)S(1)} %add_rsqrt_fusion.1), kind=kOutput, calls=%fused_computation.28 | convolution fusion | flops 5908725760 | bytes 21504000 | tf_op jit(solution)/shard_map/dot_general | solution.py:527
  430.1 9.9 multiply_convert_fusion.1
  441.6 9.1 fusion.3
  450.7 29.7 %all-reduce.17.cloned.1.call-done = f32[1024,1024]{1,0:T(8,128)} async-done(((f32[1024,1024]{1,0:T(8,128)}), f32[1024,1024]{1,0:T(8,128)}) %all-reduce.17.cloned.1.call-update) | async-done | bytes 4194320 | tf_op jit(solution)/shard_map/psum | solution.py:541
  512.7 5.7 fusion.84
  520.9 55.5 %while.60 = (s32[]{:T(128)}, f32[2,128,256]{2,1,0:T(8,128)}, f32[16,2,128,256]{3,2,1,0:T(8,128)}, f32[16,2,128,256]{3,2,1,0:T(8,128)}, f32[16,2,128]{2,1,0:T(2,128)S(1)}, /*index=5*/s32[]{:T(128)}, s32[]{:T(128)}, s32[]{:T(128)}) while((s32[]{:T(128)}, f32[2,128,256]{2,1,0:T(8,128)}, f32[16,2,128,256]{3,2,1,0:T(8,128)}, ...), condition=%wide.region_20.22_spmd.clone, body=%wide.region_19.21_spmd.clone.sunk | while | flops 262148 | bytes 1313912 | solution.py:563
  578.4 7.8 convolution_convert_fusion.1
  586.3 6.7 fusion.47
  593.0 9.0 convolution_convert_fusion
  604.3 5.1 fusion.59
  619.8 31.4 %all-gather.7.cloned.1.call-done = f32[32,128,256]{2,1,0:T(8,128)} async-done(((f32[2,128,256]{2,1,0:T(8,128)}), f32[32,128,256]{2,1,0:T(8,128)}) %all-gather.7.cloned.1.call-update) | async-done | bytes 4194320 | tf_op jit(solution)/shard_map/all_gather | solution.py:318
  655.9 37.7 %while.61 = (s32[]{:T(128)}, f32[2,128,256]{2,1,0:T(8,128)}, s32[]{:T(128)}, f32[16,2,128]{2,1,0:T(2,128)}, f32[16,2,128,256]{3,2,1,0:T(8,128)}, /*index=5*/s32[]{:T(128)}, s32[]{:T(128)}) while((s32[]{:T(128)}, f32[2,128,256]{2,1,0:T(8,128)}, s32[]{:T(128)}, f32[16,2,128]{2,1,0:T(2,128)}, f32[16,2,128,256]{3,2,1,0:T(8,128)}, ...), condition=%wide.region_22.24_spmd.clone, body=%wide.region_21.23_spmd.clone.sunk | while | flops 262148 | bytes 789609 | solution.py:330
  693.6 7.3 fusion.74
  717.7 5.0 multiply_reduce_fusion
  726.5 6.4 pad_add_fusion
  743.0 6.8 add_convert_fusion
  752.1 7.0 convolution_convert_fusion.2
  759.1 140.0 %shard_map.458 = bf16[4,16,64,128]{3,2,1,0:T(8,128)(2,1)} custom-call(s32[1,64]{1,0:T(1,128)} %select_bitcast_fusion.inv_ref, bf16[4,2,2,64,1536]{4,3,2,1,0:T(8,128)(2,1)} %bitcast.189, bf16[4,2,2,64,2816]{4,3,2,1,0:T(8,128)(2,1)} %bitcast.183, bf16[4,2,2,64,512]{4,3,2,1,0:T(8,128)(2,1)} %bitcast.192, bf16[4,2,2,64,1408]{4,3,2,1,0:T(8,128)(2,1)} %bitcast.190), custom_call_target="tpu_custom_call" | custom-call | tf_op jit(solution)/shard_map/pallas_call | solution.py:202
  901.7 17.9 %fusion.154 = f32[4,128,1024]{1,2,0:T(8,128)S(1)} fusion(bf16[4,1024,128]{2,1,0:T(8,128)(2,1)} %bitcast.178, f32[4,1024,1024]{2,1,0:T(8,128)} %param.45), kind=kOutput, calls=%fused_computation.266 | convolution fusion | flops 6442450944 | bytes 19922944 | tf_op jit(solution)/shard_map/sij,sik->sjk/dot_general | solution.py:684
  919.6 5.4 fusion.34
  925.1 16.3 %fusion.35 = f32[4,128,1024]{1,2,0:T(8,128)S(1)} fusion(f32[4,1024,1024]{2,1,0:T(8,128)S(1)} %bitcast.161, f32[4,1024,128]{2,1,0:T(8,128)} %get-tuple-element.571, f32[4,1024,128]{2,1,0:T(8,128)} %get-tuple-element.570), kind=kOutput, calls=%fused_computation.91 | convolution fusion | flops 6443499520 | bytes 23068672 | tf_op jit(solution)/shard_map/sij,sjk->sik/dot_general | solution.py:689
  949.6 26.8 %shard_map.459 = f32[40,1024]{1,0:T(8,128)S(1)} custom-call(f32[40,1024]{1,0:T(8,128)S(1)} %select_maximum_fusion.x_ref), custom_call_target="tpu_custom_call" | custom-call | tf_op jit(solution)/shard_map/pallas_call | solution.py:294
  976.5 5.1 fusion.14
  (543 shorter events, 349.7 us)
Async XLA Ops:
  7.2 912.4 %copy-start = (f32[4,128,128]{2,1,0:T(8,128)S(1)}, f32[4,128,128]{2,1,0:T(8,128)}, u32[]{:S(2)}) copy-start(f32[4,128,128]{2,1,0:T(8,128)} %param.46) | copy-start | bytes 786436
  7.2 325.1 %all-gather.5.cloned.1.call-start = ((), (), s32[]{:S(2)}) async-start(), calls=%async_computation.2 | async-start | bytes 4456448 | tf_op jit(solution)/shard_map/all_gather | solution.py:318
  8.6 158.6 %copy-start.64 = (f32[1,1024]{1,0:T(1,128)}, f32[1,1024]{1,0:T(1,128)S(1)}, u32[]{:S(2)}) copy-start(f32[1,1024]{1,0:T(1,128)S(1)} %get-tuple-element.577) | copy-start | bytes 12292
  12.6 154.6 %copy-start.62 = (f32[1024]{0:T(1024)}, f32[1024]{0:T(1024)S(1)}, u32[]{:S(2)}) copy-start(f32[1024]{0:T(1024)S(1)} %add_rsqrt_fusion.2) | copy-start | bytes 12292
  12.6 140.2 %copy-start.18 = (bf16[1024,1024]{1,0:T(8,128)(2,1)S(1)}, bf16[1024,1024]{1,0:T(8,128)(2,1)}, u32[]{:S(2)}) copy-start(bf16[1024,1024]{1,0:T(8,128)(2,1)} %param.36) | copy-start | bytes 6291460
  152.8 11.7 %copy-start.98 = (s32[8]{0:T(128)S(1)}, s32[8]{0:T(128)}, u32[]{:S(2)}) copy-start(s32[8]{0:T(128)} %param.39) | copy-start | bytes 100
  152.8 11.7 %copy-start.4 = (s32[8]{0:T(128)S(1)}, s32[8]{0:T(128)}, u32[]{:S(2)}) copy-start(s32[8]{0:T(128)} %param.38) | copy-start | bytes 100
  152.8 13.2 %copy-start.58 = (f32[4,1024]{1,0:T(4,128)S(1)}, f32[4,1024]{1,0:T(4,128)}, u32[]{:S(2)}) copy-start(f32[4,1024]{1,0:T(4,128)} %param.59) | copy-start | bytes 49156
  152.8 14.4 %copy-start.53 = (f32[1024,16]{0,1:T(8,128)S(1)}, f32[1024,16]{0,1:T(8,128)}, u32[]{:S(2)}) copy-start(f32[1024,16]{0,1:T(8,128)} %param.50) | copy-start | bytes 196612
  162.7 12.6 %collective-permute-start = (bf16[3,1024]{1,0:T(4,128)(2,1)}, bf16[3,1024]{1,0:T(4,128)(2,1)S(1)}, u32[]{:S(2)}, u32[]{:S(2)}) collective-permute-start(bf16[3,1024]{1,0:T(4,128)(2,1)} %slice.213), channel_id=1, source_target_pairs={{0,2},{2,4},{4,6},{6,8},{8,10},{10,12},{12,14},{14,16},{16,18},{18... | collective-permute-start | bytes 18440 | tf_op jit(solution)/shard_map/ppermute | solution.py:313
  166.0 9.9 copy-start.67
  166.0 9.9 copy-start.69
  166.0 9.9 copy-start.71
  166.0 9.9 copy-start.73
  197.1 55.4 %copy-start.87 = (f32[256]{0:T(256)S(1)}, f32[256]{0:T(256)}, u32[]{:S(2)}) copy-start(f32[256]{0:T(256)} %param.56) | copy-start | bytes 3076
  252.4 159.6 %all-reduce.15.cloned.1.call-start = ((), (), s32[]{:S(2)}) async-start(), calls=%async_computation | async-start | bytes 8388608 | tf_op jit(solution)/shard_map/psum | solution.py:523
  382.2 98.2 %all-reduce.17.cloned.1.call-start = ((), (), s32[]{:S(2)}) async-start(), calls=%async_computation.1 | async-start | bytes 8388608 | tf_op jit(solution)/shard_map/psum | solution.py:541
  383.0 102.1 %copy-start.84 = (f32[1024]{0:T(1024)}, f32[1024]{0:T(1024)S(1)}, u32[]{:S(2)}) copy-start(f32[1024]{0:T(1024)S(1)} %fusion.123) | copy-start | bytes 12292
  383.0 34.6 %copy-start.66 = (f32[1,1024]{1,0:T(1,128)S(1)}, f32[1,1024]{1,0:T(1,128)}, u32[]{:S(2)}) copy-start(f32[1,1024]{1,0:T(1,128)} %get-tuple-element.576) | copy-start | bytes 12292
  412.0 18.1 %slice-start.8 = ((s8[12845056]{0:T(1024)(128)(4,1)}), s8[4194304]{0:T(1024)(128)(4,1)S(1)}, s32[]{:S(2)}) async-start(s8[12845056]{0:T(1024)(128)(4,1)} %bitcast.174), calls=%async_computation.13 | async-start | bytes 8388608
  417.6 12.5 %slice-start.9 = ((s8[12845056]{0:T(1024)(128)(4,1)}), s8[4194304]{0:T(1024)(128)(4,1)S(1)}, s32[]{:S(2)}) async-start(s8[12845056]{0:T(1024)(128)(4,1)} %bitcast.174), calls=%async_computation.14 | async-start | bytes 8388608
  417.6 12.5 %slice-start.10 = ((s8[12845056]{0:T(1024)(128)(4,1)}), s8[4194304]{0:T(1024)(128)(4,1)S(1)}, s32[]{:S(2)}) async-start(s8[12845056]{0:T(1024)(128)(4,1)} %bitcast.174), calls=%async_computation.15 | async-start | bytes 8388608
  417.6 12.5 %slice-start.11 = ((s8[12845056]{0:T(1024)(128)(4,1)}), s8[262144]{0:T(1024)(128)(4,1)S(1)}, s32[]{:S(2)}) async-start(s8[12845056]{0:T(1024)(128)(4,1)} %bitcast.174), calls=%async_computation.16 | async-start | bytes 524288
  417.6 12.5 %copy-start.46 = (bf16[1024,1024]{1,0:T(8,128)(2,1)S(1)}, bf16[1024,1024]{1,0:T(8,128)(2,1)}, u32[]{:S(2)}) copy-start(bf16[1024,1024]{1,0:T(8,128)(2,1)} %param.37) | copy-start | bytes 6291460
  450.7 200.6 %all-gather.7.cloned.1.call-start = ((), (), s32[]{:S(2)}) async-start(), calls=%async_computation.3 | async-start | bytes 4456448 | tf_op jit(solution)/shard_map/all_gather | solution.py:318
  520.9 56.8 %copy-start.3 = (s32[1,49]{1,0:T(1,128)S(1)}, s32[1,49]{1,0:T(1,128)}, u32[]{:S(2)}) copy-start(s32[1,49]{1,0:T(1,128)} %owners_ref.1) | copy-start | bytes 592
  576.4 369.7 %all-reduce.19.cloned.1.call-start = ((), (), s32[]{:S(2)}) async-start(), calls=%async_computation.4 | async-start | bytes 8388608 | tf_op jit(solution)/shard_map/psum | solution.py:533
  734.8 6.2 collective-permute-start.1
  901.7 23.3 %slice-start.2 = ((s8[16777216]{0:T(1024)(128)(4,1)}), s8[4194304]{0:T(1024)(128)(4,1)S(1)}, s32[]{:S(2)}) async-start(s8[16777216]{0:T(1024)(128)(4,1)} %bitcast.160), calls=%async_computation.7 | async-start | bytes 8388608
  901.7 23.3 %slice-start.3 = ((s8[16777216]{0:T(1024)(128)(4,1)}), s8[4194304]{0:T(1024)(128)(4,1)S(1)}, s32[]{:S(2)}) async-start(s8[16777216]{0:T(1024)(128)(4,1)} %bitcast.160), calls=%async_computation.8 | async-start | bytes 8388608
  901.7 23.3 %slice-start.4 = ((s8[16777216]{0:T(1024)(128)(4,1)}), s8[4194304]{0:T(1024)(128)(4,1)S(1)}, s32[]{:S(2)}) async-start(s8[16777216]{0:T(1024)(128)(4,1)} %bitcast.160), calls=%async_computation.9 | async-start | bytes 8388608
  976.4 11.2 %copy-start.94 = (f32[1,256]{1,0:T(1,128)}, f32[1,256]{1,0:T(1,128)S(1)}, u32[]{:S(2)}) copy-start(f32[1,256]{1,0:T(1,128)S(1)} %slice.203) | copy-start | bytes 3076
  (91 other events, 393.2 us)
Sparse Core Ops, SparseCore 0:
  252.5 79.6 all-gather.4
  382.3 29.6 all-reduce.14
  450.8 29.5 all-reduce.16
  576.5 74.6 all-gather.6
  750.0 31.0 all-reduce.18

commit v2 on v1

--- a/solution.py
+++ b/solution.py
@@ -11,7 +11,6 @@
 
 DK = 128
 DV = 256
-CH = 64
 
 
 highest_precision = lax.Precision.HIGHEST
@@ -313,21 +312,622 @@
     return lax.ppermute(array, axis, pairs)
 
 
-def carried_in(value, axis, join, neutral, backward):
-    count, mine = (lax.axis_size(axis), lax.axis_index(axis))
-    pieces = jax.tree.map(lambda part: lax.all_gather(part, axis), value)
-    if backward:
-        pieces = jax.tree.map(lambda part: part[::-1], pieces)
-        mine = count - 1 - mine
-    running = jax.tree.map(
-        lambda part, zero: jnp.full_like(part, 0) + jnp.asarray(zero, part.dtype), value, neutral
-    )
-
-    def step(position, running):
-        longer = join(running, jax.tree.map(lambda part: part[position], pieces))
-        return jax.tree.map(lambda new, old: jnp.where(position < mine, new, old), longer, running)
-
-    return lax.fori_loop(0, count - 1, step, running)
+NN = (((1,), (0,)), ((), ()))
+NT = (((1,), (1,)), ((), ()))
+TN = (((0,), (0,)), ((), ()))
+TILE = 128
+
+
+def halves(values):
+    high = values.astype(jnp.bfloat16)
+    return high, (values - high.astype(jnp.float32)).astype(jnp.bfloat16)
+
+
+def product(left, right, dims):
+    (lh, ll), (rh, rl) = left, right
+    dot = functools.partial(
+        lax.dot_general, dimension_numbers=dims, preferred_element_type=jnp.float32
+    )
+    return dot(lh, rh) + (dot(lh, rl) + dot(ll, rh))
+
+
+def running_sum(table, values):
+    first = values.astype(jnp.bfloat16)
+    rest = values - first.astype(jnp.float32)
+    second, third = halves(rest)
+    dot = functools.partial(
+        lax.dot_general, dimension_numbers=NN, preferred_element_type=jnp.float32
+    )
+    return dot(table, first) + (dot(table, second) + dot(table, third))
+
+
+def sigmoid(values):
+    return 1.0 / (1.0 + jnp.exp(-values))
+
+
+def chain_tools(n, sizes, forward, mine, bufs, send, recv, result):
+    me = lax.axis_index("seq")
+    c = coords(me, sizes)
+    pieces = mine.shape[0]
+    across, along, before, held = bufs
+    most = max(sizes)
+    state = pl.ds(0, TILE)
+    decay = pl.ds(TILE, 1)
+
+    def peers(ax):
+        return [j for j in range(1, sizes[ax])]
+
+    def to(ax, j):
+        d = list(c)
+        d[ax] = lax.rem(c[ax] + j, sizes[ax])
+        return index_of(d, sizes)
+
+    def line(buf, source, ax, j, p, base):
+        s = base + j * pieces + p
+        return remote(source.at[p], buf.at[c[ax], p], send.at[s], recv.at[s], to(ax, j))
+
+    def hop(p):
+        s = 2 * most * pieces + p
+        step = 1 if forward else -1
+        d = [lax.rem(c[0] + step + sizes[0], sizes[0]), c[1], c[2]]
+        return remote(held.at[1, p], held.at[0, p], send.at[s], recv.at[s], index_of(d, sizes))
+
+    def compose(first, second):
+        return (second[1] * first[0] + second[0], first[1] * second[1])
+
+    def reduce_line(buf, ax, p):
+        size = sizes[ax]
+        order = range(size) if forward else range(size - 1, -1, -1)
+        prefix = (jnp.zeros((TILE, TILE), jnp.float32), jnp.ones((1, TILE), jnp.float32))
+        total = None
+        for i in order:
+            item = (buf[i, p, state], buf[i, p, decay])
+            longer = compose(prefix, item)
+            take = (i < c[ax]) if forward else (i > c[ax])
+            prefix = tuple(jnp.where(take, a, b) for a, b in zip(longer, prefix, strict=True))
+            total = item if total is None else compose(total, item)
+        return prefix, total
+
+    def start_x():
+        for p in range(pieces):
+            across[c[2], p] = mine[p]
+            for j in peers(2):
+                line(across, mine, 2, j, p, 0).start()
+
+    def start_y():
+        for p in range(pieces):
+            for j in peers(2):
+                line(across, mine, 2, j, p, 0).wait_recv()
+            prefix, total = reduce_line(across, 2, p)
+            before[p, state], before[p, decay] = prefix
+            held[2, p, state], held[2, p, decay] = total
+            held[2, p, pl.ds(TILE + 1, 7)] = jnp.zeros((7, TILE), jnp.float32)
+            along[c[1], p] = held[2, p]
+            for j in peers(1):
+                line(along, held.at[2], 1, j, p, most * pieces).start()
+
+    first_z = 0 if forward else sizes[0] - 1
+    last_z = sizes[0] - 1 - first_z
+
+    def start_z():
+        for p in range(pieces):
+            for j in peers(1):
+                line(along, held.at[2], 1, j, p, most * pieces).wait_recv()
+            prefix, total = reduce_line(along, 1, p)
+            own = (before[p, state], before[p, decay])
+            before[p, state], before[p, decay] = compose(prefix, own)
+            held[1, p, state], held[1, p, decay] = total
+            held[1, p, pl.ds(TILE + 1, 7)] = jnp.zeros((7, TILE), jnp.float32)
+
+            @pl.when(c[0] == first_z)
+            def _():
+                held[0, p] = jnp.zeros((TILE + 8, TILE), jnp.float32)
+                hop(p).start()
+
+    def pass_z(k):
+        at = k if forward else sizes[0] - 1 - k
+
+        @pl.when(c[0] == at)
+        def _():
+            for p in range(pieces):
+                hop(p).wait_recv()
+                if at != last_z:
+                    got = (held[0, p, state], held[0, p, decay])
+                    item = (held[1, p, state], held[1, p, decay])
+                    held[1, p, state], held[1, p, decay] = compose(got, item)
+                    hop(p).start()
+
+    def finish():
+        for p in range(pieces):
+            result[p] = before[p, decay] * held[0, p, state] + before[p, state]
+            for j in peers(2):
+                line(across, mine, 2, j, p, 0).wait_send()
+            for j in peers(1):
+                line(along, held.at[2], 1, j, p, most * pieces).wait_send()
+
+        @pl.when(c[0] != last_z)
+        def _():
+            for p in range(pieces):
+                hop(p).wait_send()
+
+    stages = [start_x, start_y, start_z]
+    stages += [functools.partial(pass_z, k) for k in range(1, sizes[0])]
+    return stages, finish
+
+
+def greet(n, sizes, extra):
+    c = coords(lax.axis_index("seq"), sizes)
+    barrier = pltpu.get_barrier_semaphore()
+    count = 0
+    for ax in range(3):
+        for j in range(1, sizes[ax]):
+            d = list(c)
+            d[ax] = lax.rem(c[ax] + j, sizes[ax])
+            pl.semaphore_signal(
+                barrier, inc=1, device_id={"seq": index_of(d, sizes)}, device_id_type=MESH
+            )
+            count += 1
+    for index in extra:
+        pl.semaphore_signal(barrier, inc=1, device_id={"seq": index}, device_id_type=MESH)
+        count += 1
+    pl.semaphore_wait(barrier, count)
+
+
+def tile_masks(rows_ref, cols_ref, c):
+    row = rows_ref[pl.ds(c, 1), :]
+    col = cols_ref[pl.ds(pl.multiple_of(c * TILE, TILE), TILE), 6:7]
+    i = lax.broadcasted_iota(jnp.int32, (TILE, TILE), 0)
+    j = lax.broadcasted_iota(jnp.int32, (TILE, TILE), 1)
+    return (i >= j) & (row == col)
+
+
+def forward_kernel(
+    n,
+    sizes,
+    proj_ref,
+    halo_ref,
+    lg_ref,
+    gate_ref,
+    cols_ref,
+    rows_ref,
+    taps_ref,
+    gain_ref,
+    conv_ref,
+    cum_ref,
+    o_ref,
+    u_ref,
+    start_ref,
+    act,
+    state,
+    prev,
+    mine,
+    across,
+    along,
+    before,
+    held,
+    result,
+    send,
+    recv,
+):
+    tiles, channels = proj_ref.shape[0] // TILE, proj_ref.shape[1]
+    keys = lg_ref.shape[1]
+    heads = keys // DK
+    value = DV * heads
+    greet(n, sizes, ())
+    scale = DK ** (-0.5)
+    i = lax.broadcasted_iota(jnp.int32, (TILE, TILE), 0)
+    j = lax.broadcasted_iota(jnp.int32, (TILE, TILE), 1)
+    lower = (i >= j).astype(jnp.bfloat16)
+    prev[...] = halo_ref[...]
+    state[...] = jnp.zeros_like(state)
+    mine[...] = jnp.zeros_like(mine)
+    for p in range(mine.shape[0]):
+        mine[p, TILE : TILE + 1] = jnp.ones((1, TILE), jnp.float32)
+
+    def local(c, _):
+        at = pl.ds(pl.multiple_of(c * TILE, TILE), TILE)
+        for g in range(0, channels, 256):
+            wide = slice(g, g + 256)
+            block = jnp.concatenate(
+                [prev[:, wide].astype(jnp.float32), proj_ref[at, wide].astype(jnp.float32)]
+            )
+            total = taps_ref[3:4, wide] * block[16:]
+            for s in (1, 2, 3):
+                total = total + taps_ref[3 - s : 4 - s, wide] * (
+                    block[16 - s : 16 - s + TILE] * cols_ref[at, 1 + s : 2 + s]
+                )
+            conv_ref[at, wide] = total
+            act[at, wide] = total * sigmoid(total)
+        prev[...] = proj_ref[pl.ds(pl.multiple_of(c * TILE + TILE - 16, 16), 16), :]
+        cum = running_sum(lower, lg_ref[at, :])
+        cum_ref[at, :] = cum
+        last = cum[TILE - 1 : TILE]
+        left = act[at, keys : 2 * keys] * jnp.exp(last - cum) * cols_ref[at, 1:2]
+        decay = jnp.exp(last) * cols_ref[at, 0:1][TILE - 1 : TILE]
+        for h in range(heads):
+            kh = slice(h * DK, (h + 1) * DK)
+            v = halves(act[at, 2 * keys + h * DV : 2 * keys + (h + 1) * DV])
+            start_ref[c, h] = state[h]
+            state[h] = state[h] * decay[:, kh] + product(v, halves(left[:, kh]), TN)
+            for e in range(DV // TILE):
+                p = h * (DV // TILE) + e
+                mine[p, TILE : TILE + 1] = mine[p, TILE : TILE + 1] * decay[:, kh]
+        return 0
+
+    lax.fori_loop(0, tiles, local, 0)
+    for h in range(heads):
+        start_ref[tiles, h] = state[h]
+        for e in range(DV // TILE):
+            mine[h * (DV // TILE) + e, 0:TILE] = state[h, e * TILE : (e + 1) * TILE]
+    stages, finish = chain_tools(
+        n, sizes, True, mine, (across, along, before, held), send, recv, result
+    )
+    stages[0]()
+
+    def inside(c, _):
+        for k, stage in enumerate(stages[1:]):
+            pl.when(c == k + 1)(stage)
+        at = pl.ds(pl.multiple_of(c * TILE, TILE), TILE)
+        cum = cum_ref[at, :]
+        middle = cum[TILE // 2 - 1 : TILE // 2]
+        q = act[at, 0:keys] * jnp.exp(cum - middle) * scale
+        k = act[at, keys : 2 * keys] * jnp.exp(middle - cum)
+        mask = tile_masks(rows_ref, cols_ref, c)
+        for h in range(heads):
+            kh = slice(h * DK, (h + 1) * DK)
+            vh = slice(h * DV, (h + 1) * DV)
+            scores = jnp.where(mask, product(halves(q[:, kh]), halves(k[:, kh]), NT), 0.0)
+            v = halves(act[at, 2 * keys + h * DV : 2 * keys + (h + 1) * DV])
+            o_ref[at, vh] = product(halves(scores), v, NN)
+        return 0
+
+    lax.fori_loop(0, tiles, inside, 0)
+    finish()
+    for h in range(heads):
+        for e in range(DV // TILE):
+            state[h, e * TILE : (e + 1) * TILE] = result[h * (DV // TILE) + e]
+
+    def outside(c, _):
+        at = pl.ds(pl.multiple_of(c * TILE, TILE), TILE)
+        cum = cum_ref[at, :]
+        q = act[at, 0:keys] * jnp.exp(cum) * scale * cols_ref[at, 0:1]
+        decay = jnp.exp(cum[TILE - 1 : TILE]) * cols_ref[at, 0:1][TILE - 1 : TILE]
+        for h in range(heads):
+            kh = slice(h * DK, (h + 1) * DK)
+            vh = slice(h * DV, (h + 1) * DV)
+            start = start_ref[c, h] + state[h]
+            start_ref[c, h] = start
+            state[h] = state[h] * decay[:, kh]
+            o = o_ref[at, vh] + product(halves(q[:, kh]), halves(start), NT)
+            o_ref[at, vh] = o
+            inverse = lax.rsqrt(jnp.mean(o * o, axis=1, keepdims=True) + norm_epsilon)
+            gate = gate_ref[at, vh]
+            u_ref[at, vh] = (o * inverse * gain_ref[...] * (gate * sigmoid(gate))).astype(
+                u_ref.dtype
+            )
+        return 0
+
+    lax.fori_loop(0, tiles, outside, 0)
+    for h in range(heads):
+        start_ref[tiles, h] = start_ref[tiles, h] + state[h]
+
+
+def chain_scratch(sizes, pieces):
+    most = max(sizes)
+    shape = (pieces, TILE + 8, TILE)
+    return [
+        pltpu.VMEM(shape, jnp.float32),
+        pltpu.VMEM((sizes[2],) + shape, jnp.float32),
+        pltpu.VMEM((sizes[1],) + shape, jnp.float32),
+        pltpu.VMEM(shape, jnp.float32),
+        pltpu.VMEM((3,) + shape, jnp.float32),
+        pltpu.VMEM((pieces, TILE, TILE), jnp.float32),
+        pltpu.SemaphoreType.DMA(((2 * most + 1) * pieces,)),
+        pltpu.SemaphoreType.DMA(((2 * most + 1) * pieces,)),
+    ]
+
+
+def recurrence(proj, halo, log_gate, gate, cols, rows, taps, gain):
+    n = lax.axis_size("seq")
+    sizes = axis_sizes(n)
+    length, channels = proj.shape
+    keys = log_gate.shape[1]
+    heads = keys // DK
+    value = heads * DV
+    tiles = length // TILE
+    f32 = jnp.float32
+    shape = jax.ShapeDtypeStruct
+    return pl.pallas_call(
+        functools.partial(forward_kernel, n, sizes),
+        out_shape=(
+            shape((length, channels), f32),
+            shape((length, keys), f32),
+            shape((length, value), f32),
+            shape((length, value), jnp.bfloat16),
+            shape((tiles + 1, heads, DV, DK), f32),
+        ),
+        scratch_shapes=[
+            pltpu.VMEM((length, channels), f32),
+            pltpu.VMEM((heads, DV, DK), f32),
+            pltpu.VMEM((16, channels), proj.dtype),
+        ]
+        + chain_scratch(sizes, heads * DV // TILE),
+        compiler_params=pltpu.CompilerParams(
+            collective_id=4, has_side_effects=True, vmem_limit_bytes=56 << 20
+        ),
+    )(proj, halo, log_gate, gate, cols, rows, taps, gain)
+
+
+def backward_kernel(
+    n,
+    sizes,
+    proj_ref,
+    halo_ref,
+    conv_ref,
+    cum_ref,
+    logits_ref,
+    o_ref,
+    gate_ref,
+    du_ref,
+    start_ref,
+    cols_ref,
+    rows_ref,
+    taps_ref,
+    gain_ref,
+    dproj_ref,
+    dgate_ref,
+    dlogits_ref,
+    dtaps_ref,
+    dgain_ref,
+    do,
+    dact,
+    adjoint,
+    ends,
+    after,
+    back,
+    tail,
+    mine,
+    across,
+    along,
+    before,
+    held,
+    result,
+    send,
+    recv,
+    b_sem,
+):
+    tiles, channels = proj_ref.shape[0] // TILE, proj_ref.shape[1]
+    keys = cum_ref.shape[1]
+    heads = keys // DK
+    me = lax.axis_index("seq")
+    greet(n, sizes, (lax.rem(me + 1, n), lax.rem(me + n - 1, n)))
+    scale = DK ** (-0.5)
+    i = lax.broadcasted_iota(jnp.int32, (TILE, TILE), 0)
+    j = lax.broadcasted_iota(jnp.int32, (TILE, TILE), 1)
+    upper = (i <= j).astype(jnp.bfloat16)
+    adjoint[...] = jnp.zeros_like(adjoint)
+    mine[...] = jnp.zeros_like(mine)
+    dgain_ref[...] = jnp.zeros_like(dgain_ref)
+    dtaps_ref[...] = jnp.zeros_like(dtaps_ref)
+    for p in range(mine.shape[0]):
+        mine[p, TILE : TILE + 1] = jnp.ones((1, TILE), jnp.float32)
+
+    def local(t, _):
+        c = tiles - 1 - t
+        at = pl.ds(pl.multiple_of(c * TILE, TILE), TILE)
+        cum = cum_ref[at, :]
+        pre = conv_ref[at, 0:keys]
+        q = pre * sigmoid(pre) * jnp.exp(cum) * scale * cols_ref[at, 0:1]
+        decay = jnp.exp(cum[TILE - 1 : TILE]) * cols_ref[at, 0:1][TILE - 1 : TILE]
+        for h in range(heads):
+            kh = slice(h * DK, (h + 1) * DK)
+            vh = slice(h * DV, (h + 1) * DV)
+            o = o_ref[at, vh]
+            inverse = lax.rsqrt(jnp.mean(o * o, axis=1, keepdims=True) + norm_epsilon)
+            gate = gate_ref[at, vh]
+            sig = sigmoid(gate)
+            du = du_ref[at, vh]
+            unit = o * inverse
+            dgate_ref[at, vh] = (
+                du * (unit * gain_ref[...]) * (sig * (1.0 + gate * (1.0 - sig)))
+            ).astype(dgate_ref.dtype)
+            don = du * (gate * sig)
+            dgain_ref[0:1] += jnp.sum(don * unit, axis=0, keepdims=True)
+            scaled = gain_ref[...] * don
+            grad = inverse * scaled - unit * (
+                inverse * inverse * jnp.mean(scaled * o, axis=1, keepdims=True)
+            )
+            do[at, vh] = grad
+            ends[c, h] = adjoint[h]
+            adjoint[h] = adjoint[h] * decay[:, kh] + product(halves(grad), halves(q[:, kh]), TN)
+            for e in range(DV // TILE):
+                p = h * (DV // TILE) + e
+                mine[p, TILE : TILE + 1] = mine[p, TILE : TILE + 1] * decay[:, kh]
+        return 0
+
+    lax.fori_loop(0, tiles, local, 0)
+    for h in range(heads):
+        for e in range(DV // TILE):
+            mine[h * (DV // TILE) + e, 0:TILE] = adjoint[h, e * TILE : (e + 1) * TILE]
+    stages, finish = chain_tools(
+        n, sizes, False, mine, (across, along, before, held), send, recv, result
+    )
+    stages[0]()
+
+    def inside(c, _):
+        for k, stage in enumerate(stages[1:]):
+            pl.when(c == k + 1)(stage)
+        at = pl.ds(pl.multiple_of(c * TILE, TILE), TILE)
+        cum = cum_ref[at, :]
+        middle = cum[TILE // 2 - 1 : TILE // 2]
+        pre = conv_ref[at, 0 : 2 * keys]
+        both = pre * sigmoid(pre)
+        grow = jnp.exp(cum - middle) * scale
+        fall = jnp.exp(middle - cum)
+        enter_decay = jnp.exp(cum) * (scale * cols_ref[at, 0:1])
+        mask = tile_masks(rows_ref, cols_ref, c)
+        for h in range(heads):
+            kh = slice(h * DK, (h + 1) * DK)
+            vh = slice(h * DV, (h + 1) * DV)
+            q = halves(both[:, kh] * grow[:, kh])
+            k = halves(both[:, keys + h * DK : keys + (h + 1) * DK] * fall[:, kh])
+            prev_v = conv_ref[at, 2 * keys + h * DV : 2 * keys + (h + 1) * DV]
+            v = halves(prev_v * sigmoid(prev_v))
+            grad = halves(do[at, vh])
+            scores = halves(jnp.where(mask, product(q, k, NT), 0.0))
+            dscores = halves(jnp.where(mask, product(grad, v, NT), 0.0))
+            dact[at, h * DK : (h + 1) * DK] = (
+                product(dscores, k, NN) * grow[:, kh]
+                + product(grad, halves(start_ref[c, h]), NN) * enter_decay[:, kh]
+            )
+            dact[at, keys + h * DK : keys + (h + 1) * DK] = (
+                product(dscores, q, TN) * fall[:, kh]
+            )
+            dact[at, 2 * keys + h * DV : 2 * keys + (h + 1) * DV] = product(scores, grad, TN)
+        return 0
+
+    lax.fori_loop(0, tiles, inside, 0)
+    finish()
+    for h in range(heads):
+        for e in range(DV // TILE):
+            adjoint[h, e * TILE : (e + 1) * TILE] = result[h * (DV // TILE) + e]
+    after[...] = jnp.zeros_like(after)
+
+    def outside(t, _):
+        c = tiles - 1 - t
+        at = pl.ds(pl.multiple_of(c * TILE, TILE), TILE)
+        cum = cum_ref[at, :]
+        last = cum[TILE - 1 : TILE]
+        remain = jnp.exp(last - cum) * cols_ref[at, 1:2]
+        decay = jnp.exp(last) * cols_ref[at, 0:1][TILE - 1 : TILE]
+        pre = conv_ref[at, 0 : 2 * keys]
+        both = pre * sigmoid(pre)
+        dkeys, edges = [], []
+        for h in range(heads):
+            kh = slice(h * DK, (h + 1) * DK)
+            wide = slice(2 * keys + h * DV, 2 * keys + (h + 1) * DV)
+            k = both[:, keys + h * DK : keys + (h + 1) * DK]
+            end = ends[c, h] + adjoint[h]
+            adjoint[h] = adjoint[h] * decay[:, kh]
+            parts = halves(end)
+            pre_v = conv_ref[at, wide]
+            v = halves(pre_v * sigmoid(pre_v))
+            dkeys.append(
+                dact[at, keys + h * DK : keys + (h + 1) * DK]
+                + product(v, parts, NN) * remain[:, kh]
+            )
+            dact[at, wide] += product(halves(k * remain[:, kh]), parts, NT)
+            edges.append(jnp.sum(end * start_ref[c + 1, h], axis=0, keepdims=True))
+        dk = jnp.concatenate(dkeys, axis=1)
+        dq = dact[at, 0:keys]
+        dact[at, keys : 2 * keys] = dk
+        drift = both[:, 0:keys] * dq - both[:, keys:] * dk
+        dl = running_sum(upper, drift) + jnp.concatenate(edges, axis=1)
+        dlogits_ref[at, :] = dl * (1.0 / gate_scale) * sigmoid(-logits_ref[at, :])
+        behind = jnp.where(
+            c == 0,
+            halo_ref[...],
+            proj_ref[pl.ds(pl.multiple_of(jnp.maximum(c * TILE - 16, 0), 16), 16), :],
+        )
+        masks = cols_ref[pl.ds(pl.multiple_of(c * TILE, TILE), TILE + 8), :]
+        for g in range(0, channels, 256):
+            wide = slice(g, g + 256)
+            pre = conv_ref[at, wide]
+            sig = sigmoid(pre)
+            dconv = dact[at, wide] * (sig * (1.0 + pre * (1.0 - sig)))
+            block = jnp.concatenate(
+                [
+                    behind[:, g : g + 256].astype(jnp.float32),
+                    proj_ref[at, wide].astype(jnp.float32),
+                ]
+            )
+            grad = jnp.concatenate([dconv, after[:, wide]])
+            total = taps_ref[3:4, wide] * dconv
+            dtaps_ref[3:4, wide] += jnp.sum(dconv * block[16:], axis=0, keepdims=True)
+            first = jnp.zeros((8, 256), jnp.float32)
+            for s in (1, 2, 3):
+                masked = grad * masks[:, 1 + s : 2 + s]
+                tap = taps_ref[3 - s : 4 - s, wide]
+                total = total + tap * masked[s : s + TILE]
+                dtaps_ref[3 - s : 4 - s, wide] += jnp.sum(
+                    masked[:TILE] * block[16 - s : 16 - s + TILE], axis=0, keepdims=True
+                )
+                first = first + tap * jnp.concatenate(
+                    [jnp.zeros((8, 256), jnp.float32), masked[0:8]]
+                )[s : s + 8]
+            dproj_ref[at, wide] = total.astype(dproj_ref.dtype)
+            after[:, wide] = dconv[0:8]
+            back[0, :, wide] = first
+
+            @pl.when(c == tiles - 1)
+            def _():
+                tail[:, wide] = total[TILE - 16 :]
+
+        return 0
+
+    lax.fori_loop(0, tiles, outside, 0)
+
+    home = remote(
+        back.at[0], back.at[1], b_sem.at[0], b_sem.at[1], lax.rem(me + n - 1, n)
+    )
+
+    @pl.when(me > 0)
+    def _():
+        home.start()
+
+    @pl.when(me < n - 1)
+    def _():
+        home.wait_recv()
+
+    @pl.when(me == n - 1)
+    def _():
+        back[1] = jnp.zeros(back.shape[1:], jnp.float32)
+
+    dproj_ref[pl.ds(tiles * TILE - 16, 16), :] = (
+        tail[...] + jnp.concatenate([jnp.zeros((8, channels), jnp.float32), back[1]])
+    ).astype(dproj_ref.dtype)
+
+    @pl.when(me > 0)
+    def _():
+        home.wait_send()
+
+
+def recurrence_back(
+    proj, halo, conv, cum, logits, o, gate, du, starts, cols, rows, taps, gain
+):
+    n = lax.axis_size("seq")
+    sizes = axis_sizes(n)
+    length, channels = proj.shape
+    keys = cum.shape[1]
+    heads = keys // DK
+    value = heads * DV
+    tiles = length // TILE
+    f32 = jnp.float32
+    shape = jax.ShapeDtypeStruct
+    return pl.pallas_call(
+        functools.partial(backward_kernel, n, sizes),
+        out_shape=(
+            shape((length, channels), jnp.bfloat16),
+            shape((length, value), jnp.bfloat16),
+            shape((length, keys), f32),
+            shape((8, channels), f32),
+            shape((8, DV), f32),
+        ),
+        scratch_shapes=[
+            pltpu.VMEM((length, value), f32),
+            pltpu.VMEM((length, channels), f32),
+            pltpu.VMEM((heads, DV, DK), f32),
+            pltpu.VMEM((tiles, heads, DV, DK), f32),
+            pltpu.VMEM((8, channels), f32),
+            pltpu.VMEM((2, 8, channels), f32),
+            pltpu.VMEM((16, channels), f32),
+        ]
+        + chain_scratch(sizes, heads * DV // TILE)
+        + [pltpu.SemaphoreType.DMA((2,))],
+        compiler_params=pltpu.CompilerParams(
+            collective_id=5, has_side_effects=True, vmem_limit_bytes=60 << 20
+        ),
+    )(proj, halo, conv, cum, logits, o, gate, du, starts, cols, rows, taps, gain)
 
 
 def rms_stats(values):
@@ -352,18 +952,6 @@
     filled = jnp.sum(packed)
     counted = jnp.sum((starts[None, :] <= positions[:, None]).astype(jnp.int32), axis=1)
     return (counted + (positions >= filled).astype(jnp.int32), positions < filled)
-
-
-def compose(earlier, later_part):
-    return (earlier[0] * later_part[0], later_part[0][..., None] * earlier[1] + later_part[1])
-
-
-def advance(current_state, piece_pair):
-    return (piece_pair[0][..., None] * current_state + piece_pair[1], current_state)
-
-
-def retreat(adjoint, piece_pair):
-    return (piece_pair[1] + piece_pair[0][..., None] * adjoint, adjoint)
 
 
 def plain_adam(param, gradient, first, second, rate):
@@ -412,9 +1000,6 @@
     key_width = gate_up.shape[1]
     channels = conv_weight.shape[1]
     value_width = channels - 2 * key_width
-    heads_here = key_width // DK
-    tile_len = CH
-    tiles = tok_rows // tile_len
     block_total = owners.shape[1]
     count_in = (channels + value_width) // block_width
     count_out = value_width // block_width
@@ -422,16 +1007,26 @@
     count_up = 2 * count_down
     up_end = count_in + count_up
     out_end = up_end + count_out
-    score_scale = DK ** (-0.5)
     seq_index = lax.axis_index("seq")
     base_pos = seq_index * tok_rows
-    ext_pos = base_pos - (tap_count - 1) + jnp.arange(tok_rows + tap_count - 1, dtype=jnp.int32)
-    ext_seg, ext_valid = segment_of(ext_pos, lengths, packing)
-    own_seg = ext_seg[tap_count - 1 :]
-    own_valid = ext_valid[tap_count - 1 :].astype(jnp.float32)
-    tile_prev = segment_of(
-        base_pos - 1 + tile_len * jnp.arange(tiles, dtype=jnp.int32), lengths, packing
-    )[0]
+    ext_seg, ext_valid = segment_of(
+        base_pos - 8 + jnp.arange(tok_rows + 8, dtype=jnp.int32), lengths, packing
+    )
+    own_seg = ext_seg[8:]
+    own_valid = ext_valid[8:].astype(jnp.float32)
+    tiles = tok_rows // TILE
+    seg_tiles = own_seg.reshape(tiles, TILE)
+    tile_prev = jnp.repeat(ext_seg[7 : 7 + tok_rows : TILE], TILE)
+    tile_last = jnp.repeat(seg_tiles[:, -1], TILE)
+    same = [tile_prev, tile_last] + [ext_seg[8 - s : 8 - s + tok_rows] for s in (1, 2, 3)]
+    cols = jnp.stack(
+        [(other == own_seg).astype(jnp.float32) for other in same]
+        + [jnp.zeros_like(own_valid), own_seg.astype(jnp.float32), own_valid],
+        axis=1,
+    )
+    cols = jnp.pad(cols, ((0, 8), (0, 0)))
+    rows = seg_tiles.astype(jnp.float32)
+    rim_tokens = passed_along(tokens[tok_rows - 16 :], "seq", 1).astype(jnp.float32)
     weights = gather_weights(
         slot_copy,
         owners,
@@ -449,6 +1044,7 @@
     inputs = tokens.astype(jnp.float32)
     inverse_one = rms_stats(inputs)
     normed = (inputs * inverse_one * norm_gains[0]).astype(jnp.bfloat16)
+    rim_normed = (rim_tokens * rms_stats(rim_tokens) * norm_gains[0]).astype(jnp.bfloat16)
     projected = jnp.dot(normed, in_weights, preferred_element_type=jnp.float32)
     mixed_proj = projected[:, :channels].astype(jnp.bfloat16)
     gate_pre = projected[:, channels:]
@@ -458,65 +1054,13 @@
         jnp.dot(lowrank, gate_up[:rank_width], precision=highest_precision) + gate_up[rank_width]
     )
     log_gate = jax.nn.log_sigmoid(logits) / gate_scale
-    rim_rows = passed_along(mixed_proj[tok_rows - (tap_count - 1) :], "seq", 1)
-    extended = jnp.concatenate([rim_rows, mixed_proj], axis=0).astype(jnp.float32)
-    same_seg = []
-    conv_pre = jnp.zeros((tok_rows, channels), jnp.float32)
-    for tap_index in range(tap_count):
-        tap_mask = (ext_seg[tap_index : tap_index + tok_rows] == own_seg).astype(jnp.float32)[
-            :, None
-        ]
-        same_seg.append(tap_mask)
-        conv_pre = (
-            conv_pre
-            + conv_weight[tap_index] * extended[tap_index : tap_index + tok_rows] * tap_mask
-        )
-    active = jax.nn.silu(conv_pre)
-    queries = active[:, :key_width].reshape(tiles, tile_len, heads_here, DK)
-    keys_all = active[:, key_width : 2 * key_width].reshape(tiles, tile_len, heads_here, DK)
-    values_all = active[:, 2 * key_width :].reshape(tiles, tile_len, heads_here, DV)
-    log_gates = log_gate.reshape(tiles, tile_len, heads_here, DK)
-    seg_tiles = own_seg.reshape(tiles, tile_len)
-    incoming_carry = (seg_tiles == tile_prev[:, None]).astype(jnp.float32)
-    causal = jnp.tril(jnp.ones((tile_len, tile_len), jnp.float32))
-    pair_mask = causal[None] * (seg_tiles[:, :, None] == seg_tiles[:, None, :]).astype(jnp.float32)
-    tail_mask = (seg_tiles == seg_tiles[:, -1:]).astype(jnp.float32)
-    cumulative = jnp.cumsum(log_gates, axis=1)
-    final_cumulative_decay = cumulative[:, -1]
-    query_scaled = queries * jnp.exp(cumulative) * score_scale
-    k_scaled = keys_all * jnp.exp(-cumulative)
-    key_remainder = (
-        keys_all
-        * jnp.exp(final_cumulative_decay[:, None] - cumulative)
-        * tail_mask[:, :, None, None]
-    )
-    scores = (
-        jnp.einsum("cthk,cshk->chts", query_scaled, k_scaled, precision=highest_precision)
-        * pair_mask[:, None]
-    )
-    intra_out = jnp.einsum("chts,cshv->cthv", scores, values_all, precision=highest_precision)
-    contrib = jnp.einsum("cshk,cshv->chkv", key_remainder, values_all, precision=highest_precision)
-    tile_decay = jnp.exp(final_cumulative_decay) * incoming_carry[:, -1][:, None, None]
-    zero_state = jnp.zeros((heads_here, DK, DV), jnp.float32)
-    unit_decay = jnp.ones((heads_here, DK), jnp.float32)
-    local_end, local_start = lax.scan(advance, zero_state, (tile_decay, contrib))
-    running = jnp.cumprod(tile_decay, axis=0)
-    before = jnp.concatenate([unit_decay[None], running[:-1]], axis=0)
-    device_decay = running[-1]
-    incoming = carried_in(
-        (device_decay, local_end), "seq", compose, (unit_decay, zero_state), False
-    )[1]
-    start_state = before[..., None] * incoming[None] + local_start
-    cross_piece_output = (
-        jnp.einsum("cthk,chkv->cthv", query_scaled, start_state, precision=highest_precision)
-        * incoming_carry[:, :, None, None]
-    )
-    attended = (cross_piece_output + intra_out).reshape(tok_rows, heads_here, DV)
-    inverse_head = rms_stats(attended)
-    head_normed = attended * inverse_head * head_gain
-    gate_view = gate_pre.reshape(tok_rows, heads_here, DV)
-    swished = jax.nn.silu(gate_view)
-    gated_out = (head_normed * swished).reshape(tok_rows, value_width).astype(jnp.bfloat16)
+    halo = jnp.dot(
+        rim_normed, in_weights[:, :channels], preferred_element_type=jnp.float32
+    ).astype(jnp.bfloat16)
+    gain_row = head_gain[None]
+    conv_pre, cumulative, attended, gated_out, starts = recurrence(
+        mixed_proj, halo, log_gate, gate_pre, cols, rows, conv_weight, gain_row
+    )
     attn_part = jnp.einsum(
         "tn,dn->td", gated_out, out_weights, preferred_element_type=jnp.float32
     )
@@ -544,90 +1088,24 @@
     grad_gains_two = jnp.sum(grad_normed_two * hidden_one * inverse_two, axis=0)
     grad_one = upstream + rms_back(hidden_one, inverse_two, norm_gains[1], grad_normed_two)
     grad_attn = grad_one.astype(jnp.bfloat16)
-    grad_gated = jnp.dot(grad_attn, out_weights, preferred_element_type=jnp.float32).reshape(
-        tok_rows, heads_here, DV
-    )
-    grad_gate_pre = (grad_gated * head_normed * swish_slope(gate_view)).reshape(
-        tok_rows, value_width
-    )
-    grad_head_normed = grad_gated * swished
-    grad_head_gain = jnp.sum(grad_head_normed * attended * inverse_head, axis=(0, 1))
-    grad_attended = rms_back(attended, inverse_head, head_gain, grad_head_normed)
-    grad_out = grad_attended.reshape(tiles, tile_len, heads_here, DV)
-    weighted = jnp.einsum(
-        "cthk,cthv->chkv",
-        query_scaled * incoming_carry[:, :, None, None],
-        grad_out,
-        precision=highest_precision,
-    )
-    local_adjoint, local_end_adj = lax.scan(
-        retreat, zero_state, (tile_decay, weighted), reverse=True
-    )
-    reverse_run = jnp.cumprod(tile_decay[::-1], axis=0)[::-1]
-    after_decay = jnp.concatenate([reverse_run[1:], unit_decay[None]], axis=0)
-    outgoing = carried_in(
-        (device_decay, local_adjoint), "seq", compose, (unit_decay, zero_state), True
-    )[1]
-    end_adjoint = after_decay[..., None] * outgoing[None] + local_end_adj
-    end_state = tile_decay[..., None] * start_state + contrib
-    grad_scores = (
-        jnp.einsum("cthv,cshv->chts", grad_out, values_all, precision=highest_precision)
-        * pair_mask[:, None]
-    )
-    grad_q_scaled = jnp.einsum(
-        "chts,cshk->cthk", grad_scores, k_scaled, precision=highest_precision
-    ) + incoming_carry[:, :, None, None] * jnp.einsum(
-        "cthv,chkv->cthk", grad_out, start_state, precision=highest_precision
-    )
-    grad_queries = grad_q_scaled * jnp.exp(cumulative) * score_scale
-    grad_k_scaled = jnp.einsum(
-        "chts,cthk->cshk", grad_scores, query_scaled, precision=highest_precision
-    )
-    grad_k_tail = jnp.einsum(
-        "cshv,chkv->cshk", values_all, end_adjoint, precision=highest_precision
-    )
-    grad_keys = (
-        grad_k_scaled * jnp.exp(-cumulative)
-        + grad_k_tail
-        * jnp.exp(final_cumulative_decay[:, None] - cumulative)
-        * tail_mask[:, :, None, None]
-    )
-    grad_values = jnp.einsum(
-        "chts,cthv->cshv", scores, grad_out, precision=highest_precision
-    ) + jnp.einsum("cshk,chkv->cshv", key_remainder, end_adjoint, precision=highest_precision)
-    boundary = jnp.sum(end_adjoint * end_state, axis=-1)
-    grad_cumul = queries * grad_queries - keys_all * grad_keys
-    grad_cumul = jnp.concatenate(
-        [grad_cumul[:, :-1], grad_cumul[:, -1:] + boundary[:, None]], axis=1
-    )
-    grad_log_gates = jnp.cumsum(grad_cumul[:, ::-1], axis=1)[:, ::-1]
-    grad_active = jnp.concatenate(
-        [
-            grad_queries.reshape(tok_rows, key_width),
-            grad_keys.reshape(tok_rows, key_width),
-            grad_values.reshape(tok_rows, value_width),
-        ],
-        axis=1,
-    )
-    grad_conv = grad_active * swish_slope(conv_pre)
-    grad_extended = jnp.zeros((tok_rows + tap_count - 1, channels), jnp.float32)
-    tap_grads = []
-    for tap_index in range(tap_count):
-        grad_extended = grad_extended + jnp.pad(
-            conv_weight[tap_index] * same_seg[tap_index] * grad_conv,
-            ((tap_index, tap_count - 1 - tap_index), (0, 0)),
-        )
-        tap_grads.append(
-            jnp.sum(
-                same_seg[tap_index] * extended[tap_index : tap_index + tok_rows] * grad_conv, axis=0
-            )
-        )
-    grad_conv_weight = jnp.stack(tap_grads)
-    returned = passed_along(grad_extended[: tap_count - 1], "seq", -1)
-    grad_mixed = grad_extended[tap_count - 1 :] + jnp.concatenate(
-        [jnp.zeros((tok_rows - (tap_count - 1), channels), jnp.float32), returned], axis=0
-    )
-    grad_logits = grad_log_gates.reshape(tok_rows, key_width) / gate_scale * jax.nn.sigmoid(-logits)
+    grad_gated = jnp.dot(grad_attn, out_weights, preferred_element_type=jnp.float32)
+    grad_mixed, grad_gate_pre, grad_logits, tap_grads, gain_grads = recurrence_back(
+        mixed_proj,
+        halo,
+        conv_pre,
+        cumulative,
+        logits,
+        attended,
+        gate_pre,
+        grad_gated,
+        starts,
+        cols,
+        rows,
+        conv_weight,
+        gain_row,
+    )
+    grad_conv_weight = tap_grads[:tap_count]
+    grad_head_gain = gain_grads[0]
     grad_upper = jnp.concatenate(
         [
             jnp.einsum("tr,tk->rk", lowrank, grad_logits, precision=highest_precision),
@@ -642,7 +1120,7 @@
         "tr,td->rd", grad_lowrank, normed, preferred_element_type=jnp.float32
     )
     grad_projected = jnp.concatenate(
-        [grad_mixed.astype(jnp.bfloat16), grad_gate_pre.astype(jnp.bfloat16)], axis=1
+        [grad_mixed, grad_gate_pre], axis=1
     )
     grad_normed_part = jnp.einsum(
         "tn,dn->td", grad_projected, in_weights, preferred_element_type=jnp.float32

time: 1010 us -> 664 us (0.66)
  other arithmetic: 240 us -> 35.7 us
  Pallas kernels: 307 us -> 404 us
  waiting for transfers between devices: 119 us -> 34.9 us
  local copies, waits for them, and re-layouts: 76.3 us -> 18.2 us
  matrix products: 193 us -> 143 us
  blocking collectives: 37.6 us -> 0 us
    pallas_call x0 -> x2, Pallas kernels: none -> 85.1 us  [the longest x1 45.1 us: recurrence_back(): pl.pallas_call(functools.partial(backward_kernel, n, sizes), out_shape=(s...]
    add x36 -> x1, other arithmetic: 65.2 us -> 0.01 us  [body(): base_pos - 8 + jnp.arange(tok_rows + 8, dtype=jnp.int32)]
    all_gather x2 -> x0, waiting for transfers between devices: 60.6 us -> none  [carried_in(): pieces = jax.tree.map(lambda part: lax.all_gather(part, axis), value)]
    select_n x31 -> x0, other arithmetic: 55.2 us -> none  [the longest x30 55.2 us: step(): jnp.where(position < mine, new, old)]
    dot_general x12 -> x1, matrix products: 55.8 us -> 2.64 us  [body(): jnp.dot(rim_normed, in_weights[:, :channels], preferred_element_type=jnp....]
    dynamic_update_slice x32 -> x0, other arithmetic: 51.9 us -> none  [body(): lax.scan(advance, zero_state, (tile_decay, contrib))]
    all_gather x1 -> x0, blocking collectives: 37.6 us -> none  [carried_in(): pieces = jax.tree.map(lambda part: lax.all_gather(part, axis), value)]
    psum x1, waiting for transfers between devices: 29.7 us -> 4.36 us  [body(): lax.psum(jnp.einsum('tn,dn->td', grad_pair, up_weights, preferred_element...]
  transfers between devices with their start and end apart: 7 -> 4, of which waited for: 4 -> 2; matrix products, arithmetic and copies ran while one was open for 13% -> 16% of each run, Pallas kernels for 14% -> 45%
where the time goes in v2:
time: 664 us; the launch traced here: 652 us
  Pallas kernels  404 us (61%)
  matrix products  143 us (22%)
  other arithmetic  35.7 us (5%)
  waiting for transfers between devices  34.9 us (5%)
  local copies, waits for them, and re-layouts  18.2 us (3%)
  between operations  14.9 us (2%)
    pallas_call x1, Pallas kernels, scatter_grads(): pl.pallas_call(functools.partial(scatter_kernel, n, sizes, plan, len(view...  147 us
    pallas_call x1, Pallas kernels, gather_weights(): pl.pallas_call(functools.partial(gather_kernel, n, sizes, plan), out_shap...  145 us
    pallas_call x1, Pallas kernels, recurrence_back(): pl.pallas_call(functools.partial(backward_kernel, n, sizes), out_shape=(s...  45.1 us
    pallas_call x1, Pallas kernels, recurrence(): pl.pallas_call(functools.partial(forward_kernel, n, sizes), out_shape=(sh...  39.9 us
    psum x1, waiting for transfers between devices, body(): attn_branch = lax.psum(attn_part, 'head')  30.5 us
    pallas_call x1, Pallas kernels, sum_small(): pl.pallas_call(functools.partial(sum_kernel, n, sizes, shared), out_shape...  27.2 us
    dot_general x4, matrix products, body(): jnp.einsum('td,tn->dn', left, right, preferred_element_type=jnp.float32)  25.5 us
    dot_general x1, matrix products, body(): jnp.einsum('sij,sik->sjk', basis_left, owned_grads, precision=highest_pre...  18.7 us
  transfers between devices with their start and end apart: 4, of which 2 were waited for; matrix products, arithmetic and copies ran while one was open for 16% of the time, Pallas kernels for 45%

profile of v2, /device:TPU:30, one launch (start us, length us, event | category | flops | bytes accessed | tf_op | source)
XLA Modules:
  0.0 652.2 jit_solution(11310826286885613815)
XLA Ops:
  14.3 2.1 fusion.13
  19.3 145.1 %shard_map.457 = bf16[4,2,2,64,6272]{4,3,2,1,0:T(8,128)(2,1)} custom-call(s32[1,49]{1,0:T(1,128)S(1)} %copy-done.2, bf16[4,1024,128]{2,1,0:T(8,128)(2,1)S(1)} %copy-done.1), custom_call_target="tpu_custom_call" | custom-call | tf_op jit(solution)/shard_map/pallas_call | solution.py:95
  164.4 5.4 fusion.20
  170.6 2.9 fusion.40
  178.5 2.6 fusion.36.halo_ref
  181.1 39.9 %shard_map.458 = (f32[1024,1024]{1,0:T(8,128)}, f32[1024,256]{1,0:T(8,128)}, f32[1024,512]{1,0:T(8,128)}, bf16[1024,512]{1,0:T(8,128)(2,1)}, f32[9,2,256,128]{3,2,1,0:T(8,128)}) custom-call(bf16[1024,1024]{1,0:T(8,128)(2,1)} %slice.201.proj_ref, bf16[16,1024]{1,0:T(8,128)(2,1)} %fusion.36.halo_ref, f32[1024,256]{1,0:T(8,128)} %get-tuple-element.91.lg_ref, ...), custom_call_target="tpu_custom_call" | custom-call | tf_op jit(solution)/shard_map/pallas_call | solution.py:640
  221.1 4.8 fusion.46
  226.2 30.5 %all-reduce.9.cloned.1.call-done = f32[1024,1024]{1,0:T(8,128)} async-done(((f32[1024,1024]{1,0:T(8,128)}), f32[1024,1024]{1,0:T(8,128)}) %all-reduce.9.cloned.1.call-update) | async-done | bytes 4194320 | tf_op jit(solution)/shard_map/psum | solution.py:1067
  256.7 3.0 multiply_reduce_fusion.2
  261.6 11.8 %fusion.3 = f32[1024,2816]{1,0:T(8,128)} fusion(bf16[1024,6272]{1,0:T(8,128)(2,1)} %bitcast.71, f32[1024,1024]{1,0:T(8,128)S(1)} %get-tuple-element.73, f32[1024]{0:T(1024)S(1)} %bitcast.92, f32[1024]{0:T(1024)S(1)} %add_rsqrt_fusion), kind=kOutput, calls=%fused_computation.16 | convolution fusion | flops 5908725760 | bytes 21504000 | tf_op jit(solution)/shard_map/dot_general | solution.py:1071
  273.5 9.9 %multiply_convert_fusion.1 = (bf16[1024,1408]{1,0:T(8,128)(2,1)S(1)}, bf16[1024,1408]{1,0:T(8,128)(2,1)}, bf16[1024,1408]{1,0:T(8,128)(2,1)}) fusion(f32[1024,2816]{1,0:T(8,128)} %fusion.3, bf16[1024,6272]{1,0:T(8,128)(2,1)S(1)} %bitcast.77, bf16[1024,1024]{1,0:T(8,128)(2,1)S(1)} %copy-done.13, f32[1024]{0:T(1024)S(1)} %fusion.71), kind=kOutput, calls=%fused_computation.8 | convolution fusion | flops 2977562624 | bytes 25169920 | tf_op jit(solution)/shard_map/dot_general | solution.py:1081
  284.9 9.0 %fusion.1 = f32[1024,1024]{1,0:T(8,128)} fusion(bf16[1024,6272]{1,0:T(8,128)(2,1)S(1)} %bitcast.78, bf16[1024,1408]{1,0:T(8,128)(2,1)} %get-tuple-element.77, bf16[1024,1408]{1,0:T(8,128)(2,1)S(1)} %get-tuple-element.76), kind=kOutput, calls=%fused_computation.14 | convolution fusion | flops 5917114368 | bytes 15728640 | tf_op jit(solution)/shard_map/tn,dn->td/dot_general | solution.py:1086
  295.3 7.7 %convolution_convert_fusion.1 = bf16[1024,1408]{1,0:T(8,128)(2,1)} fusion(bf16[1024,1408]{1,0:T(8,128)(2,1)} %get-tuple-element.78, bf16[1024,1024]{1,0:T(8,128)(2,1)} %param.27, f32[1024]{0:T(1024)S(1)} %fusion.71), kind=kOutput, calls=%fused_computation.40 | convolution fusion | flops 2957377536 | bytes 7868416 | tf_op jit(solution)/shard_map/td,tn->dn/dot_general | solution.py:1134
  303.1 7.7 %fusion.33 = bf16[1024,1024]{1,0:T(8,128)(2,1)} fusion(bf16[1024,1408]{1,0:T(8,128)(2,1)S(1)} %copy-done.41, bf16[1024,6272]{1,0:T(8,128)(2,1)} %bitcast.72), kind=kOutput, calls=%fused_computation.61 | convolution fusion | flops 2953838592 | bytes 7864320 | tf_op jit(solution)/shard_map/tn,dn->td/dot_general | solution.py:1076
  310.8 8.6 %convolution_convert_fusion = bf16[1024,2816]{1,0:T(8,128)(2,1)} fusion(bf16[1024,1408]{1,0:T(8,128)(2,1)S(1)} %copy-done.40, bf16[1024,1408]{1,0:T(8,128)(2,1)S(1)} %copy-done.39, f32[1024,1024]{1,0:T(8,128)S(1)} %copy-done.5, f32[1024]{0:T(1024)S(1)} %bitcast.93, f32[1024]{0:T(1024)S(1)} %add_rsqrt_fusion), kind=kOutput, calls=%fused_computation.12 | convolution fusion | flops 5923143680 | bytes 15736832 | tf_op jit(solution)/shard_map/td,tn->dn/dot_general | solution.py:1134
  319.4 4.4 all-reduce.11.cloned.1.call-done
  323.8 5.2 multiply_reduce_fusion
  329.7 3.2 subtract_add_fusion
  332.9 4.7 fusion.43.du_ref
  337.6 2.3 convolution_convert_fusion.3
  339.9 45.1 %shard_map.459 = (bf16[1024,1024]{1,0:T(8,128)(2,1)}, bf16[1024,512]{1,0:T(8,128)(2,1)}, f32[1024,256]{1,0:T(8,128)}, f32[8,1024]{1,0:T(8,128)}, f32[8,256]{1,0:T(8,128)}) custom-call(bf16[1024,1024]{1,0:T(8,128)(2,1)} %slice.201.proj_ref, bf16[16,1024]{1,0:T(8,128)(2,1)} %fusion.36.halo_ref, f32[1024,1024]{1,0:T(8,128)} %get-tuple-element.38.conv_ref, ...), custom_call_target="tpu_custom_call" | custom-call | tf_op jit(solution)/shard_map/pallas_call | solution.py:907
  387.0 6.5 fusion.18
  394.5 2.1 add_convert_fusion
  400.8 6.9 %convolution_convert_fusion.2 = bf16[1024,1536]{1,0:T(8,128)(2,1)} fusion(bf16[1024,1536]{1,0:T(8,128)(2,1)} %copy-done.14, bf16[1024,1024]{1,0:T(8,128)(2,1)S(1)} %copy-done.7, f32[1024]{0:T(1024)S(1)} %bitcast.88, f32[1024]{0:T(1024)S(1)} %add_rsqrt_fusion.1), kind=kOutput, calls=%fused_computation.41 | convolution fusion | flops 3226992640 | bytes 8396800 | tf_op jit(solution)/shard_map/td,tn->dn/dot_general | solution.py:1134
  407.7 146.9 %shard_map.460 = bf16[4,16,64,128]{3,2,1,0:T(8,128)(2,1)} custom-call(s32[1,64]{1,0:T(1,128)} %select_bitcast_fusion.inv_ref, bf16[4,2,2,64,1536]{4,3,2,1,0:T(8,128)(2,1)} %bitcast.81, bf16[4,2,2,64,2816]{4,3,2,1,0:T(8,128)(2,1)} %bitcast.80, bf16[4,2,2,64,512]{4,3,2,1,0:T(8,128)(2,1)} %bitcast.83, bf16[4,2,2,64,1408]{4,3,2,1,0:T(8,128)(2,1)} %bitcast.82), custom_call_target="tpu_custom_call" | custom-call | tf_op jit(solution)/shard_map/pallas_call | solution.py:201
  557.4 18.7 %fusion.90 = f32[4,128,1024]{1,2,0:T(8,128)S(1)} fusion(bf16[4,1024,128]{2,1,0:T(8,128)(2,1)S(1)} %bitcast.79, f32[4,1024,1024]{2,1,0:T(8,128)} %param.35), kind=kOutput, calls=%fused_computation.156 | convolution fusion | flops 6442450944 | bytes 19922944 | tf_op jit(solution)/shard_map/sij,sik->sjk/dot_general | solution.py:1162
  576.1 5.3 fusion.26
  581.5 17.5 %fusion.29 = f32[4,128,1024]{1,2,0:T(8,128)S(1)} fusion(f32[4,1024,1024]{2,1,0:T(8,128)S(1)} %bitcast.67, f32[4,1024,128]{2,1,0:T(8,128)} %get-tuple-element.80, f32[4,1024,128]{2,1,0:T(8,128)S(1)} %get-tuple-element.79), kind=kOutput, calls=%fused_computation.57 | convolution fusion | flops 6443499520 | bytes 23068672 | tf_op jit(solution)/shard_map/sij,sjk->sik/dot_general | solution.py:1167
  599.0 4.6 fusion.89
  603.6 5.9 fusion.16
  609.6 27.2 %shard_map.461 = f32[40,1024]{1,0:T(8,128)S(1)} custom-call(f32[40,1024]{1,0:T(8,128)S(1)} %pad_maximum_fusion.3.x_ref), custom_call_target="tpu_custom_call" | custom-call | tf_op jit(solution)/shard_map/pallas_call | solution.py:293
  637.0 5.0 fusion.12
  (171 shorter events, 35.0 us)
Async XLA Ops:
  7.2 568.9 %copy-start = (f32[4,128,128]{2,1,0:T(8,128)S(1)}, f32[4,128,128]{2,1,0:T(8,128)}, u32[]{:S(2)}) copy-start(f32[4,128,128]{2,1,0:T(8,128)} %param.36) | copy-start | bytes 786436
  7.2 249.5 %all-reduce.9.cloned.1.call-start = ((), (), s32[]{:S(2)}) async-start(), calls=%async_computation | async-start | bytes 8388608 | tf_op jit(solution)/shard_map/psum | solution.py:1067
  8.1 170.3 %collective-permute-start = (bf16[16,1024]{1,0:T(8,128)(2,1)S(1)}, bf16[16,1024]{1,0:T(8,128)(2,1)S(1)}, u32[]{:S(2)}, u32[]{:S(2)}) collective-permute-start(bf16[16,1024]{1,0:T(8,128)(2,1)S(1)} %slice.99), channel_id=1, source_target_pairs={{0,2},{2,4},{4,6},{6,8},{8,10},{10,12},{12,14},{14,16},{16,18},{18... | collective-permute-start | bytes 98312 | tf_op jit(solution)/shard_map/ppermute | solution.py:312
  17.4 161.1 %copy-start.22 = (f32[1,1024]{1,0:T(1,128)}, f32[1,1024]{1,0:T(1,128)S(1)}, u32[]{:S(2)}) copy-start(f32[1,1024]{1,0:T(1,128)S(1)} %get-tuple-element.82) | copy-start | bytes 12292
  19.3 145.1 %copy-start.7 = (bf16[1024,1024]{1,0:T(8,128)(2,1)S(1)}, bf16[1024,1024]{1,0:T(8,128)(2,1)}, u32[]{:S(2)}) copy-start(bf16[1024,1024]{1,0:T(8,128)(2,1)} %param.26) | copy-start | bytes 6291460
  170.5 6.7 %copy-start.19 = (f32[1024,16]{0,1:T(8,128)}, f32[1024,16]{0,1:T(8,128)S(1)}, u32[]{:S(2)}) copy-start(f32[1024,16]{0,1:T(8,128)S(1)} %fusion.61) | copy-start | bytes 196612
  225.9 97.8 %all-reduce.11.cloned.1.call-start = ((), (), s32[]{:S(2)}) async-start(), calls=%async_computation.1 | async-start | bytes 8388608 | tf_op jit(solution)/shard_map/psum | solution.py:1085
  256.7 16.8 %slice-start.4 = ((s8[12845056]{0:T(1024)(128)(4,1)}), s8[4194304]{0:T(1024)(128)(4,1)S(1)}, s32[]{:S(2)}) async-start(s8[12845056]{0:T(1024)(128)(4,1)} %bitcast.75), calls=%async_computation.7 | async-start | bytes 8388608
  261.6 11.8 %slice-start.5 = ((s8[12845056]{0:T(1024)(128)(4,1)}), s8[4194304]{0:T(1024)(128)(4,1)S(1)}, s32[]{:S(2)}) async-start(s8[12845056]{0:T(1024)(128)(4,1)} %bitcast.75), calls=%async_computation.8 | async-start | bytes 8388608
  261.6 11.8 %slice-start.6 = ((s8[12845056]{0:T(1024)(128)(4,1)}), s8[4194304]{0:T(1024)(128)(4,1)S(1)}, s32[]{:S(2)}) async-start(s8[12845056]{0:T(1024)(128)(4,1)} %bitcast.75), calls=%async_computation.9 | async-start | bytes 8388608
  261.6 11.8 %slice-start.7 = ((s8[12845056]{0:T(1024)(128)(4,1)}), s8[262144]{0:T(1024)(128)(4,1)S(1)}, s32[]{:S(2)}) async-start(s8[12845056]{0:T(1024)(128)(4,1)} %bitcast.75), calls=%async_computation.10 | async-start | bytes 524288
  261.6 11.8 %copy-start.13 = (bf16[1024,1024]{1,0:T(8,128)(2,1)S(1)}, bf16[1024,1024]{1,0:T(8,128)(2,1)}, u32[]{:S(2)}) copy-start(bf16[1024,1024]{1,0:T(8,128)(2,1)} %param.27) | copy-start | bytes 6291460
  294.0 309.6 %all-reduce.13.cloned.1.call-start = ((), (), s32[]{:S(2)}) async-start(), calls=%async_computation.2 | async-start | bytes 8388608 | tf_op jit(solution)/shard_map/psum | solution.py:1077
  295.3 7.7 %copy-start.41 = (bf16[1024,1408]{1,0:T(8,128)(2,1)S(1)}, bf16[1024,1408]{1,0:T(8,128)(2,1)}, u32[]{:S(2)}) copy-start(bf16[1024,1408]{1,0:T(8,128)(2,1)} %get-tuple-element.78) | copy-start | bytes 8650756
  303.1 7.7 %copy-start.5 = (f32[1024,1024]{1,0:T(8,128)S(1)}, f32[1024,1024]{1,0:T(8,128)}, u32[]{:S(2)}) copy-start(f32[1024,1024]{1,0:T(8,128)} %copy-done.4) | copy-start | bytes 12582916
  303.1 7.7 %copy-start.39 = (bf16[1024,1408]{1,0:T(8,128)(2,1)S(1)}, bf16[1024,1408]{1,0:T(8,128)(2,1)}, u32[]{:S(2)}) copy-start(bf16[1024,1408]{1,0:T(8,128)(2,1)} %copy-done.38) | copy-start | bytes 8650756
  303.1 7.7 %copy-start.40 = (bf16[1024,1408]{1,0:T(8,128)(2,1)S(1)}, bf16[1024,1408]{1,0:T(8,128)(2,1)}, u32[]{:S(2)}) copy-start(bf16[1024,1408]{1,0:T(8,128)(2,1)} %get-tuple-element.77) | copy-start | bytes 8650756
  387.0 6.5 copy-start.14
  387.0 6.5 copy-start.10
  557.4 24.1 %slice-start = ((s8[16777216]{0:T(1024)(128)(4,1)}), s8[4194304]{0:T(1024)(128)(4,1)S(1)}, s32[]{:S(2)}) async-start(s8[16777216]{0:T(1024)(128)(4,1)} %bitcast.66), calls=%async_computation.3 | async-start | bytes 8388608
  557.4 24.1 %slice-start.1 = ((s8[16777216]{0:T(1024)(128)(4,1)}), s8[4194304]{0:T(1024)(128)(4,1)S(1)}, s32[]{:S(2)}) async-start(s8[16777216]{0:T(1024)(128)(4,1)} %bitcast.66), calls=%async_computation.4 | async-start | bytes 8388608
  557.4 24.1 %slice-start.2 = ((s8[16777216]{0:T(1024)(128)(4,1)}), s8[4194304]{0:T(1024)(128)(4,1)S(1)}, s32[]{:S(2)}) async-start(s8[16777216]{0:T(1024)(128)(4,1)} %bitcast.66), calls=%async_computation.5 | async-start | bytes 8388608
  581.4 17.5 %copy-start.12 = (f32[4,1024,128]{2,1,0:T(8,128)}, f32[4,1024,128]{2,1,0:T(8,128)S(1)}, u32[]{:S(2)}) copy-start(f32[4,1024,128]{2,1,0:T(8,128)S(1)} %get-tuple-element.79) | copy-start | bytes 6291460
  636.8 7.8 %copy-start.33 = (f32[1,256]{1,0:T(1,128)}, f32[1,256]{1,0:T(1,128)S(1)}, u32[]{:S(2)}) copy-start(f32[1,256]{1,0:T(1,128)S(1)} %slice.124) | copy-start | bytes 3076
  636.9 6.4 copy-start.24
  637.0 6.4 copy-start.31
  637.0 6.4 copy-start.32
  637.0 7.0 %copy-start.25 = (f32[17,256]{1,0:T(8,128)S(1)}, f32[17,256]{1,0:T(8,128)}, u32[]{:S(2)}) copy-start(f32[17,256]{1,0:T(8,128)} %param.44) | copy-start | bytes 52228
  637.0 7.0 %copy-start.26 = (f32[17,256]{1,0:T(8,128)S(1)}, f32[17,256]{1,0:T(8,128)}, u32[]{:S(2)}) copy-start(f32[17,256]{1,0:T(8,128)} %param.45) | copy-start | bytes 52228
  637.0 7.7 %copy-start.30 = (f32[256]{0:T(256)S(1)}, f32[256]{0:T(256)}, u32[]{:S(2)}) copy-start(f32[256]{0:T(256)} %param.46) | copy-start | bytes 3076
  637.0 7.7 %copy-start.34 = (f32[256]{0:T(256)S(1)}, f32[256]{0:T(256)}, u32[]{:S(2)}) copy-start(f32[256]{0:T(256)} %param.47) | copy-start | bytes 3076
  637.0 7.7 %copy-start.35 = (f32[256]{0:T(256)S(1)}, f32[256]{0:T(256)}, u32[]{:S(2)}) copy-start(f32[256]{0:T(256)} %param.48) | copy-start | bytes 3076
  (23 other events, 96.7 us)
Sparse Core Ops, SparseCore 0:
  226.1 30.5 all-reduce.8
  294.1 29.5 all-reduce.10
  396.7 38.1 all-reduce.12

commit v3 on v2

v3 whole, which is shorter than its diff:
```python
import functools

import jax
import jax.numpy as jnp
from jax import lax
from jax.experimental import pallas as pl
from jax.experimental.pallas import tpu as pltpu
from jax.sharding import PartitionSpec as P

MESH = pl.DeviceIdType.MESH

DK = 128
DV = 256


highest_precision = lax.Precision.HIGHEST
norm_epsilon = 1e-06
adam_epsilon = 1e-08
gate_scale = 16.0
moment_decay = 0.5
rate_block = 0.03
rate_gains = 0.45
rate_down = 0.02
rate_upper = 0.6
rate_head = 0.5
rate_conv = 0.1


def axis_sizes(n):
    side = 1
    while (side * 2) ** 2 * 4 <= n:
        side *= 2
    return (n // (side * side), side, side)


def coords(me, sizes):
    _, rows, columns = sizes
    return [me // (rows * columns), (me // columns) % rows, me % columns]


def index_of(c, sizes):
    _, rows, columns = sizes
    return (c[0] * rows + c[1]) * columns + c[2]


def neighbour(c, sizes, ax, j):
    d = list(c)
    d[ax] = lax.rem(c[ax] + j, sizes[ax])
    return index_of(d, sizes)


def enter(n, me, mate=False):
    barrier = pltpu.get_barrier_semaphore()
    if mate:
        core = lax.axis_index("head")
        pl.semaphore_signal(barrier, inc=1, device_id={"head": 1 - core}, device_id_type=MESH)
    for j in range(1, n):
        pl.semaphore_signal(
            barrier, inc=1, device_id={"seq": lax.rem(me + j, n)}, device_id_type=MESH
        )
    pl.semaphore_wait(barrier, n - 1 + int(mate))


def remote(src, dst, send_sem, recv_sem, peer):
    return pltpu.make_async_remote_copy(
        src_ref=src,
        dst_ref=dst,
        send_sem=send_sem,
        recv_sem=recv_sem,
        device_id={"seq": peer},
        device_id_type=MESH,
    )


def build_plan(widths, parts, pieces, orders, base=0):
    total = sum(widths)
    bounds = [sum(widths[:i]) for i in range(len(widths) + 1)]
    cuts = [round(total * f) for f in (0.0,) + parts]
    plan, at = [], 0
    for i in range(pieces):
        for order, lo, hi in zip(orders, cuts[:-1], cuts[1:], strict=True):
            size = hi - lo
            left = size * (i + 1) // pieces - size * i // pieces
            while left:
                which = max(q for q in range(len(widths)) if bounds[q] <= at)
                step = min(left, bounds[which + 1] - at)
                start = at - bounds[which]
                plan.append((which, start, start + step, at + base, order, i))
                at += step
                left -= step
    return plan


def groups_of(plan):
    streams = {}
    for i, chunk in enumerate(plan):
        streams.setdefault(chunk[4], {}).setdefault(chunk[5], []).append(i)
    return streams


def gather_steps(sizes, plan, piece, outs, bw, send, recv):
    c = coords(lax.axis_index("seq"), sizes)
    most = max(sizes)

    def copies(i, k):
        which, lo, hi, at, order, _ = plan[i]
        ax = order[k]
        wide = pl.ds(lo * bw, (hi - lo) * bw)
        index = tuple(slice(None) if a in order[:k] else c[a] for a in range(3))
        index += (slice(None), wide)
        target = outs[which].at[index]
        source = target if k else piece.at[:, pl.ds(at * bw, (hi - lo) * bw)]
        return [
            remote(
                source,
                target,
                send.at[(i * 3 + k) * most + j],
                recv.at[(i * 3 + k) * most + j],
                neighbour(c, sizes, ax, j),
            )
            for j in range(1, sizes[ax])
        ]

    streams = groups_of(plan)
    longest = max(max(s) for s in streams.values()) + 1

    def step(s):
        for k in (2, 1, 0):
            for groups in streams.values():
                for i in groups.get(s - k, ()):
                    if k:
                        for copy in copies(i, k - 1):
                            copy.wait_recv()
                    for copy in copies(i, k):
                        copy.start()

    def arrived(piece_range):
        for groups in streams.values():
            for s in piece_range:
                for i in groups.get(s, ()):
                    for copy in copies(i, 2):
                        copy.wait_recv()

    def sent():
        for i in range(len(plan)):
            for k in range(3):
                for copy in copies(i, k):
                    copy.wait_send()

    return [functools.partial(step, s) for s in range(longest + 2)], arrived, sent


def scatter_scratch(sizes, plan, rows, bw, dtype):
    own, first, second, third = [], [], [], []
    for _, lo, hi, _, order, _ in plan:
        wide = (hi - lo) * bw
        rest = tuple(sizes[q] for q in range(3) if q != order[0])
        own.append(pltpu.VMEM(rest + (rows, wide), dtype))
        first.append(pltpu.VMEM((sizes[order[0]] - 1,) + rest + (rows, wide), dtype))
        second.append(pltpu.VMEM((sizes[order[1]], sizes[order[2]], rows, wide), dtype))
        third.append(pltpu.VMEM((sizes[order[2]], rows, wide), dtype))
    count = len(plan) * 3 * max(sizes)
    return (
        own
        + first
        + second
        + third
        + [
            pltpu.SemaphoreType.DMA((count,)),
            pltpu.SemaphoreType.DMA((count,)),
            pltpu.SemaphoreType.DMA((len(plan),)),
        ]
    )


def scatter_steps(sizes, plan, grads, scratch, fin, bw):
    c = coords(lax.axis_index("seq"), sizes)
    most, count = max(sizes), len(plan)
    own, first, second, third = (scratch[i * count : (i + 1) * count] for i in range(4))
    send, recv, load = scratch[4 * count :]

    def loading(i):
        which, lo, hi, _, order, _ = plan[i]
        index = tuple(c[q] if q == order[0] else slice(None) for q in range(3))
        index += (slice(None), pl.ds(lo * bw, (hi - lo) * bw))
        return pltpu.make_async_copy(grads[which].at[index], own[i], load.at[i])

    def copies(i, k):
        which, lo, hi, _, order, _ = plan[i]
        ax = order[k]
        left = sorted(set(range(3)) - set(order[:k]))
        result = []
        for j in range(1, sizes[ax]):
            there = lax.rem(c[ax] + j, sizes[ax])
            index = tuple(there if q == ax else slice(None) for q in left)
            if k == 0:
                index += (slice(None), pl.ds(lo * bw, (hi - lo) * bw))
                source, target = grads[which].at[index], first[i].at[j - 1]
            elif k == 1:
                source, target = own[i].at[index], second[i].at[j]
            else:
                source, target = second[i].at[(0,) + index], third[i].at[j]
            s = (i * 3 + k) * most + j
            result.append(
                remote(source, target, send.at[s], recv.at[s], neighbour(c, sizes, ax, j))
            )
        return result

    def combine(i, k):
        _, lo, hi, at, order, _ = plan[i]
        if k == 0:
            loading(i).wait()
        for copy in copies(i, k):
            copy.wait_recv()
        size = sizes[order[k]]
        if k == 0:
            outer, inner = own[i].shape[:2]

            def add(t, _):
                u, v = t // inner, t % inner
                total = own[i][u, v].astype(jnp.float32)
                for j in range(size - 1):
                    total = total + first[i][j, u, v].astype(jnp.float32)
                own[i][u, v] = total.astype(own[i].dtype)
                return 0

            lax.fori_loop(0, outer * inner, add, 0)
        elif k == 1:
            leading = sorted(set(range(3)) - {order[0]}).index(order[1]) == 0

            def add(t, _):
                total = own[i][(c[order[1]], t) if leading else (t, c[order[1]])]
                total = total.astype(jnp.float32)
                for j in range(1, size):
                    total = total + second[i][j, t].astype(jnp.float32)
                second[i][0, t] = total.astype(own[i].dtype)
                return 0

            lax.fori_loop(0, sizes[order[2]], add, 0)
        else:
            total = second[i][0, c[order[2]]].astype(jnp.float32)
            for j in range(1, size):
                total = total + third[i][j].astype(jnp.float32)
            for b in range(hi - lo):
                fin[at + b] = total[:, b * bw : (b + 1) * bw].astype(fin.dtype)

    streams = groups_of(plan)
    longest = max(max(s) for s in streams.values()) + 1

    def step(s):
        for k in range(4):
            for groups in streams.values():
                for i in groups.get(s - k, ()):
                    if k == 0:
                        loading(i).start()
                    else:
                        combine(i, k - 1)
                    if k < 3:
                        for copy in copies(i, k):
                            copy.start()

    def sent():
        for i in range(count):
            for k in range(3):
                for copy in copies(i, k):
                    copy.wait_send()

    return [functools.partial(step, s) for s in range(longest + 3)], sent


SPREAD = ((2, 1, 0), (1, 2, 0), (0, 1, 2))
COLLECT = ((0, 1, 2), (0, 2, 1), (2, 1, 0))
SHARES = (0.43, 0.86, 1.0)


def scatter_kernel(n, sizes, plan, shared, inv_ref, small_ref, grad_ref, early_ref, *refs):
    out_ref, small_out, fin, send, a_send, a_recv, l_sem = refs[:7]
    small = sum_steps(sizes, shared, small_ref, small_out, *refs[-5:])
    me = lax.axis_index("seq")
    slots, _, rows, bw = out_ref.shape
    count = fin.shape[0] - 1 - early_ref.shape[0]
    enter(n, me, True)
    steps, sent = scatter_steps(sizes, plan, [grad_ref], refs[7:-5], fin, bw)
    small[0]()
    steps[0]()
    fin[fin.shape[0] - 1] = jnp.zeros(fin.shape[1:], fin.dtype)
    fin[count : fin.shape[0] - 1] = early_ref[...]
    for s, step in enumerate(steps[1:]):
        step()
        if s + 1 < len(small):
            small[s + 1]()
    for s in range(send.shape[0]):
        send[s] = fin[inv_ref[0, s]]

    def move(j):
        p = lax.rem(me + j, n)
        return remote(
            send.at[pl.ds(p * slots, slots)], out_ref.at[:, me], a_send.at[j], a_recv.at[j], p
        )

    for j in range(1, n):
        move(j).start()
    mine = pltpu.make_async_copy(
        send.at[pl.ds(me * slots, slots)], out_ref.at[:, me], l_sem.at[0]
    )
    mine.start()
    for step in small[len(steps) :]:
        step()
    mine.wait()
    for j in range(1, n):
        move(j).wait()
    sent()


def scatter_grads(grad, early, inverse, slots, small, shared):
    n = lax.axis_size("seq")
    sizes = axis_sizes(n)
    most = max(sizes)
    depth, columns = grad.shape
    _, rows, bw = early.shape
    blocks = columns // bw
    plan = build_plan((blocks,), SHARES, 2, SPREAD)
    shape = jax.ShapeDtypeStruct
    vmem, anywhere = pl.BlockSpec(memory_space=pltpu.VMEM), pl.BlockSpec(memory_space=pl.ANY)
    out, summed = pl.pallas_call(
        functools.partial(scatter_kernel, n, sizes, plan, shared),
        out_shape=(shape((slots, n, rows, bw), grad.dtype), shape(small.shape, small.dtype)),
        in_specs=[pl.BlockSpec(memory_space=pltpu.SMEM), vmem, anywhere, vmem],
        out_specs=(anywhere, vmem),
        scratch_shapes=[
            pltpu.VMEM((blocks + early.shape[0] + 1, rows, bw), grad.dtype),
            pltpu.VMEM((slots * n, rows, bw), grad.dtype),
            pltpu.SemaphoreType.DMA((n,)),
            pltpu.SemaphoreType.DMA((n,)),
            pltpu.SemaphoreType.DMA((1,)),
        ]
        + scatter_scratch(sizes, plan, rows, bw, grad.dtype)
        + [
            pltpu.VMEM((shared,) + small.shape[1:], small.dtype),
            pltpu.VMEM((3,) + small.shape, small.dtype),
            pltpu.VMEM((3, most) + small.shape, small.dtype),
            pltpu.SemaphoreType.DMA((1 + 3 * most,)),
            pltpu.SemaphoreType.DMA((1 + 3 * most,)),
        ],
        compiler_params=pltpu.CompilerParams(
            collective_id=2, has_side_effects=True, vmem_limit_bytes=48 << 20
        ),
    )(inverse, small, grad.reshape(sizes + (rows, columns)), early)
    return out.reshape(slots, depth, bw), summed


def sum_steps(sizes, shared, x_ref, out_ref, mate, acc, bufs, send, recv):
    me, core = lax.axis_index("seq"), lax.axis_index("head")
    c = coords(me, sizes)
    most = max(sizes)
    swap = pltpu.make_async_remote_copy(
        src_ref=x_ref.at[pl.ds(0, shared)],
        dst_ref=mate,
        send_sem=send.at[0],
        recv_sem=recv.at[0],
        device_id={"head": 1 - core},
        device_id_type=MESH,
    )

    def going(step, ax):
        copies = []
        for j in range(1, sizes[ax]):
            d = list(c)
            d[ax] = lax.rem(c[ax] + j, sizes[ax])
            q = 1 + ax * most + j
            copies.append(
                remote(
                    acc.at[step], bufs.at[ax, c[ax]], send.at[q], recv.at[q], index_of(d, sizes)
                )
            )
        return copies

    def total(ax):
        value = bufs[ax, 0]
        for j in range(1, sizes[ax]):
            value = value + bufs[ax, j]
        return value

    def start(step, ax):
        bufs[ax, c[ax]] = acc[step]
        for copy in going(step, ax):
            copy.start()

    def swapped():
        swap.wait()
        acc[0, 0:shared] = x_ref[0:shared] + mate[...]
        acc[0, shared:] = x_ref[shared:]
        start(0, 2)

    def moved(step, ax):
        for copy in going(step, ax):
            copy.wait()
        if step < 2:
            acc[step + 1] = total(ax)
            start(step + 1, ax - 1)
        else:
            out_ref[...] = total(ax)

    return [
        swap.start,
        swapped,
        functools.partial(moved, 0, 2),
        functools.partial(moved, 1, 1),
        functools.partial(moved, 2, 0),
    ]


NN = (((1,), (0,)), ((), ()))
NT = (((1,), (1,)), ((), ()))
TN = (((0,), (0,)), ((), ()))
TILE = 128


def halves(values):
    high = values.astype(jnp.bfloat16)
    return high, (values - high.astype(jnp.float32)).astype(jnp.bfloat16)


def product(left, right, dims):
    (lh, ll), (rh, rl) = left, right
    dot = functools.partial(
        lax.dot_general, dimension_numbers=dims, preferred_element_type=jnp.float32
    )
    return dot(lh, rh) + (dot(lh, rl) + dot(ll, rh))


def running_sum(table, values):
    first = values.astype(jnp.bfloat16)
    rest = values - first.astype(jnp.float32)
    second, third = halves(rest)
    dot = functools.partial(
        lax.dot_general, dimension_numbers=NN, preferred_element_type=jnp.float32
    )
    return dot(table, first) + (dot(table, second) + dot(table, third))


def sigmoid(values):
    return 1.0 / (1.0 + jnp.exp(-values))


def chain_tools(n, sizes, forward, mine, bufs, send, recv, result):
    me = lax.axis_index("seq")
    c = coords(me, sizes)
    pieces = mine.shape[0]
    across, along, before, held = bufs
    most = max(sizes)
    state = pl.ds(0, TILE)
    decay = pl.ds(TILE, 1)

    def peers(ax):
        return [j for j in range(1, sizes[ax])]

    def to(ax, j):
        d = list(c)
        d[ax] = lax.rem(c[ax] + j, sizes[ax])
        return index_of(d, sizes)

    def line(buf, source, ax, j, p, base):
        s = base + j * pieces + p
        return remote(source.at[p], buf.at[c[ax], p], send.at[s], recv.at[s], to(ax, j))

    def hop(p):
        s = 2 * most * pieces + p
        step = 1 if forward else -1
        d = [lax.rem(c[0] + step + sizes[0], sizes[0]), c[1], c[2]]
        return remote(held.at[1, p], held.at[0, p], send.at[s], recv.at[s], index_of(d, sizes))

    def compose(first, second):
        return (second[1] * first[0] + second[0], first[1] * second[1])

    def reduce_line(buf, ax, p):
        size = sizes[ax]
        order = range(size) if forward else range(size - 1, -1, -1)
        prefix = (jnp.zeros((TILE, TILE), jnp.float32), jnp.ones((1, TILE), jnp.float32))
        total = None
        for i in order:
            item = (buf[i, p, state], buf[i, p, decay])
            longer = compose(prefix, item)
            take = (i < c[ax]) if forward else (i > c[ax])
            prefix = tuple(jnp.where(take, a, b) for a, b in zip(longer, prefix, strict=True))
            total = item if total is None else compose(total, item)
        return prefix, total

    def start_x():
        for p in range(pieces):
            across[c[2], p] = mine[p]
            for j in peers(2):
                line(across, mine, 2, j, p, 0).start()

    def start_y():
        for p in range(pieces):
            for j in peers(2):
                line(across, mine, 2, j, p, 0).wait_recv()
            prefix, total = reduce_line(across, 2, p)
            before[p, state], before[p, decay] = prefix
            held[2, p, state], held[2, p, decay] = total
            held[2, p, pl.ds(TILE + 1, 7)] = jnp.zeros((7, TILE), jnp.float32)
            along[c[1], p] = held[2, p]
            for j in peers(1):
                line(along, held.at[2], 1, j, p, most * pieces).start()

    first_z = 0 if forward else sizes[0] - 1
    last_z = sizes[0] - 1 - first_z

    def start_z():
        for p in range(pieces):
            for j in peers(1):
                line(along, held.at[2], 1, j, p, most * pieces).wait_recv()
            prefix, total = reduce_line(along, 1, p)
            own = (before[p, state], before[p, decay])
            before[p, state], before[p, decay] = compose(prefix, own)
            held[1, p, state], held[1, p, decay] = total
            held[1, p, pl.ds(TILE + 1, 7)] = jnp.zeros((7, TILE), jnp.float32)

            @pl.when(c[0] == first_z)
            def _():
                held[0, p] = jnp.zeros((TILE + 8, TILE), jnp.float32)
                hop(p).start()

    def pass_z(k):
        at = k if forward else sizes[0] - 1 - k

        @pl.when(c[0] == at)
        def _():
            for p in range(pieces):
                hop(p).wait_recv()
                if at != last_z:
                    got = (held[0, p, state], held[0, p, decay])
                    item = (held[1, p, state], held[1, p, decay])
                    held[1, p, state], held[1, p, decay] = compose(got, item)
                    hop(p).start()

    def finish():
        for p in range(pieces):
            result[p] = before[p, decay] * held[0, p, state] + before[p, state]
            for j in peers(2):
                line(across, mine, 2, j, p, 0).wait_send()
            for j in peers(1):
                line(along, held.at[2], 1, j, p, most * pieces).wait_send()

        @pl.when(c[0] != last_z)
        def _():
            for p in range(pieces):
                hop(p).wait_send()

    stages = [start_x, start_y, start_z]
    stages += [functools.partial(pass_z, k) for k in range(1, sizes[0])]
    return stages, finish


def greet(n, sizes, extra):
    c = coords(lax.axis_index("seq"), sizes)
    barrier = pltpu.get_barrier_semaphore()
    count = 0
    for ax in range(3):
        for j in range(1, sizes[ax]):
            d = list(c)
            d[ax] = lax.rem(c[ax] + j, sizes[ax])
            pl.semaphore_signal(
                barrier, inc=1, device_id={"seq": index_of(d, sizes)}, device_id_type=MESH
            )
            count += 1
    for index in extra:
        pl.semaphore_signal(barrier, inc=1, device_id={"seq": index}, device_id_type=MESH)
        count += 1
    pl.semaphore_wait(barrier, count)


def tile_masks(rows_ref, cols_ref, c):
    row = rows_ref[pl.ds(c, 1), :]
    col = cols_ref[pl.ds(pl.multiple_of(c * TILE, TILE), TILE), 6:7]
    i = lax.broadcasted_iota(jnp.int32, (TILE, TILE), 0)
    j = lax.broadcasted_iota(jnp.int32, (TILE, TILE), 1)
    return (i >= j) & (row == col)


def forward_kernel(
    n,
    sizes,
    plan,
    ready,
    owners_ref,
    lengths_ref,
    packing_ref,
    slot_ref,
    tokens_ref,
    norm_ref,
    down_ref,
    upper_ref,
    taps_ref,
    gain_ref,
    w_in_out,
    w_up_out,
    w_out_out,
    w_down_out,
    normed_out,
    lowrank_ref,
    logits_out,
    proj_out,
    halo_ref,
    gate_out,
    conv_out,
    cum_out,
    o_out,
    u_out,
    start_out,
    cols_ref,
    rows_ref,
    normed,
    logits_ref,
    proj_ref,
    gate_ref,
    conv_ref,
    cum_ref,
    o_ref,
    u_ref,
    start_ref,
    slots,
    piece,
    w_in,
    rim,
    segs,
    act,
    state,
    prev,
    a_send,
    a_recv,
    g_send,
    g_recv,
    l_sem,
    mine,
    across,
    along,
    before,
    held,
    result,
    send,
    recv,
):
    me = lax.axis_index("seq")
    c3 = coords(me, sizes)
    length, width = tokens_ref.shape
    tiles, channels = length // TILE, proj_ref.shape[1]
    keys = logits_ref.shape[1]
    rank = down_ref.shape[1]
    heads = keys // DK
    value = DV * heads
    slots_dev, _, bw = slot_ref.shape
    rows = piece.shape[0]
    scale = DK ** (-0.5)
    enter(n, me)

    def move(j):
        p = lax.rem(me + j, n)
        return remote(
            slot_ref.at[:, pl.ds(p * rows, rows), :],
            slots.at[pl.ds(me * slots_dev, slots_dev)],
            a_send.at[j],
            a_recv.at[j],
            p,
        )

    for j in range(1, n):
        move(j).start()
    local_move = pltpu.make_async_copy(
        slot_ref.at[:, pl.ds(me * rows, rows), :],
        slots.at[pl.ds(me * slots_dev, slots_dev)],
        l_sem.at[0],
    )
    local_move.start()
    edge = remote(
        tokens_ref.at[pl.ds(length - 16, 16)],
        rim,
        a_send.at[0],
        a_recv.at[0],
        lax.rem(me + 1, n),
    )

    @pl.when(me < n - 1)
    def _():
        edge.start()

    base = me * length
    where_col = base - 8 + lax.broadcasted_iota(jnp.int32, (length + 8, 1), 0)
    lane = lax.broadcasted_iota(jnp.int32, (tiles, TILE), 1)
    where_row = base + TILE * lax.broadcasted_iota(jnp.int32, (tiles, TILE), 0) + lane
    start = jnp.int32(0)
    seg_col = jnp.zeros((length + 8, 1), jnp.float32)
    seg_row = jnp.zeros((tiles, TILE), jnp.float32)
    for q in range(lengths_ref.shape[0]):
        seg_col += (where_col >= start).astype(jnp.float32)
        seg_row += (where_row >= start).astype(jnp.float32)
        start = start + lengths_ref[packing_ref[q]]
    filled = start
    segs[...] = seg_col + (where_col >= filled).astype(jnp.float32)
    rows_ref[...] = seg_row + (where_row >= filled).astype(jnp.float32)
    lane = lax.broadcasted_iota(jnp.int32, (TILE, TILE), 1)
    for c in range(tiles):
        lo = 8 + c * TILE
        own = segs[lo : lo + TILE]
        flags = [segs[lo - 1 : lo], segs[lo + TILE - 1 : lo + TILE]]
        flags += [segs[lo - s : lo - s + TILE] for s in (1, 2, 3)]
        flags = [(other == own).astype(jnp.float32) for other in flags]
        place = base + c * TILE + lax.broadcasted_iota(jnp.int32, (TILE, 1), 0)
        flags += [None, own, (place < filled).astype(jnp.float32)]
        total = jnp.zeros((TILE, TILE), jnp.float32)
        for k, flag in enumerate(flags):
            if flag is not None:
                total = jnp.where(lane == k, flag, total)
        cols_ref[c * TILE : (c + 1) * TILE, :] = total
    cols_ref[length : length + 8, :] = jnp.zeros((8, TILE), jnp.float32)

    def norm(values):
        values = values.astype(jnp.float32)
        inverse = lax.rsqrt(jnp.mean(values * values, axis=1, keepdims=True) + norm_epsilon)
        return (values * inverse * norm_ref[...]).astype(jnp.bfloat16)

    i = lax.broadcasted_iota(jnp.int32, (TILE, TILE), 0)
    j = lax.broadcasted_iota(jnp.int32, (TILE, TILE), 1)
    lower = (i >= j).astype(jnp.bfloat16)
    down_low = down_ref[...].astype(jnp.bfloat16)
    upper = halves(upper_ref[0:rank, :])

    def gates(c, _):
        at = pl.ds(pl.multiple_of(c * TILE, TILE), TILE)
        x = norm(tokens_ref[at, :])
        normed[at, :] = x
        low = lax.dot_general(x, down_low, NN, preferred_element_type=jnp.float32)
        lowrank_ref[at, :] = low
        logits = product(halves(low), upper, NN) + upper_ref[rank : rank + 1, :]
        logits_ref[at, :] = logits
        gate = jnp.minimum(logits, 0.0) - jnp.log1p(jnp.exp(-jnp.abs(logits)))
        cum_ref[at, :] = running_sum(lower, gate * (1.0 / gate_scale))
        return 0

    lax.fori_loop(0, tiles, gates, 0)
    flushes = []

    def flush(source, target):
        copy = pltpu.make_async_copy(source, target, l_sem.at[6 + len(flushes)])
        copy.start()
        flushes.append(copy)

    flush(normed, normed_out)
    flush(logits_ref, logits_out)
    flush(cum_ref, cum_out)

    @pl.when(me > 0)
    def _():
        edge.wait_recv()

    @pl.when(me == 0)
    def _():
        rim[...] = jnp.zeros_like(rim)

    rim[...] = norm(rim[...])

    local_move.wait()
    for j in range(1, n):
        move(j).wait()
    for b in range(owners_ref.shape[1]):
        piece[:, b * bw : (b + 1) * bw] = slots[owners_ref[0, b]]
    outs = (w_in, w_up_out, w_out_out, w_down_out)
    offset, owns = 0, []
    for q, out in enumerate(outs):
        columns = out.shape[4]
        owns.append(
            pltpu.make_async_copy(
                piece.at[:, pl.ds(offset, columns)],
                out.at[c3[0], c3[1], c3[2]],
                l_sem.at[1 + q],
            )
        )
        offset += columns
    for copy in owns:
        copy.start()
    for copy in owns:
        copy.wait()
    steps, arrived, sent = gather_steps(sizes, plan, piece, outs, bw, g_send, g_recv)
    for step in steps[: ready + 2]:
        step()
    arrived(range(ready))
    rest = list(steps[ready + 2 :])
    flush(w_in, w_in_out)

    def advance():
        if rest:
            rest.pop(0)()

    advance()

    def project(r, _):
        at = pl.ds(pl.multiple_of(r * 256, 256), 256)
        x = normed[at, :]
        for lo in range(0, w_in.shape[4], 512):
            part = lax.dot_general(
                x,
                w_in[:, :, :, :, lo : lo + 512].reshape(width, 512),
                NN,
                preferred_element_type=jnp.float32,
            )
            if lo < channels:
                proj_ref[at, lo : lo + 512] = part.astype(proj_ref.dtype)
            else:
                gate_ref[at, lo - channels : lo - channels + 512] = part
        return 0

    lax.fori_loop(0, length // 256, project, 0)
    for lo in range(0, channels, 512):
        halo_ref[:, lo : lo + 512] = lax.dot_general(
            rim[...],
            w_in[:, :, :, :, lo : lo + 512].reshape(width, 512),
            NN,
            preferred_element_type=jnp.float32,
        ).astype(halo_ref.dtype)
    flush(proj_ref, proj_out)
    flush(gate_ref, gate_out)

    prev[...] = halo_ref[...]
    state[...] = jnp.zeros_like(state)
    mine[...] = jnp.zeros_like(mine)
    for p in range(mine.shape[0]):
        mine[p, TILE : TILE + 1] = jnp.ones((1, TILE), jnp.float32)
    first_step = rest.pop(0) if rest else None

    def local(c, _):
        if first_step is not None:
            pl.when(c == tiles // 2)(first_step)
        at = pl.ds(pl.multiple_of(c * TILE, TILE), TILE)
        for g in range(0, channels, 256):
            wide = slice(g, g + 256)
            block = jnp.concatenate(
                [prev[:, wide].astype(jnp.float32), proj_ref[at, wide].astype(jnp.float32)]
            )
            total = taps_ref[3:4, wide] * block[16:]
            for s in (1, 2, 3):
                total = total + taps_ref[3 - s : 4 - s, wide] * (
                    block[16 - s : 16 - s + TILE] * cols_ref[at, 1 + s : 2 + s]
                )
            conv_ref[at, wide] = total
            act[at, wide] = total * sigmoid(total)
        prev[...] = proj_ref[pl.ds(pl.multiple_of(c * TILE + TILE - 16, 16), 16), :]
        cum = cum_ref[at, :]
        last = cum[TILE - 1 : TILE]
        left = act[at, keys : 2 * keys] * jnp.exp(last - cum) * cols_ref[at, 1:2]
        decay = jnp.exp(last) * cols_ref[at, 0:1][TILE - 1 : TILE]
        for h in range(heads):
            kh = slice(h * DK, (h + 1) * DK)
            v = halves(act[at, 2 * keys + h * DV : 2 * keys + (h + 1) * DV])
            start_ref[c, h] = state[h]
            state[h] = state[h] * decay[:, kh] + product(v, halves(left[:, kh]), TN)
            for e in range(DV // TILE):
                p = h * (DV // TILE) + e
                mine[p, TILE : TILE + 1] = mine[p, TILE : TILE + 1] * decay[:, kh]
        return 0

    lax.fori_loop(0, tiles, local, 0)
    flush(conv_ref, conv_out)
    for h in range(heads):
        start_ref[tiles, h] = state[h]
        for e in range(DV // TILE):
            mine[h * (DV // TILE) + e, 0:TILE] = state[h, e * TILE : (e + 1) * TILE]
    stages, finish = chain_tools(
        n, sizes, True, mine, (across, along, before, held), send, recv, result
    )
    stages[0]()
    second_step = rest.pop(0) if rest else None

    def inside(c, _):
        for k, stage in enumerate(stages[1:]):
            pl.when(c == k + 1)(stage)
        if second_step is not None:
            pl.when(c == tiles // 2)(second_step)
        at = pl.ds(pl.multiple_of(c * TILE, TILE), TILE)
        cum = cum_ref[at, :]
        middle = cum[TILE // 2 - 1 : TILE // 2]
        q = act[at, 0:keys] * jnp.exp(cum - middle) * scale
        k = act[at, keys : 2 * keys] * jnp.exp(middle - cum)
        mask = tile_masks(rows_ref, cols_ref, c)
        for h in range(heads):
            kh = slice(h * DK, (h + 1) * DK)
            vh = slice(h * DV, (h + 1) * DV)
            scores = jnp.where(mask, product(halves(q[:, kh]), halves(k[:, kh]), NT), 0.0)
            v = halves(act[at, 2 * keys + h * DV : 2 * keys + (h + 1) * DV])
            o_ref[at, vh] = product(halves(scores), v, NN)
        return 0

    lax.fori_loop(0, tiles, inside, 0)
    finish()
    for h in range(heads):
        for e in range(DV // TILE):
            state[h, e * TILE : (e + 1) * TILE] = result[h * (DV // TILE) + e]

    def outside(c, _):
        at = pl.ds(pl.multiple_of(c * TILE, TILE), TILE)
        cum = cum_ref[at, :]
        q = act[at, 0:keys] * jnp.exp(cum) * scale * cols_ref[at, 0:1]
        decay = jnp.exp(cum[TILE - 1 : TILE]) * cols_ref[at, 0:1][TILE - 1 : TILE]
        for h in range(heads):
            kh = slice(h * DK, (h + 1) * DK)
            vh = slice(h * DV, (h + 1) * DV)
            begin = start_ref[c, h] + state[h]
            start_ref[c, h] = begin
            state[h] = state[h] * decay[:, kh]
            o = o_ref[at, vh] + product(halves(q[:, kh]), halves(begin), NT)
            o_ref[at, vh] = o
            inverse = lax.rsqrt(jnp.mean(o * o, axis=1, keepdims=True) + norm_epsilon)
            gate = gate_ref[at, vh]
            u_ref[at, vh] = (o * inverse * gain_ref[...] * (gate * sigmoid(gate))).astype(
                u_ref.dtype
            )
        return 0

    lax.fori_loop(0, tiles, outside, 0)
    for h in range(heads):
        start_ref[tiles, h] = start_ref[tiles, h] + state[h]
    flush(o_ref, o_out)
    flush(u_ref, u_out)
    flush(start_ref, start_out)
    while rest:
        advance()
    groups = {chunk[5] for chunk in plan}
    arrived(sorted(g for g in groups if g >= ready))
    sent()
    for copy in flushes:
        copy.wait()

    @pl.when(me < n - 1)
    def _():
        edge.wait_send()


def forward(
    owners, lengths, packing, slot_copy, tokens, norm, down, upper, taps, gain, counts
):
    n = lax.axis_size("seq")
    sizes = axis_sizes(n)
    length, width = tokens.shape
    slots_dev, depth, bw = slot_copy.shape
    rows = depth // n
    keys, channels = upper.shape[1], taps.shape[1]
    heads = keys // DK
    value = heads * DV
    tiles = length // TILE
    blocks = sum(counts)
    ready = 2
    plan = build_plan(counts[:1], SHARES, ready, COLLECT)
    plan += [
        (which + 1, lo, hi, at, order, group + ready)
        for which, lo, hi, at, order, group in build_plan(
            counts[1:], SHARES, 4, COLLECT, counts[0]
        )
    ]
    f32, b16 = jnp.float32, jnp.bfloat16
    shape = jax.ShapeDtypeStruct
    vmem, anywhere = pl.BlockSpec(memory_space=pltpu.VMEM), pl.BlockSpec(memory_space=pl.ANY)
    smem = pl.BlockSpec(memory_space=pltpu.SMEM)
    kept = [
        ((length, width), b16),
        ((length, keys), f32),
        ((length, channels), b16),
        ((length, value), f32),
        ((length, channels), f32),
        ((length, keys), f32),
        ((length, value), f32),
        ((length, value), b16),
        ((tiles + 1, heads, DV, DK), f32),
    ]
    big = [shape(*k) for k in kept]
    outs = [shape(sizes + (rows, count * bw), b16) for count in counts]
    outs += [big[0], shape((length, down.shape[1]), f32), big[1], big[2]]
    outs += [shape((16, channels), b16)] + big[3:]
    outs += [shape((length + 8, TILE), f32), shape((tiles, TILE), f32)]
    specs = [anywhere] * 5 + [vmem, anywhere, anywhere, vmem] + [anywhere] * 6 + [vmem, vmem]
    most = max(sizes)
    copies = len(plan) * 3 * most
    result = pl.pallas_call(
        functools.partial(forward_kernel, n, sizes, plan, ready),
        out_shape=tuple(outs),
        in_specs=[smem] * 3 + [anywhere] + [vmem] * 6,
        out_specs=tuple(specs),
        scratch_shapes=[pltpu.VMEM(*k) for k in kept]
        + [
            pltpu.VMEM((n * slots_dev, rows, bw), b16),
            pltpu.VMEM((rows, blocks * bw), b16),
            pltpu.VMEM(sizes + (rows, counts[0] * bw), b16),
            pltpu.VMEM((16, width), b16),
            pltpu.VMEM((length + 8, 1), f32),
            pltpu.VMEM((length, channels), f32),
            pltpu.VMEM((heads, DV, DK), f32),
            pltpu.VMEM((16, channels), b16),
            pltpu.SemaphoreType.DMA((n,)),
            pltpu.SemaphoreType.DMA((n,)),
            pltpu.SemaphoreType.DMA((copies,)),
            pltpu.SemaphoreType.DMA((copies,)),
            pltpu.SemaphoreType.DMA((18,)),
        ]
        + chain_scratch(sizes, heads * DV // TILE),
        compiler_params=pltpu.CompilerParams(
            collective_id=1, has_side_effects=True, vmem_limit_bytes=60 << 20
        ),
    )(owners, lengths, packing, slot_copy, tokens, norm, down, upper, taps, gain)
    return [w.reshape(depth, w.shape[4]) for w in result[:4]], result[4:]


def chain_scratch(sizes, pieces):
    most = max(sizes)
    shape = (pieces, TILE + 8, TILE)
    return [
        pltpu.VMEM(shape, jnp.float32),
        pltpu.VMEM((sizes[2],) + shape, jnp.float32),
        pltpu.VMEM((sizes[1],) + shape, jnp.float32),
        pltpu.VMEM(shape, jnp.float32),
        pltpu.VMEM((3,) + shape, jnp.float32),
        pltpu.VMEM((pieces, TILE, TILE), jnp.float32),
        pltpu.SemaphoreType.DMA(((2 * most + 1) * pieces,)),
        pltpu.SemaphoreType.DMA(((2 * most + 1) * pieces,)),
    ]


def backward_kernel(
    n,
    sizes,
    plan,
    proj_ref,
    halo_ref,
    conv_ref,
    cum_ref,
    logits_ref,
    o_ref,
    gate_ref,
    du_ref,
    start_ref,
    cols_ref,
    rows_ref,
    taps_ref,
    gain_ref,
    g_up_ref,
    g_out_ref,
    g_down_ref,
    dproj_ref,
    dgate_ref,
    dlogits_ref,
    dtaps_ref,
    dgain_ref,
    early_ref,
    do,
    dact,
    adjoint,
    ends,
    after,
    back,
    tail,
    mine,
    across,
    along,
    before,
    held,
    result,
    send,
    recv,
    b_sem,
    *scatter_refs,
):
    tiles, channels = proj_ref.shape[0] // TILE, proj_ref.shape[1]
    keys = cum_ref.shape[1]
    heads = keys // DK
    me = lax.axis_index("seq")
    greet(n, sizes, (lax.rem(me + 1, n), lax.rem(me + n - 1, n)))
    steps, sent = scatter_steps(
        sizes, plan, [g_up_ref, g_out_ref, g_down_ref], scatter_refs, early_ref, TILE
    )
    steps[0]()
    scale = DK ** (-0.5)
    i = lax.broadcasted_iota(jnp.int32, (TILE, TILE), 0)
    j = lax.broadcasted_iota(jnp.int32, (TILE, TILE), 1)
    upper = (i <= j).astype(jnp.bfloat16)
    adjoint[...] = jnp.zeros_like(adjoint)
    mine[...] = jnp.zeros_like(mine)
    dgain_ref[...] = jnp.zeros_like(dgain_ref)
    dtaps_ref[...] = jnp.zeros_like(dtaps_ref)
    for p in range(mine.shape[0]):
        mine[p, TILE : TILE + 1] = jnp.ones((1, TILE), jnp.float32)

    def local(t, _):
        pl.when(t == tiles // 2)(steps[1])
        c = tiles - 1 - t
        at = pl.ds(pl.multiple_of(c * TILE, TILE), TILE)
        cum = cum_ref[at, :]
        pre = conv_ref[at, 0:keys]
        q = pre * sigmoid(pre) * jnp.exp(cum) * scale * cols_ref[at, 0:1]
        decay = jnp.exp(cum[TILE - 1 : TILE]) * cols_ref[at, 0:1][TILE - 1 : TILE]
        for h in range(heads):
            kh = slice(h * DK, (h + 1) * DK)
            vh = slice(h * DV, (h + 1) * DV)
            o = o_ref[at, vh]
            inverse = lax.rsqrt(jnp.mean(o * o, axis=1, keepdims=True) + norm_epsilon)
            gate = gate_ref[at, vh]
            sig = sigmoid(gate)
            du = du_ref[at, vh]
            unit = o * inverse
            dgate_ref[at, vh] = (
                du * (unit * gain_ref[...]) * (sig * (1.0 + gate * (1.0 - sig)))
            ).astype(dgate_ref.dtype)
            don = du * (gate * sig)
            dgain_ref[0:1] += jnp.sum(don * unit, axis=0, keepdims=True)
            scaled = gain_ref[...] * don
            grad = inverse * scaled - unit * (
                inverse * inverse * jnp.mean(scaled * o, axis=1, keepdims=True)
            )
            do[at, vh] = grad
            ends[c, h] = adjoint[h]
            adjoint[h] = adjoint[h] * decay[:, kh] + product(halves(grad), halves(q[:, kh]), TN)
            for e in range(DV // TILE):
                p = h * (DV // TILE) + e
                mine[p, TILE : TILE + 1] = mine[p, TILE : TILE + 1] * decay[:, kh]
        return 0

    lax.fori_loop(0, tiles, local, 0)
    for h in range(heads):
        for e in range(DV // TILE):
            mine[h * (DV // TILE) + e, 0:TILE] = adjoint[h, e * TILE : (e + 1) * TILE]
    stages, finish = chain_tools(
        n, sizes, False, mine, (across, along, before, held), send, recv, result
    )
    stages[0]()

    def inside(c, _):
        for k, stage in enumerate(stages[1:]):
            pl.when(c == k + 1)(stage)
        pl.when(c == 0)(steps[2])
        pl.when(c == tiles - 2)(steps[3])
        at = pl.ds(pl.multiple_of(c * TILE, TILE), TILE)
        cum = cum_ref[at, :]
        middle = cum[TILE // 2 - 1 : TILE // 2]
        pre = conv_ref[at, 0 : 2 * keys]
        both = pre * sigmoid(pre)
        grow = jnp.exp(cum - middle) * scale
        fall = jnp.exp(middle - cum)
        enter_decay = jnp.exp(cum) * (scale * cols_ref[at, 0:1])
        mask = tile_masks(rows_ref, cols_ref, c)
        for h in range(heads):
            kh = slice(h * DK, (h + 1) * DK)
            vh = slice(h * DV, (h + 1) * DV)
            q = halves(both[:, kh] * grow[:, kh])
            k = halves(both[:, keys + h * DK : keys + (h + 1) * DK] * fall[:, kh])
            prev_v = conv_ref[at, 2 * keys + h * DV : 2 * keys + (h + 1) * DV]
            v = halves(prev_v * sigmoid(prev_v))
            grad = halves(do[at, vh])
            scores = halves(jnp.where(mask, product(q, k, NT), 0.0))
            dscores = halves(jnp.where(mask, product(grad, v, NT), 0.0))
            dact[at, h * DK : (h + 1) * DK] = (
                product(dscores, k, NN) * grow[:, kh]
                + product(grad, halves(start_ref[c, h]), NN) * enter_decay[:, kh]
            )
            dact[at, keys + h * DK : keys + (h + 1) * DK] = (
                product(dscores, q, TN) * fall[:, kh]
            )
            dact[at, 2 * keys + h * DV : 2 * keys + (h + 1) * DV] = product(scores, grad, TN)
        return 0

    lax.fori_loop(0, tiles, inside, 0)
    finish()
    for h in range(heads):
        for e in range(DV // TILE):
            adjoint[h, e * TILE : (e + 1) * TILE] = result[h * (DV // TILE) + e]
    after[...] = jnp.zeros_like(after)

    def outside(t, _):
        pl.when(t == tiles // 4)(steps[4])
        pl.when(t == 3 * tiles // 4)(steps[5])
        c = tiles - 1 - t
        at = pl.ds(pl.multiple_of(c * TILE, TILE), TILE)
        cum = cum_ref[at, :]
        last = cum[TILE - 1 : TILE]
        remain = jnp.exp(last - cum) * cols_ref[at, 1:2]
        decay = jnp.exp(last) * cols_ref[at, 0:1][TILE - 1 : TILE]
        pre = conv_ref[at, 0 : 2 * keys]
        both = pre * sigmoid(pre)
        dkeys, edges = [], []
        for h in range(heads):
            kh = slice(h * DK, (h + 1) * DK)
            wide = slice(2 * keys + h * DV, 2 * keys + (h + 1) * DV)
            k = both[:, keys + h * DK : keys + (h + 1) * DK]
            end = ends[c, h] + adjoint[h]
            adjoint[h] = adjoint[h] * decay[:, kh]
            parts = halves(end)
            pre_v = conv_ref[at, wide]
            v = halves(pre_v * sigmoid(pre_v))
            dkeys.append(
                dact[at, keys + h * DK : keys + (h + 1) * DK]
                + product(v, parts, NN) * remain[:, kh]
            )
            dact[at, wide] += product(halves(k * remain[:, kh]), parts, NT)
            edges.append(jnp.sum(end * start_ref[c + 1, h], axis=0, keepdims=True))
        dk = jnp.concatenate(dkeys, axis=1)
        dq = dact[at, 0:keys]
        dact[at, keys : 2 * keys] = dk
        drift = both[:, 0:keys] * dq - both[:, keys:] * dk
        dl = running_sum(upper, drift) + jnp.concatenate(edges, axis=1)
        dlogits_ref[at, :] = dl * (1.0 / gate_scale) * sigmoid(-logits_ref[at, :])
        behind = jnp.where(
            c == 0,
            halo_ref[...],
            proj_ref[pl.ds(pl.multiple_of(jnp.maximum(c * TILE - 16, 0), 16), 16), :],
        )
        masks = cols_ref[pl.ds(pl.multiple_of(c * TILE, TILE), TILE + 8), :]
        for g in range(0, channels, 256):
            wide = slice(g, g + 256)
            pre = conv_ref[at, wide]
            sig = sigmoid(pre)
            dconv = dact[at, wide] * (sig * (1.0 + pre * (1.0 - sig)))
            block = jnp.concatenate(
                [
                    behind[:, g : g + 256].astype(jnp.float32),
                    proj_ref[at, wide].astype(jnp.float32),
                ]
            )
            grad = jnp.concatenate([dconv, after[:, wide]])
            total = taps_ref[3:4, wide] * dconv
            dtaps_ref[3:4, wide] += jnp.sum(dconv * block[16:], axis=0, keepdims=True)
            first = jnp.zeros((8, 256), jnp.float32)
            for s in (1, 2, 3):
                masked = grad * masks[:, 1 + s : 2 + s]
                tap = taps_ref[3 - s : 4 - s, wide]
                total = total + tap * masked[s : s + TILE]
                dtaps_ref[3 - s : 4 - s, wide] += jnp.sum(
                    masked[:TILE] * block[16 - s : 16 - s + TILE], axis=0, keepdims=True
                )
                first = first + tap * jnp.concatenate(
                    [jnp.zeros((8, 256), jnp.float32), masked[0:8]]
                )[s : s + 8]
            dproj_ref[at, wide] = total.astype(dproj_ref.dtype)
            after[:, wide] = dconv[0:8]
            back[0, :, wide] = first

            @pl.when(c == tiles - 1)
            def _():
                tail[:, wide] = total[TILE - 16 :]

        return 0

    lax.fori_loop(0, tiles, outside, 0)

    home = remote(
        back.at[0], back.at[1], b_sem.at[0], b_sem.at[1], lax.rem(me + n - 1, n)
    )

    @pl.when(me > 0)
    def _():
        home.start()

    for step in steps[6:]:
        step()
    sent()

    @pl.when(me < n - 1)
    def _():
        home.wait_recv()

    @pl.when(me == n - 1)
    def _():
        back[1] = jnp.zeros(back.shape[1:], jnp.float32)

    dproj_ref[pl.ds(tiles * TILE - 16, 16), :] = (
        tail[...] + jnp.concatenate([jnp.zeros((8, channels), jnp.float32), back[1]])
    ).astype(dproj_ref.dtype)

    @pl.when(me > 0)
    def _():
        home.wait_send()


def recurrence_back(
    proj, halo, conv, cum, logits, o, gate, du, starts, cols, rows, taps, gain, grads
):
    n = lax.axis_size("seq")
    sizes = axis_sizes(n)
    length, channels = proj.shape
    keys = cum.shape[1]
    heads = keys // DK
    value = heads * DV
    tiles = length // TILE
    f32 = jnp.float32
    shape = jax.ShapeDtypeStruct
    depth = grads[0].shape[0] // n
    plan = build_plan(tuple(g.shape[1] // TILE for g in grads), SHARES, 4, SPREAD)
    blocks = sum(g.shape[1] for g in grads) // TILE
    views = [g.reshape(sizes + (depth, g.shape[1])) for g in grads]
    vmem, anywhere = pl.BlockSpec(memory_space=pltpu.VMEM), pl.BlockSpec(memory_space=pl.ANY)
    return pl.pallas_call(
        functools.partial(backward_kernel, n, sizes, plan),
        in_specs=[vmem] * 13 + [anywhere] * 3,
        out_shape=(
            shape((length, channels), jnp.bfloat16),
            shape((length, value), jnp.bfloat16),
            shape((length, keys), f32),
            shape((8, channels), f32),
            shape((8, DV), f32),
            shape((blocks, depth, TILE), jnp.bfloat16),
        ),
        scratch_shapes=[
            pltpu.VMEM((length, value), f32),
            pltpu.VMEM((length, channels), f32),
            pltpu.VMEM((heads, DV, DK), f32),
            pltpu.VMEM((tiles, heads, DV, DK), f32),
            pltpu.VMEM((8, channels), f32),
            pltpu.VMEM((2, 8, channels), f32),
            pltpu.VMEM((16, channels), f32),
        ]
        + chain_scratch(sizes, heads * DV // TILE)
        + [pltpu.SemaphoreType.DMA((2,))]
        + scatter_scratch(sizes, plan, depth, TILE, jnp.bfloat16),
        compiler_params=pltpu.CompilerParams(
            collective_id=5, has_side_effects=True, vmem_limit_bytes=60 << 20
        ),
    )(proj, halo, conv, cum, logits, o, gate, du, starts, cols, rows, taps, gain, *views)


def adam_kernel(
    grad_ref,
    left_ref,
    right_ref,
    master_ref,
    first_ref,
    second_ref,
    grad_out,
    master_out,
    first_out,
    second_out,
    copy_out,
    high,
    low,
):
    width = left_ref.shape[1]
    step = min(256, width)
    dot = functools.partial(
        lax.dot_general, dimension_numbers=TN, preferred_element_type=jnp.float32
    )
    grad_out[0] = grad_ref[0].astype(jnp.float32)
    total = None
    for r in range(0, width, step):
        at = slice(r, r + step)
        lh, ll = halves(left_ref[0, at, :])
        high[at, :], low[at, :] = lh, ll
        term = dot(grad_ref[0, at, :], lh) + dot(grad_ref[0, at, :], ll)
        total = term if total is None else total + term
    right = halves(right_ref[0])
    rotated = product(right, halves(total), TN).T
    first = moment_decay * first_ref[0] + (1.0 - moment_decay) * rotated
    second = moment_decay * second_ref[0] + (1.0 - moment_decay) * rotated * rotated
    first_out[0] = first
    second_out[0] = second
    direction = first / (jnp.sqrt(second) + adam_epsilon)
    eh, el = halves(product(halves(direction), right, NT))
    both = jnp.concatenate([eh, el], axis=1)
    columns = eh.shape[1]
    dot = functools.partial(
        lax.dot_general, dimension_numbers=NN, preferred_element_type=jnp.float32
    )
    for r in range(0, width, step):
        at = slice(r, r + step)
        pair = dot(high[at, :], both)
        restored = pair[:, :columns] + (pair[:, columns:] + dot(low[at, :], eh))
        master = master_ref[0, at, :] - rate_block * restored
        master_out[0, at, :] = master
        copy_out[0, at, :] = master.astype(copy_out.dtype)


def block_adam(grads, left, right, master, first, second):
    slots, width, columns = master.shape
    tall = pl.BlockSpec((1, width, columns), lambda i: (i, 0, 0))
    shape = jax.ShapeDtypeStruct
    full = shape(master.shape, jnp.float32)
    return pl.pallas_call(
        adam_kernel,
        grid=(slots,),
        out_shape=(full, full, full, full, shape(master.shape, jnp.bfloat16)),
        in_specs=[
            tall,
            pl.BlockSpec((1, width, width), lambda i: (i, 0, 0)),
            pl.BlockSpec((1, columns, columns), lambda i: (i, 0, 0)),
            tall,
            tall,
            tall,
        ],
        out_specs=[tall] * 5,
        scratch_shapes=[
            pltpu.VMEM((width, width), jnp.bfloat16),
            pltpu.VMEM((width, width), jnp.bfloat16),
        ],
        compiler_params=pltpu.CompilerParams(vmem_limit_bytes=48 << 20),
    )(grads, left, right, master, first, second)


def join_kernel(u_ref, w_ref, tok_ref, gain_ref, h_ref, x_ref, inv_ref, send, recv, s_sem, r_sem):
    core = lax.axis_index("head")
    barrier = pltpu.get_barrier_semaphore()
    pl.semaphore_signal(barrier, inc=1, device_id={"head": 1 - core}, device_id_type=MESH)
    pl.semaphore_wait(barrier, 1)
    count = s_sem.shape[0]
    step = u_ref.shape[0] // count

    def swap(t):
        at = pl.ds(t * step, step)
        return pltpu.make_async_remote_copy(
            src_ref=send.at[at],
            dst_ref=recv.at[at],
            send_sem=s_sem.at[t],
            recv_sem=r_sem.at[t],
            device_id={"head": 1 - core},
            device_id_type=MESH,
        )

    for t in range(count):
        at = slice(t * step, (t + 1) * step)
        send[at, :] = lax.dot_general(
            u_ref[at, :], w_ref[...], NT, preferred_element_type=jnp.float32
        ).astype(send.dtype)
        swap(t).start()
    for t in range(count):
        at = slice(t * step, (t + 1) * step)
        swap(t).wait_recv()
        branch = send[at, :].astype(jnp.float32) + recv[at, :].astype(jnp.float32)
        hidden = tok_ref[at, :].astype(jnp.float32) + branch
        inverse = lax.rsqrt(jnp.mean(hidden * hidden, axis=1, keepdims=True) + norm_epsilon)
        h_ref[at, :] = hidden
        inv_ref[at, :] = inverse
        x_ref[at, :] = (hidden * inverse * gain_ref[...]).astype(x_ref.dtype)
    for t in range(count):
        swap(t).wait_send()


def join_heads(u, w, tokens, gain):
    length, width = tokens.shape
    shape = jax.ShapeDtypeStruct
    count = 4
    return pl.pallas_call(
        join_kernel,
        out_shape=(
            shape((length, width), jnp.float32),
            shape((length, width), jnp.bfloat16),
            shape((length, 1), jnp.float32),
        ),
        scratch_shapes=[
            pltpu.VMEM((length, width), jnp.bfloat16),
            pltpu.VMEM((length, width), jnp.bfloat16),
            pltpu.SemaphoreType.DMA((count,)),
            pltpu.SemaphoreType.DMA((count,)),
        ],
        compiler_params=pltpu.CompilerParams(
            collective_id=6, has_side_effects=True, vmem_limit_bytes=48 << 20
        ),
    )(u, w, tokens, gain)


def mlp_kernel(x_ref, up_ref, down_ref, dy_ref, hid_ref, dpair_ref):
    hidden = down_ref.shape[1]
    dot = functools.partial(
        lax.dot_general, dimension_numbers=NN, preferred_element_type=jnp.float32
    )
    x, dy = x_ref[...], dy_ref[...]
    for lo in range(0, hidden, 512):
        hi = min(lo + 512, hidden)
        gate = dot(x, up_ref[:, lo:hi])
        up = dot(x, up_ref[:, hidden + lo : hidden + hi])
        grad = dot(dy, down_ref[:, lo:hi])
        sig = sigmoid(gate)
        swish = gate * sig
        hid_ref[:, lo:hi] = (swish * up).astype(hid_ref.dtype)
        dpair_ref[:, lo:hi] = (grad * up * (sig + swish * (1.0 - sig))).astype(dpair_ref.dtype)
        dpair_ref[:, hidden + lo : hidden + hi] = (grad * swish).astype(dpair_ref.dtype)


def mlp(x, up, down, dy):
    length, width = x.shape
    hidden = down.shape[1]
    step = 256
    shape = jax.ShapeDtypeStruct

    def rows(columns):
        return pl.BlockSpec((step, columns), lambda i: (i, 0))

    def whole(columns):
        return pl.BlockSpec((width, columns), lambda i: (0, 0), pipeline_mode=pl.Buffered(1))

    return pl.pallas_call(
        mlp_kernel,
        grid=(length // step,),
        out_shape=(shape((length, hidden), x.dtype), shape((length, 2 * hidden), x.dtype)),
        in_specs=[rows(width), whole(2 * hidden), whole(hidden), rows(width)],
        out_specs=(rows(hidden), rows(2 * hidden)),
        compiler_params=pltpu.CompilerParams(vmem_limit_bytes=56 << 20),
    )(x, up, down, dy)


def join_back_kernel(
    g_ref,
    w_ref,
    h_ref,
    inv_ref,
    gain_ref,
    dy_ref,
    dh_ref,
    dattn_ref,
    sum_ref,
    send,
    recv,
    s_sem,
    r_sem,
):
    core = lax.axis_index("head")
    barrier = pltpu.get_barrier_semaphore()
    pl.semaphore_signal(barrier, inc=1, device_id={"head": 1 - core}, device_id_type=MESH)
    pl.semaphore_wait(barrier, 1)
    count = s_sem.shape[0]
    step = g_ref.shape[0] // count

    def swap(t):
        at = pl.ds(t * step, step)
        return pltpu.make_async_remote_copy(
            src_ref=send.at[at],
            dst_ref=recv.at[at],
            send_sem=s_sem.at[t],
            recv_sem=r_sem.at[t],
            device_id={"head": 1 - core},
            device_id_type=MESH,
        )

    total = jnp.zeros((1, h_ref.shape[1]), jnp.float32)

    def close(t, total):
        at = slice(t * step, (t + 1) * step)
        swap(t).wait_recv()
        grad = send[at, :] + recv[at, :]
        hidden, inverse = h_ref[at, :], inv_ref[at, :]
        unit = hidden * inverse
        scaled = gain_ref[...] * grad
        mean = jnp.mean(scaled * hidden, axis=1, keepdims=True)
        dh = dy_ref[at, :].astype(jnp.float32) + (
            inverse * scaled - unit * (inverse * inverse * mean)
        )
        dh_ref[at, :] = dh
        dattn_ref[at, :] = dh.astype(dattn_ref.dtype)
        return total + jnp.sum(grad * unit, axis=0, keepdims=True)

    for t in range(count):
        at = slice(t * step, (t + 1) * step)
        send[at, :] = lax.dot_general(
            g_ref[at, :], w_ref[...], NT, preferred_element_type=jnp.float32
        )
        swap(t).start()
        if t:
            total = close(t - 1, total)
    sum_ref[...] = jnp.broadcast_to(close(count - 1, total), sum_ref.shape)
    for t in range(count):
        swap(t).wait_send()


def join_back(grads, w, hidden, inverse, gain, dy):
    length, width = hidden.shape
    shape = jax.ShapeDtypeStruct
    count = 4
    return pl.pallas_call(
        join_back_kernel,
        out_shape=(
            shape((length, width), jnp.float32),
            shape((length, width), jnp.bfloat16),
            shape((8, width), jnp.float32),
        ),
        scratch_shapes=[
            pltpu.VMEM((length, width), jnp.float32),
            pltpu.VMEM((length, width), jnp.float32),
            pltpu.SemaphoreType.DMA((count,)),
            pltpu.SemaphoreType.DMA((count,)),
        ],
        compiler_params=pltpu.CompilerParams(
            collective_id=7, has_side_effects=True, vmem_limit_bytes=56 << 20
        ),
    )(grads, w, hidden, inverse, gain, dy)


def rms_stats(values):
    return lax.rsqrt(jnp.mean(values * values, axis=-1, keepdims=True) + norm_epsilon)


def rms_back(values, inverse, gain, upstream):
    scaled = gain * upstream
    return inverse * scaled - values * inverse * inverse * inverse * jnp.mean(
        scaled * values, axis=-1, keepdims=True
    )


def swish_slope(values):
    sigmoid = jax.nn.sigmoid(values)
    return sigmoid * (1.0 + values * (1.0 - sigmoid))


def plain_adam(param, gradient, first, second, rate):
    first_next = moment_decay * first + (1.0 - moment_decay) * gradient
    second_next = moment_decay * second + (1.0 - moment_decay) * gradient * gradient
    return (
        param - rate * first_next / (jnp.sqrt(second_next) + adam_epsilon),
        first_next,
        second_next,
    )


def body(
    tokens,
    cotangent,
    lengths,
    packing,
    owners,
    slot_copy,
    slot_master,
    slot_first,
    slot_second,
    basis_left,
    basis_right,
    norm_gains,
    gains_first,
    gains_second,
    gate_down,
    down_first,
    down_second,
    gate_up,
    upper_first,
    upper_second,
    head_gain,
    head_first,
    head_second,
    conv_weight,
    conv_first,
    conv_second,
):
    tok_rows = tokens.shape[0]
    model_width = tokens.shape[1]
    block_width = slot_copy.shape[2]
    rank_width = gate_down.shape[1]
    tap_count = conv_weight.shape[0]
    key_width = gate_up.shape[1]
    channels = conv_weight.shape[1]
    value_width = channels - 2 * key_width
    block_total = owners.shape[1]
    count_in = (channels + value_width) // block_width
    count_out = value_width // block_width
    count_down = (block_total - count_in - count_out) // 3
    count_up = 2 * count_down
    (in_weights, up_weights, out_weights, down_weights), kept = forward(
        owners,
        lengths,
        packing,
        slot_copy,
        tokens,
        norm_gains[0:1],
        gate_down,
        gate_up,
        conv_weight,
        head_gain[None],
        (count_in, count_up, count_out, count_down),
    )
    normed, lowrank, logits, mixed_proj, halo, gate_pre = kept[:6]
    conv_pre, cumulative, attended, gated_out, starts, cols, rows = kept[6:]
    own_valid = cols[:tok_rows, 7]
    gain_row = head_gain[None]
    down_low = gate_down.astype(jnp.bfloat16)
    inputs = tokens.astype(jnp.float32)
    inverse_one = rms_stats(inputs)
    hidden_one, normed_two, inverse_two = join_heads(
        gated_out, out_weights, tokens, norm_gains[1:2]
    )
    upstream_low = (cotangent.astype(jnp.float32) * own_valid[:, None]).astype(jnp.bfloat16)
    hidden, grad_pair = mlp(normed_two, up_weights, down_weights, upstream_low)
    mlp_part = jnp.einsum("tn,dn->td", hidden, down_weights, preferred_element_type=jnp.float32)
    mlp_branch = lax.psum(mlp_part.astype(jnp.bfloat16), "head").astype(jnp.float32)
    result = (hidden_one + mlp_branch).astype(jnp.bfloat16)
    grad_one, grad_attn, gains_two = join_back(
        grad_pair, up_weights, hidden_one, inverse_two, norm_gains[1:2], upstream_low
    )
    grad_gains_two = gains_two[0]
    grad_gated = jnp.dot(grad_attn, out_weights, preferred_element_type=jnp.float32)
    early = [
        jnp.einsum("td,tn->dn", left, right, preferred_element_type=jnp.float32).astype(
            jnp.bfloat16
        )
        for left, right in (
            (normed_two, grad_pair),
            (grad_attn, gated_out),
            (upstream_low, hidden),
        )
    ]
    grad_mixed, grad_gate_pre, grad_logits, tap_grads, gain_grads, early = recurrence_back(
        mixed_proj,
        halo,
        conv_pre,
        cumulative,
        logits,
        attended,
        gate_pre,
        grad_gated,
        starts,
        cols,
        rows,
        conv_weight,
        gain_row,
        early,
    )
    grad_conv_weight = tap_grads[:tap_count]
    grad_head_gain = gain_grads[0]
    grad_upper = jnp.concatenate(
        [
            jnp.einsum("tr,tk->rk", lowrank, grad_logits, precision=highest_precision),
            jnp.sum(grad_logits, axis=0, keepdims=True),
        ],
        axis=0,
    )
    grad_lowrank = jnp.einsum(
        "tk,rk->tr", grad_logits, gate_up[:rank_width], precision=highest_precision
    ).astype(jnp.bfloat16)
    grad_down_part = jnp.einsum(
        "tr,td->rd", grad_lowrank, normed, preferred_element_type=jnp.float32
    )
    grad_projected = jnp.concatenate(
        [grad_mixed, grad_gate_pre], axis=1
    )
    grad_normed_part = jnp.einsum(
        "tn,dn->td", grad_projected, in_weights, preferred_element_type=jnp.float32
    ) + jnp.einsum("tr,dr->td", grad_lowrank, down_low, preferred_element_type=jnp.float32)
    grad_normed = lax.psum(grad_normed_part.astype(jnp.bfloat16), "head").astype(jnp.float32)
    grad_gains_one = jnp.sum(grad_normed_part * inputs * inverse_one, axis=0)
    grad_input = grad_one + rms_back(inputs, inverse_one, norm_gains[0], grad_normed)
    shared_rows, own_rows = rank_width + 8, 16
    shared = jnp.concatenate(
        [
            grad_down_part,
            jnp.pad(grad_head_gain, (0, model_width - grad_head_gain.shape[0]))[None],
            grad_gains_one[None],
            jnp.zeros((6, model_width), jnp.float32),
        ]
    )
    flat_upper = grad_upper.reshape(-1)
    upper_rows = -(-flat_upper.shape[0] // model_width)
    alone = jnp.concatenate(
        [
            grad_gains_two[None],
            grad_conv_weight,
            jnp.pad(flat_upper, (0, upper_rows * model_width - flat_upper.shape[0])).reshape(
                upper_rows, model_width
            ),
        ]
    )
    alone = jnp.pad(alone, ((0, own_rows - alone.shape[0]), (0, 0)))
    slots_dev = slot_copy.shape[0]
    slot_total = slots_dev * lax.axis_size("seq")
    late = jnp.einsum(
        "td,tn->dn", normed, grad_projected, preferred_element_type=jnp.float32
    ).astype(jnp.bfloat16)
    named = jnp.arange(slot_total, dtype=jnp.int32)[:, None] == owners
    inverse = jnp.where(
        jnp.any(named, axis=1),
        jnp.sum(named * jnp.arange(block_total, dtype=jnp.int32), axis=1),
        block_total,
    ).astype(jnp.int32)[None]
    owned_grads, summed = scatter_grads(
        late, early, inverse, slots_dev, jnp.concatenate([shared, alone]), shared_rows
    )
    owned_grads, master_next, first_next, second_next, copy_next = block_adam(
        owned_grads, basis_left, basis_right, slot_master, slot_first, slot_second
    )
    down_grad = summed[:rank_width].T
    head_grad = summed[rank_width, : grad_head_gain.shape[0]]
    gains_grad = jnp.stack([summed[rank_width + 1], summed[shared_rows]])
    conv_grad = summed[shared_rows + 1 : shared_rows + 1 + tap_count]
    upper_grad = (
        summed[shared_rows + 1 + tap_count : shared_rows + 1 + tap_count + upper_rows]
        .reshape(-1)[: flat_upper.shape[0]]
        .reshape(grad_upper.shape)
    )
    gains_next, gains_first_next, gains_second_next = plain_adam(
        norm_gains, gains_grad, gains_first, gains_second, rate_gains
    )
    down_next, down_first_next, down_second_next = plain_adam(
        gate_down, down_grad, down_first, down_second, rate_down
    )
    upper_next, upper_first_next, upper_second_next = plain_adam(
        gate_up, upper_grad, upper_first, upper_second, rate_upper
    )
    head_next, head_first_next, head_second_next = plain_adam(
        head_gain, head_grad, head_first, head_second, rate_head
    )
    conv_next, conv_first_next, conv_second_next = plain_adam(
        conv_weight, conv_grad, conv_first, conv_second, rate_conv
    )
    return (
        result,
        grad_input,
        owned_grads,
        master_next,
        first_next,
        second_next,
        copy_next,
        gains_grad,
        gains_next,
        gains_first_next,
        gains_second_next,
        down_grad,
        down_next,
        down_first_next,
        down_second_next,
        upper_grad,
        upper_next,
        upper_first_next,
        upper_second_next,
        head_grad,
        head_next,
        head_first_next,
        head_second_next,
        conv_grad,
        conv_next,
        conv_first_next,
        conv_second_next,
    )


def solution(mesh):
    placed = (
        P("seq", None),
        P("seq", None),
        P(),
        P(),
        P("head", None),
        P(("seq", "head"), None, None),
        P(("seq", "head"), None, None),
        P(("seq", "head"), None, None),
        P(("seq", "head"), None, None),
        P(("seq", "head"), None, None),
        P(("seq", "head"), None, None),
        P(),
        P(),
        P(),
        P(),
        P(),
        P(),
        P(None, "head"),
        P(None, "head"),
        P(None, "head"),
        P(),
        P(),
        P(),
        P(None, "head"),
        P(None, "head"),
        P(None, "head"),
    )
    return jax.shard_map(
        body,
        mesh=mesh,
        in_specs=placed,
        out_specs=(
            P("seq", None),
            P("seq", None),
            P(("seq", "head"), None, None),
            P(("seq", "head"), None, None),
            P(("seq", "head"), None, None),
            P(("seq", "head"), None, None),
            P(("seq", "head"), None, None),
            P(),
            P(),
            P(),
            P(),
            P(),
            P(),
            P(),
            P(),
            P(None, "head"),
            P(None, "head"),
            P(None, "head"),
            P(None, "head"),
            P(),
            P(),
            P(),
            P(),
            P(None, "head"),
            P(None, "head"),
            P(None, "head"),
            P(None, "head"),
        ),
        check_vma=False,
    )
```

time: 664 us -> 561 us (0.84)
  matrix products: 143 us -> 45.6 us
  Pallas kernels: 404 us -> 435 us
  other arithmetic: 35.7 us -> 19.4 us
  waiting for transfers between devices: 34.9 us -> 21.8 us
    dot_general x12 -> x1, matrix products: 93.2 us -> 5.79 us  [body(): jnp.einsum('td,tn->dn', normed, grad_projected, preferred_element_type=jn...]
    psum x2 -> x0, waiting for transfers between devices: 34.9 us -> none  [the longest x1 30.5 us: body(): attn_branch = lax.psum(attn_part, 'head')]
    pallas_call x5 -> x7, Pallas kernels: 404 us -> 435 us  [the longest x1 157 us: forward(): pl.pallas_call(functools.partial(forward_kernel, n, sizes, plan, ready),...]
    psum x1, waiting for transfers between devices: 0.01 us -> 21.8 us  [body(): lax.psum(mlp_part.astype(jnp.bfloat16), 'head').astype(jnp.float32)]
    dot_general x4 -> x3, matrix products: 25.5 us -> 17.5 us  [body(): jnp.einsum('td,tn->dn', left, right, preferred_element_type=jnp.float32)]
  transfers between devices with their start and end apart: 4 -> 1, of which waited for: 2 -> 1; matrix products, arithmetic and copies ran while one was open for 16% -> 2% of each run, Pallas kernels for 45% -> 0%
where the time goes in v3:
time: 561 us; the launch traced here: 551 us
  Pallas kernels  435 us (78%)
  matrix products  45.6 us (8%)
  waiting for transfers between devices  21.8 us (4%)
  other arithmetic  19.4 us (3%)
  between operations  14.9 us (3%)
  local copies, waits for them, and re-layouts  14.7 us (3%)
    pallas_call x1, Pallas kernels, forward(): pl.pallas_call(functools.partial(forward_kernel, n, sizes, plan, ready),...  157 us
    pallas_call x1, Pallas kernels, recurrence_back(): pl.pallas_call(functools.partial(backward_kernel, n, sizes, plan), in_spe...  139 us
    pallas_call x1, Pallas kernels, scatter_grads(): pl.pallas_call(functools.partial(scatter_kernel, n, sizes, plan, shared),...  78.1 us
    psum x1, waiting for transfers between devices, body(): lax.psum(mlp_part.astype(jnp.bfloat16), 'head').astype(jnp.float32)  21.8 us
    pallas_call x1, Pallas kernels, join_back(): pl.pallas_call(join_back_kernel, out_shape=(shape((length, width), jnp.fl...  20.1 us
    dot_general x3, matrix products, body(): jnp.einsum('td,tn->dn', left, right, preferred_element_type=jnp.float32)  17.5 us
    pallas_call x1, Pallas kernels, block_adam(): pl.pallas_call(adam_kernel, grid=(slots,), out_shape=(full, full, full, f...  16.3 us
    pallas_call x1, Pallas kernels, mlp(): pl.pallas_call(mlp_kernel, grid=(length // step,), out_shape=(shape((leng...  16.3 us
  transfers between devices with their start and end apart: 1, of which 1 were waited for; matrix products, arithmetic and copies ran while one was open for 2% of the time, Pallas kernels for 0%

profile of v3, /device:TPU:30, one launch (start us, length us, event | category | flops | bytes accessed | tf_op | source)
XLA Modules:
  0.0 551.3 jit_solution(17129818421869825283)
XLA Ops:
  7.3 1.5 fusion.23
  8.7 1.8 copy.55.down_ref
  10.6 157.0 %shard_map.457 = (bf16[4,2,2,64,1536]{4,3,2,1,0:T(8,128)(2,1)}, bf16[4,2,2,64,2816]{4,3,2,1,0:T(8,128)(2,1)}, bf16[4,2,2,64,512]{4,3,2,1,0:T(8,128)(2,1)}, bf16[...) custom-call(s32[1,49]{1,0:T(1,128)} %owners_ref.1, ...), custom_call_target="tpu_custom_call" | custom-call | tf_op jit(solution)/shard_map/pallas_call | solution.py:982
  167.6 1.6 slice_reduce_fusion
  169.1 1.7 multiply_convert_fusion.dy_ref
  170.9 8.6 %shard_map.458 = (f32[1024,1024]{1,0:T(8,128)}, bf16[1024,1024]{1,0:T(8,128)(2,1)S(1)}, f32[1024,1]{1,0:T(8,128)S(1)}) custom-call(bf16[1024,512]{1,0:T(8,128)(2,1)S(1)} %copy-done.7, bf16[1024,512]{1,0:T(8,128)(2,1)S(1)} %bitcast.44, bf16[1024,1024]{1,0:T(8,128)(2,1)} %tok_ref.1, f32[1,1024]{1,0:T(1,128)S(1)} %get-tuple-element.128.gain_ref), custom_call_target="tpu_custom_call" | custom-call | tf_op jit(solution)/shard_map/pallas_call | solution.py:1443
  179.5 1.3 copy-done.2
  180.8 0.8 copy-done.9
  181.6 16.3 %shard_map.459 = (bf16[1024,1408]{1,0:T(8,128)(2,1)}, bf16[1024,2816]{1,0:T(8,128)(2,1)}) custom-call(bf16[1024,1024]{1,0:T(8,128)(2,1)} %copy-done.2, bf16[1024,2816]{1,0:T(8,128)(2,1)} %bitcast.46, bf16[1024,1408]{1,0:T(8,128)(2,1)} %bitcast.50, bf16[1024,1024]{1,0:T(8,128)(2,1)} %multiply_convert_fusion.dy_ref), custom_call_target="tpu_custom_call" | custom-call | tf_op jit(solution)/shard_map/pallas_call | solution.py:1492
  197.9 6.6 %convolution_convert_fusion.3 = bf16[1024,1024]{1,0:T(8,128)(2,1)} fusion(bf16[1024,1408]{1,0:T(8,128)(2,1)} %get-tuple-element.72, bf16[1024,1408]{1,0:T(8,128)(2,1)S(1)} %bitcast.51), kind=kOutput, calls=%fused_computation.20 | convolution fusion | flops 2953838592 | bytes 7864320 | tf_op jit(solution)/shard_map/tn,dn->td/dot_general | solution.py:1680
  204.5 5.2 convolution_convert_fusion.2
  209.7 8.3 %convolution_convert_fusion = bf16[1024,2816]{1,0:T(8,128)(2,1)} fusion(bf16[1024,1024]{1,0:T(8,128)(2,1)S(1)} %copy-done.3, bf16[1024,2816]{1,0:T(8,128)(2,1)S(1)} %copy-done.15), kind=kOutput, calls=%fused_computation.4 | convolution fusion | flops 5908463616 | bytes 13631488 | tf_op jit(solution)/shard_map/td,tn->dn/dot_general | solution.py:1689
  218.0 20.1 %shard_map.460 = (f32[1024,1024]{1,0:T(8,128)}, bf16[1024,1024]{1,0:T(8,128)(2,1)}, f32[8,1024]{1,0:T(8,128)}) custom-call(bf16[1024,2816]{1,0:T(8,128)(2,1)} %get-tuple-element.73.g_ref, bf16[1024,2816]{1,0:T(8,128)(2,1)} %bitcast.47, f32[1024,1024]{1,0:T(8,128)} %get-tuple-element.67.h_ref, f32[1024,1]{1,0:T(8,128)} %copy-done.9, f32[1,1024]{1,0:T(1,128)} %copy-done.11, ...), custom_call_target="tpu_custom_call" | custom-call | tf_op jit(solution)/shard_map/pallas_call | solution.py:1569
  238.1 4.0 convolution_convert_fusion.4
  242.1 2.6 fusion.25.du_ref
  244.7 138.5 %shard_map.461 = (bf16[1024,1024]{1,0:T(8,128)(2,1)}, bf16[1024,512]{1,0:T(8,128)(2,1)}, f32[1024,256]{1,0:T(8,128)}, f32[8,1024]{1,0:T(8,128)}, f32[8,256]{1,0:T(8,128)}, /*index=5*/bf16[37,64,128]{2,1,0:T(8,128)(2,1)}) custom-call(bf16[1024,1024]{1,0:T(8,128)(2,1)} %get-tuple-element.76.proj_ref, bf16[16,1024]{1,0:T(8,128)(2,1)} %get-tuple-element.77.halo_ref, ...), custom_call_target="tpu_custom_call" | custom-call | tf_op jit(solution)/shard_map/pallas_call | solution.py:1296
  383.3 2.3 convolution_convert_fusion.5
  385.6 1.9 constant_dynamic-update-slice_fusion.1
  388.1 3.4 fusion.26
  391.5 3.4 fusion.24
  395.0 0.9 slice.52
  395.9 0.7 slice.51
  397.4 2.0 fusion.28
  400.3 2.0 fusion.27
  402.2 5.8 %convolution_convert_fusion.1 = bf16[1024,1536]{1,0:T(8,128)(2,1)S(1)} fusion(bf16[1024,1024]{1,0:T(8,128)(2,1)S(1)} %copy-done.18, bf16[1024,1536]{1,0:T(8,128)(2,1)} %copy-done.19), kind=kOutput, calls=%fused_computation.17 | convolution fusion | flops 3222798336 | bytes 8388608 | tf_op jit(solution)/shard_map/td,tn->dn/dot_general | solution.py:1761
  408.0 21.8 %all-reduce.6.cloned.1.call-done = (bf16[1024,1024]{1,0:T(8,128)(2,1)}, bf16[1024,1024]{1,0:T(8,128)(2,1)}) async-done(((bf16[1024,1024]{1,0:T(8,128)(2,1)}, bf16[1024,1024]{1,0:T(8,128)(2,1)}), (bf16[1024,1024]{1,0:T(8,128)(2,1)}, bf16[1024,1024]{1,0:T(8,128)(2,1)})) %all-reduce.6.cloned.1.call-update) | async-done | bytes 4194320 | tf_op jit(solution)/shard_map/psum | solution.py:1681
  429.9 7.9 %fusion.8 = (f32[1024]{0:T(1024)S(1)}, f32[1024]{0:T(1024)}, bf16[1024,1024]{1,0:T(8,128)(2,1)}) fusion(f32[1024,1024]{1,0:T(8,128)} %get-tuple-element.131, bf16[1024,1024]{1,0:T(8,128)(2,1)} %tok_ref.1, f32[1024]{0:T(1024)S(1)} %add_rsqrt_fusion, bf16[1024,1024]{1,0:T(8,128)(2,1)} %get-tuple-element.106, f32[1024]{0:T(1024)S(1)} %bitcast.53, ...), kind=kLoop, calls=%fused_computation.13 | loop fusion | flops 11532288 | bytes 16793600 | tf_op jit(solution)/shard_map/reduce_sum | solution.py:1736
  438.5 1.1 copy-done.8
  439.6 78.1 %shard_map.462 = (bf16[4,16,64,128]{3,2,1,0:T(8,128)(2,1)S(1)}, f32[40,1024]{1,0:T(8,128)S(1)}) custom-call(s32[1,64]{1,0:T(1,128)S(1)} %select_bitcast_fusion.inv_ref, f32[40,1024]{1,0:T(8,128)S(1)} %concatenate.15.small_ref, bf16[4,2,2,64,1536]{4,3,2,1,0:T(8,128)(2,1)S(1)} %bitcast.42, bf16[37,64,128]{2,1,0:T(8,128)(2,1)S(1)} %copy-done.8), custom_call_target="tpu_custom_call" | custom-call | tf_op jit(solution)/shard_map/pallas_call | solution.py:325
  517.7 1.0 copy-done.4
  518.9 5.7 %fusion.5 = f32[1024,1024]{1,0:T(8,128)} fusion(f32[1024,1024]{1,0:T(8,128)} %get-tuple-element.75, bf16[1024,1024]{1,0:T(8,128)(2,1)} %tok_ref.1, bf16[1024,1024]{1,0:T(8,128)(2,1)} %get-tuple-element.106, f32[1024]{0:T(1024)S(1)} %broadcast_multiply_fusion, f32[1024]{0:T(1024)S(1)} %bitcast.54, f32[1024]{0:T(1024)S(1)} %add_rsqrt_fusion), kind=kLoop, calls=%fused_computation.10 | loop fusion | flops 10485760 | bytes 12595200 | tf_op jit(solution)/shard_map/add | solution.py:1737
  528.0 16.3 %shard_map.463 = (f32[4,1024,128]{2,1,0:T(8,128)}, f32[4,1024,128]{2,1,0:T(8,128)}, f32[4,1024,128]{2,1,0:T(8,128)}, f32[4,1024,128]{2,1,0:T(8,128)}, bf16[4,1024,128]{2,1,0:T(8,128)(2,1)}) custom-call(bf16[4,1024,128]{2,1,0:T(8,128)(2,1)S(1)} %bitcast.43, f32[4,1024,1024]{2,1,0:T(8,128)} %left_ref.1, f32[4,128,128]{2,1,0:T(8,128)S(1)} %copy-done.10, ...), custom_call_target="tpu_custom_call" | custom-call | tf_op jit(solution)/shard_map/pallas_call | solution.py:1380
  (114 shorter events, 6.3 us)
Async XLA Ops:
  7.2 161.9 %copy-start.17 = (bf16[1024,1024]{1,0:T(8,128)(2,1)S(1)}, bf16[1024,1024]{1,0:T(8,128)(2,1)}, u32[]{:S(2)}) copy-start(bf16[1024,1024]{1,0:T(8,128)(2,1)} %param.27) | copy-start | bytes 6291460
  7.2 422.6 %all-reduce.6.cloned.1.call-start = ((), (), s32[]{:S(2)}) async-start(), calls=%async_computation | async-start | bytes 8388608 | tf_op jit(solution)/shard_map/psum | solution.py:1681
  8.7 162.1 %copy-start.11 = (f32[1,1024]{1,0:T(1,128)}, f32[1,1024]{1,0:T(1,128)S(1)}, u32[]{:S(2)}) copy-start(f32[1,1024]{1,0:T(1,128)S(1)} %get-tuple-element.128.gain_ref) | copy-start | bytes 12292
  181.6 16.3 %copy-start.16 = (bf16[4,2,2,64,1408]{4,3,2,1,0:T(8,128)(2,1)S(1)}, bf16[4,2,2,64,1408]{4,3,2,1,0:T(8,128)(2,1)}, u32[]{:S(2)}) copy-start(bf16[4,2,2,64,1408]{4,3,2,1,0:T(8,128)(2,1)} %get-tuple-element.70) | copy-start | bytes 8650756
  197.9 6.6 %copy-start.13 = (bf16[1024,1024]{1,0:T(8,128)(2,1)S(1)}, bf16[1024,1024]{1,0:T(8,128)(2,1)}, u32[]{:S(2)}) copy-start(bf16[1024,1024]{1,0:T(8,128)(2,1)} %multiply_convert_fusion.dy_ref) | copy-start | bytes 6291460
  197.9 6.6 %copy-start.43 = (bf16[1024,1408]{1,0:T(8,128)(2,1)S(1)}, bf16[1024,1408]{1,0:T(8,128)(2,1)}, u32[]{:S(2)}) copy-start(bf16[1024,1408]{1,0:T(8,128)(2,1)} %get-tuple-element.72) | copy-start | bytes 8650756
  204.5 5.2 copy-start.3
  204.5 5.2 copy-start.15
  244.7 138.6 %copy-start.22 = (f32[17,256]{1,0:T(8,128)S(1)}, f32[17,256]{1,0:T(8,128)}, u32[]{:S(2)}) copy-start(f32[17,256]{1,0:T(8,128)} %upper_ref.1) | copy-start | bytes 52228
  395.0 4.5 copy-start.41
  395.0 4.8 copy-start.12
  402.2 27.6 %copy-start.25 = (f32[1,1024]{1,0:T(1,128)S(1)}, f32[1,1024]{1,0:T(1,128)}, u32[]{:S(2)}) copy-start(f32[1,1024]{1,0:T(1,128)} %get-tuple-element.129.norm_ref) | copy-start | bytes 12292
  439.6 79.1 %copy-start.31 = (f32[1024]{0:T(1024)S(1)}, f32[1024]{0:T(1024)}, u32[]{:S(2)}) copy-start(f32[1024]{0:T(1024)} %get-tuple-element.104) | copy-start | bytes 12292
  518.7 7.4 %copy-start.38 = (f32[1,256]{1,0:T(1,128)}, f32[1,256]{1,0:T(1,128)S(1)}, u32[]{:S(2)}) copy-start(f32[1,256]{1,0:T(1,128)S(1)} %slice.60) | copy-start | bytes 3076
  518.7 5.9 %copy-start.24 = (f32[4,1024]{1,0:T(4,128)S(1)}, f32[4,1024]{1,0:T(4,128)}, u32[]{:S(2)}) copy-start(f32[4,1024]{1,0:T(4,128)} %taps_ref.3) | copy-start | bytes 49156
  518.7 5.9 %copy-start.32 = (f32[4,1024]{1,0:T(4,128)S(1)}, f32[4,1024]{1,0:T(4,128)}, u32[]{:S(2)}) copy-start(f32[4,1024]{1,0:T(4,128)} %param.50) | copy-start | bytes 49156
  518.8 5.9 %copy-start.33 = (f32[4,1024]{1,0:T(4,128)S(1)}, f32[4,1024]{1,0:T(4,128)}, u32[]{:S(2)}) copy-start(f32[4,1024]{1,0:T(4,128)} %param.51) | copy-start | bytes 49156
  518.8 6.6 %copy-start.26 = (f32[1024,16]{0,1:T(8,128)S(1)}, f32[1024,16]{0,1:T(8,128)}, u32[]{:S(2)}) copy-start(f32[1024,16]{0,1:T(8,128)} %param.41) | copy-start | bytes 196612
  518.8 6.5 %copy-start.27 = (f32[1024,16]{0,1:T(8,128)S(1)}, f32[1024,16]{0,1:T(8,128)}, u32[]{:S(2)}) copy-start(f32[1024,16]{0,1:T(8,128)} %param.42) | copy-start | bytes 196612
  518.8 7.2 %copy-start.34 = (f32[256]{0:T(256)S(1)}, f32[256]{0:T(256)}, u32[]{:S(2)}) copy-start(f32[256]{0:T(256)} %param.46) | copy-start | bytes 3076
  518.8 7.2 %copy-start.39 = (f32[256]{0:T(256)S(1)}, f32[256]{0:T(256)}, u32[]{:S(2)}) copy-start(f32[256]{0:T(256)} %param.47) | copy-start | bytes 3076
  518.8 7.2 %copy-start.40 = (f32[256]{0:T(256)S(1)}, f32[256]{0:T(256)}, u32[]{:S(2)}) copy-start(f32[256]{0:T(256)} %param.48) | copy-start | bytes 3076
  518.8 7.8 %copy-start.23 = (f32[17,256]{1,0:T(8,128)S(1)}, f32[17,256]{1,0:T(8,128)}, u32[]{:S(2)}) copy-start(f32[17,256]{1,0:T(8,128)} %upper_ref.1) | copy-start | bytes 52228
  518.8 7.8 %copy-start.29 = (f32[17,256]{1,0:T(8,128)S(1)}, f32[17,256]{1,0:T(8,128)}, u32[]{:S(2)}) copy-start(f32[17,256]{1,0:T(8,128)} %param.44) | copy-start | bytes 52228
  518.8 7.8 %copy-start.30 = (f32[17,256]{1,0:T(8,128)S(1)}, f32[17,256]{1,0:T(8,128)}, u32[]{:S(2)}) copy-start(f32[17,256]{1,0:T(8,128)} %param.45) | copy-start | bytes 52228
  518.9 8.4 %copy-start.28 = (f32[2,1024]{1,0:T(2,128)S(1)}, f32[2,1024]{1,0:T(2,128)}, u32[]{:S(2)}) copy-start(f32[2,1024]{1,0:T(2,128)} %param.37) | copy-start | bytes 24580
  518.9 8.4 %copy-start.36 = (f32[2,1024]{1,0:T(2,128)S(1)}, f32[2,1024]{1,0:T(2,128)}, u32[]{:S(2)}) copy-start(f32[2,1024]{1,0:T(2,128)} %param.38) | copy-start | bytes 24580
  518.9 8.4 %copy-start.37 = (f32[2,1024]{1,0:T(2,128)S(1)}, f32[2,1024]{1,0:T(2,128)}, u32[]{:S(2)}) copy-start(f32[2,1024]{1,0:T(2,128)} %param.39) | copy-start | bytes 24580
  518.9 9.0 %copy-start = (f32[4,1024,128]{2,1,0:T(8,128)S(1)}, f32[4,1024,128]{2,1,0:T(8,128)}, u32[]{:S(2)}) copy-start(f32[4,1024,128]{2,1,0:T(8,128)} %master_ref.1) | copy-start | bytes 6291460
  518.9 9.0 %copy-start.1 = (f32[4,1024,128]{2,1,0:T(8,128)S(1)}, f32[4,1024,128]{2,1,0:T(8,128)}, u32[]{:S(2)}) copy-start(f32[4,1024,128]{2,1,0:T(8,128)} %first_ref.1) | copy-start | bytes 6291460
  518.9 9.0 %copy-start.5 = (bf16[4,16,64,128]{3,2,1,0:T(8,128)(2,1)S(1)}, bf16[4,16,64,128]{3,2,1,0:T(8,128)(2,1)}, u32[]{:S(2)}) copy-start(bf16[4,16,64,128]{3,2,1,0:T(8,128)(2,1)} %copy-done.4) | copy-start | bytes 3145732
  518.9 9.0 %copy-start.10 = (f32[4,128,128]{2,1,0:T(8,128)S(1)}, f32[4,128,128]{2,1,0:T(8,128)}, u32[]{:S(2)}) copy-start(f32[4,128,128]{2,1,0:T(8,128)} %right_ref.1) | copy-start | bytes 786436
  (14 other events, 37.9 us)
Sparse Core Ops, SparseCore 0:
  395.1 34.6 all-reduce.5
